TPU v7x, 32 devices: a whole 2x2x4 slice. The times are simulated.
32 devices in a mesh: region: 4 (over x, core), member: 8 (over z, y).
Axes of the slice: x: 2, y: 2, z: 4, core: 2. Of those that a mesh axis runs over, the one named last changes fastest.
Arguments:
- predicted_states: float32 [16, 100, 128, 128], P('member', None, 'region'), may hold values from -20 to 20, as said below
- observed_analysis: float32 [100, 128, 128], P(None, 'region'), may hold values from -20 to 20
- tile_location_sequence: int32 [4, 4096], P('region'), may hold values from 0 to 4095, each once within a row
Outputs:
- gradient: float32 [16, 100, 128, 128], P('member', None, 'region')
Inputs may be any that keep to these rules, and one draw needn't show every extreme that they name: Each row of tile_location_sequence is a permutation of the cells of one region. `predicted_states`: members share a common field per variable and cell, with variable and cell scales.
All inputs are finite; a program needn't handle non-finite values.
Results may differ from a plain program's by a relative error of at most 0.0003.
Values sent between devices are 32-bit elements; how exact they have to be, the bound alone decides.
No kernel may reach another device: no remote copies, remote signals or barrier semaphores. Data moves between devices by JAX's collectives and lax.ppermute only.
A program may use at most 128 MiB of HBM per device.

v0:
```python
import jax
import jax.numpy as jnp
from jax import lax
from jax.sharding import PartitionSpec as P

LON = 128
HALF = 32
PATCH = 128


def extended(block, sides, width):
    for axis, dim in sides:
        count = lax.axis_size(axis)
        forward = [(i, i + 1) for i in range(count - 1)]
        backward = [(target, source) for source, target in forward]
        low = lax.ppermute(
            lax.slice_in_dim(block, block.shape[dim] - width, None, axis=dim), axis, forward
        )
        high = lax.ppermute(lax.slice_in_dim(block, 0, width, axis=dim), axis, backward)
        block = jnp.concatenate([low, block, high], axis=dim)
    return block


def kernel_value(offset, half):
    sigma = half / 2.0
    steps = jnp.arange(-half, half + 1).astype(jnp.float32)
    norm_sum = jnp.sum(jnp.exp(-(steps * steps) / (2.0 * sigma * sigma)))
    bell = jnp.exp(-(offset * offset) / (2.0 * sigma * sigma)) / norm_sum
    value = 0.5 * (offset == 0.0).astype(jnp.float32) + 0.5 * bell
    return jnp.where(jnp.abs(offset) <= half, value, jnp.zeros_like(value))


def lon_matrix():
    first = jnp.arange(LON)[:, None]
    second = jnp.arange(LON)[None, :]
    offset = second - first
    return kernel_value(offset.astype(jnp.float32), HALF)


def band_rows(along_lon):
    padded = extended(along_lon, (("region", 2),), HALF)
    local_rows = along_lon.shape[2]
    out_rows = jnp.arange(local_rows)[:, None]
    in_rows = jnp.arange(local_rows + 2 * HALF)[None, :]
    lat_band = kernel_value((in_rows - HALF - out_rows).astype(jnp.float32), HALF)
    return jnp.einsum("rp,mvpk->mvrk", lat_band, padded, precision=lax.Precision.HIGHEST)


def smooth_surface(values):
    along_lon = jnp.einsum("mvrl,lk->mvrk", values, lon_matrix(), precision=lax.Precision.HIGHEST)
    return band_rows(along_lon)


def pair_terms(gathered):
    members = gathered.shape[0]
    inner_products = jnp.einsum(
        "mvkp,nvkp->vkmn", gathered, gathered, precision=lax.Precision.HIGHEST
    )
    squares = jnp.einsum("mvkp,mvkp->vkm", gathered, gathered, precision=lax.Precision.HIGHEST)
    dist_sq = jnp.maximum(
        squares[:, :, :, None] + squares[:, :, None, :] - 2.0 * inner_products, 0.0
    )
    self_pair = jnp.arange(members)[:, None] == jnp.arange(members)[None, :]
    pair_weights = jnp.where(
        self_pair[None, None], jnp.zeros_like(dist_sq), 1.0 / jnp.sqrt(dist_sq + 1e-06)
    )
    pulled = jnp.transpose(jnp.sum(pair_weights, axis=-1), (2, 0, 1))
    apart = pulled[..., None] * gathered - jnp.einsum(
        "vkmn,nvkp->mvkp", pair_weights, gathered, precision=lax.Precision.HIGHEST
    )
    apart = apart / members
    return lax.all_to_all(apart, "member", split_axis=0, concat_axis=2, tiled=True)


def reorder_cells(values, positions):
    cell_count = values.shape[-1]
    flattened = values.reshape(-1, cell_count).T
    reordered = jnp.take(flattened, positions, axis=0)
    return reordered.T.reshape(values.shape)


def on_device(predicted_states, observed_analysis, tile_location_sequence):
    local_ensemble_copies = predicted_states.shape[0]
    quantity_names = predicted_states.shape[1]
    mesh_locations = predicted_states.shape[2] * predicted_states.shape[3]
    blocks = mesh_locations // PATCH
    order = tile_location_sequence[0]
    inverse_order = (
        jnp.zeros((mesh_locations,), jnp.int32).at[order].set(jnp.arange(mesh_locations))
    )
    softened_surface = smooth_surface(predicted_states)
    picked = reorder_cells(
        softened_surface.reshape(local_ensemble_copies, quantity_names, mesh_locations), order
    )
    picked = picked.reshape(local_ensemble_copies, quantity_names, blocks, PATCH)
    truth = reorder_cells(observed_analysis.reshape(quantity_names, mesh_locations), order).reshape(
        quantity_names, blocks, PATCH
    )
    diff = picked - truth[None]
    toward = diff / jnp.sqrt(jnp.sum(diff * diff, axis=-1, keepdims=True) + 1e-06)
    apart = pair_terms(lax.all_to_all(picked, "member", split_axis=2, concat_axis=0, tiled=True))
    patch_grad = jnp.sqrt(jnp.float32(PATCH)) * (toward - apart)
    located_points = reorder_cells(
        patch_grad.reshape(local_ensemble_copies, quantity_names, mesh_locations), inverse_order
    )
    return smooth_surface(located_points.reshape(predicted_states.shape))


def solution(mesh):
    in_specs = (P("member", None, "region", None), P(None, "region", None), P("region", None))
    out_specs = P("member", None, "region", None)
    return jax.shard_map(
        on_device, mesh=mesh, in_specs=in_specs, out_specs=out_specs, check_vma=False
    )
```

profile of v0, /device:TPU:1, one launch (start us, length us, event | category | flops | bytes accessed | tf_op | source)
XLA Modules:
  0.0 349.0 jit_solution(8841044070534873520)
XLA Ops:
  1.9 5.8 %fusion.14 = f32[2,100,32,128]{3,1,2,0:T(8,128)S(1)} fusion(f32[2,100,32,128]{3,2,1,0:T(8,128)S(1)} %copy-done, f32[]{:T(128)} %exponential_reduce_fusion), kind=kOutput, calls=%fused_computation.29 | convolution fusion | flops 1258504192 | bytes 6553604 | tf_op jit(solution)/shard_map/mvrl,lk->mvrk/dot_general | solution.py:50
  9.4 4.5 %collective-permute-start = (f32[2,100,32,128]{3,2,1,0:T(8,128)S(1)}, f32[2,100,32,128]{3,2,1,0:T(8,128)S(1)}, u32[]{:S(2)}, u32[]{:S(2)}) collective-permute-start(f32[2,100,32,128]{3,2,1,0:T(8,128)S(1)} %copy.65), channel_id=1, source_target_pairs={{0,8},{8,16},{16,24},{1,9},{9,17},{17,25},{2,10},{10,18},{18,26},{... | collective-permute-start | bytes 9830408 | tf_op jit(solution)/shard_map/ppermute | solution.py:16
  16.1 33.4 %collective-permute-done = f32[2,100,32,128]{3,2,1,0:T(8,128)S(1)} collective-permute-done((f32[2,100,32,128]{3,2,1,0:T(8,128)S(1)}, f32[2,100,32,128]{3,2,1,0:T(8,128)S(1)}, u32[]{:S(2)}, u32[]{:S(2)}) %collective-permute-start) | collective-permute-done | bytes 3276832 | tf_op jit(solution)/shard_map/ppermute | solution.py:16
  57.7 8.5 %pad_maximum_fusion = f32[2,100,96,128]{3,1,2,0:T(8,128)} fusion(f32[2,100,32,128]{3,1,2,0:T(8,128)} %copy.68, f32[2,100,32,128]{3,1,2,0:T(8,128)} %copy-done.2, f32[2,100,32,128]{3,1,2,0:T(8,128)} %copy.67), kind=kLoop, calls=%fused_computation.4 | loop fusion | flops 4915200 | bytes 19660800 | tf_op jit(solution)/shard_map/concatenate | solution.py:20
  66.2 10.9 %fusion.6 = f32[2,100,128,32]{2,3,1,0:T(8,128)S(1)} fusion(f32[2,100,96,128]{3,1,2,0:T(8,128)} %pad_maximum_fusion, f32[]{:T(128)} %exponential_reduce_fusion, s32[96]{0:T(128)S(1)} %iota_add_fusion), kind=kOutput, calls=%fused_computation.11 | convolution fusion | flops 943758336 | bytes 13107588 | tf_op jit(solution)/shard_map/rp,mvpk->mvrk/dot_general | solution.py:46
  83.3 18.3 %gather_fusion.1 = f32[4096,200]{1,0:T(8,128)} fusion(f32[4096,200]{1,0:T(8,128)} %bitcast.86, s32[4096]{0:T(1024)S(1)} %fusion.25), kind=kCustom, calls=%fused_computation.clone | custom fusion | bytes 6569984 | tf_op jit(solution)/shard_map/jit(_take)/gather | solution.py:78
  107.9 4.2 %copy.74 = f32[2,100,32,128]{3,0,1,2:T(2,128)} copy(f32[2,100,32,128]{3,2,1,0:T(8,128)S(1)} %bitcast.91) | data formatting | bytes 6553600 | tf_op jit(solution)/shard_map/reshape;reshape | solution.py:95
  112.1 6.0 %all-to-all-start = ((f32[2,100,32,128]{3,0,1,2:T(2,128)}), f32[2,100,32,128]{3,0,1,2:T(2,128)S(1)}, u32[]{:S(2)}, u32[]{:S(2)}) async-start(f32[2,100,32,128]{3,0,1,2:T(2,128)} %copy.74), calls=%async_computation | async-start | bytes 6553600 | tf_op jit(solution)/shard_map/all_to_all | solution.py:101
  118.1 42.4 %all-to-all-done = f32[2,100,32,128]{3,0,1,2:T(2,128)S(1)} async-done(((f32[2,100,32,128]{3,0,1,2:T(2,128)}), f32[2,100,32,128]{3,0,1,2:T(2,128)S(1)}, u32[]{:S(2)}, u32[]{:S(2)}) %all-to-all-start) | async-done | bytes 3276832 | tf_op jit(solution)/shard_map/all_to_all | solution.py:101
  165.4 6.2 %fusion.46 = (f32[100,4,16]{2,1,0:T(4,128)S(1)}, f32[100,4,16,16]{2,3,1,0:T(8,128)S(1)}) fusion(f32[16,100,4,128]{3,0,2,1:T(8,128)S(1)} %bitcast.89, f32[100,4,16]{2,1,0:T(4,128)S(1)} %multiply_reduce_fusion, pred[16,16]{0,1:T(8,128)(4,1)S(1)} %iota_compare_fusion), kind=kOutput, calls=%fused_computation.74 | convolution fusion | flops 157996800 | bytes 3737856 | tf_op jit(solution)/shard_map/mvkp,nvkp->vkmn/dot_general | solution.py:56
  171.6 6.7 %fusion.13 = f32[16,100,4,128]{3,0,2,1:T(8,128)S(1)} fusion(f32[16,100,4,128]{3,0,2,1:T(8,128)S(1)} %bitcast.90, f32[100,4,16,16]{2,3,1,0:T(8,128)S(1)} %get-tuple-element.7, f32[16,100,4]{0,2,1:T(4,128)S(1)} %bitcast.102), kind=kOutput, calls=%fused_computation.23 | convolution fusion | flops 159744000 | bytes 6988800 | tf_op jit(solution)/shard_map/vkmn,nvkp->mvkp/dot_general | solution.py:68
  181.3 4.5 %all-to-all-start.1 = ((f32[16,100,4,128]{3,2,1,0:T(4,128)}), f32[16,100,4,128]{3,2,1,0:T(4,128)}, u32[]{:S(2)}, u32[]{:S(2)}) async-start(f32[16,100,4,128]{3,2,1,0:T(4,128)} %copy.78), calls=%async_computation.1 | async-start | bytes 6553600 | tf_op jit(solution)/shard_map/all_to_all | solution.py:72
  187.7 14.1 %gather_fusion = f32[4096,100]{1,0:T(8,128)} fusion(f32[4096,100]{1,0:T(8,128)S(1)} %bitcast.87, s32[4096]{0:T(1024)S(1)} %broadcast_clamp_fusion), kind=kCustom, calls=%fused_computation.2 | custom fusion | bytes 3293184 | tf_op jit(solution)/shard_map/jit(_take)/gather | solution.py:78
  201.8 4.8 %broadcast_select_fusion = f32[4096,100]{1,0:T(8,128)} fusion(f32[4096,100]{1,0:T(8,128)} %gather_fusion, pred[4096]{0:T(1024)(128)(4,1)S(1)} %compare_and_fusion.1), kind=kLoop, calls=%fused_computation.31 | loop fusion | flops 409600 | bytes 3280896 | tf_op jit(solution)/shard_map/jit(_take)/select_n | solution.py:78
  209.7 15.7 %scatter_custom_fusion = s32[4096]{0:T(1024)S(1)} fusion(s32[4096]{0:T(1024)S(1)} %bitcast.106, s32[4096]{0:T(1024)S(1)} %iota.51, s32[]{:T(128)} %constant.26.clone.1), kind=kCustom, calls=%fused_computation.53 | custom fusion | bytes 16388 | tf_op jit(solution)/shard_map/scatter | solution.py:89
  227.8 13.9 %all-to-all-done.1 = f32[16,100,4,128]{3,2,1,0:T(4,128)} async-done(((f32[16,100,4,128]{3,2,1,0:T(4,128)}), f32[16,100,4,128]{3,2,1,0:T(4,128)}, u32[]{:S(2)}, u32[]{:S(2)}) %all-to-all-start.1) | async-done | bytes 3276832 | tf_op jit(solution)/shard_map/all_to_all | solution.py:72
  251.3 8.4 %fusion.12 = f32[4096,200]{0,1:T(8,128)} fusion(f32[200,4096]{1,0:T(8,128)S(1)} %copy-done.8, f32[25,8,32,128]{3,2,1,0:T(8,128)S(1)} %bitcast.98, f32[25,8,32,128]{3,2,1,0:T(8,128)S(1)} %bitcast.99, f32[4096,200]{0,1:T(8,128)S(1)} %copy-done.6, pred[4096]{0:T(1024)(128)(4,1)S(1)} %compare_and_fusion.1), kind=kLoop, calls=%fused_computation.19 | loop fusion | flops 4096000 | bytes 16388096 | tf_op jit(solution)/shard_map/transpose | solution.py:77
  259.7 5.4 %copy.80 = f32[4096,200]{1,0:T(8,128)} copy(f32[4096,200]{0,1:T(8,128)} %fusion.12) | data formatting | bytes 6553600 | tf_op jit(solution)/shard_map/transpose | solution.py:77
  265.1 18.3 %gather_fusion.2 = f32[4096,200]{1,0:T(8,128)} fusion(f32[4096,200]{1,0:T(8,128)} %copy.80, s32[4096]{0:T(1024)S(1)} %fusion.26), kind=kCustom, calls=%fused_computation.1.clone | custom fusion | bytes 6569984 | tf_op jit(solution)/shard_map/jit(_take)/gather | solution.py:78
  283.4 3.9 %select_bitcast_fusion = f32[200,4096]{0,1:T(8,128)} fusion(f32[4096,200]{1,0:T(8,128)} %gather_fusion.2, pred[4096]{0:T(1024)(128)(4,1)S(1)} %compare_and_fusion), kind=kLoop, calls=%fused_computation.13 | loop fusion | flops 819200 | bytes 6557696 | tf_op jit(solution)/shard_map/transpose | solution.py:79
  287.3 5.3 %copy.81 = f32[200,4096]{1,0:T(8,128)} copy(f32[200,4096]{0,1:T(8,128)} %select_bitcast_fusion) | data formatting | bytes 6553600 | tf_op jit(solution)/shard_map/transpose | solution.py:79
  303.1 33.0 %collective-permute-done.2 = f32[2,100,32,128]{3,2,1,0:T(8,128)S(1)} collective-permute-done((f32[2,100,32,128]{3,2,1,0:T(8,128)S(1)}, f32[2,100,32,128]{3,2,1,0:T(8,128)S(1)}, u32[]{:S(2)}, u32[]{:S(2)}) %collective-permute-start.2) | collective-permute-done | bytes 3276832 | tf_op jit(solution)/shard_map/ppermute | solution.py:16
  336.1 4.4 %collective-permute-done.3 = f32[2,100,32,128]{3,2,1,0:T(8,128)S(1)} collective-permute-done((f32[2,100,32,128]{3,2,1,0:T(8,128)S(1)}, f32[2,100,32,128]{3,2,1,0:T(8,128)S(1)}, u32[]{:S(2)}, u32[]{:S(2)}) %collective-permute-start.3) | collective-permute-done | bytes 3276832 | tf_op jit(solution)/shard_map/ppermute | solution.py:19
  340.5 8.0 %fusion.17 = f32[2,100,32,128]{3,2,1,0:T(8,128)} fusion(f32[2,100,32,128]{3,2,1,0:T(8,128)S(1)} %collective-permute-done.3, f32[2,100,32,128]{3,2,1,0:T(8,128)S(1)} %fusion.20, f32[2,100,32,128]{3,2,1,0:T(8,128)S(1)} %collective-permute-done.2, f32[]{:T(128)} %exponential_reduce_fusion, s32[96]{0:T(128)S(1)} %iota_add_fusion), kind=kOutput, calls=%fused_computation.30 | convolution fusion | flops 948673536 | bytes 13107588 | tf_op jit(solution)/shard_map/rp,mvpk->mvrk/dot_general | solution.py:46
  (56 shorter events, 61.5 us)
Async XLA Ops:
  0.0 1.9 copy-start
  7.7 1.7 copy-start.2
  7.8 8.4 %copy-start.9 = (s32[1,4096]{1,0:T(1,128)S(1)}, s32[1,4096]{1,0:T(1,128)}, u32[]{:S(2)}) copy-start(s32[1,4096]{1,0:T(1,128)} %param.7) | copy-start | bytes 49156
  9.4 40.1 %collective-permute-start = (f32[2,100,32,128]{3,2,1,0:T(8,128)S(1)}, f32[2,100,32,128]{3,2,1,0:T(8,128)S(1)}, u32[]{:S(2)}, u32[]{:S(2)}) collective-permute-start(f32[2,100,32,128]{3,2,1,0:T(8,128)S(1)} %copy.65), channel_id=1, source_target_pairs={{0,8},{8,16},{16,24},{1,9},{9,17},{17,25},{2,10},{10,18},{18,26},{... | collective-permute-start | bytes 9830408 | tf_op jit(solution)/shard_map/ppermute | solution.py:16
  14.0 40.0 %collective-permute-start.1 = (f32[2,100,32,128]{3,2,1,0:T(8,128)S(1)}, f32[2,100,32,128]{3,2,1,0:T(8,128)S(1)}, u32[]{:S(2)}, u32[]{:S(2)}) collective-permute-start(f32[2,100,32,128]{3,2,1,0:T(8,128)S(1)} %copy.65), channel_id=1, source_target_pairs={{8,0},{16,8},{24,16},{9,1},{17,9},{25,17},{10,2},{18,10},{26,18},{... | collective-permute-start | bytes 9830408 | tf_op jit(solution)/shard_map/ppermute | solution.py:19
  105.4 1.7 copy-start.5
  107.9 4.2 %copy-start.3 = (f32[25,8,32,128]{3,2,1,0:T(8,128)}, f32[25,8,32,128]{3,2,1,0:T(8,128)S(1)}, u32[]{:S(2)}) copy-start(f32[25,8,32,128]{3,2,1,0:T(8,128)S(1)} %copy.92) | copy-start | bytes 9830404
  112.1 48.4 %all-to-all-start = ((f32[2,100,32,128]{3,0,1,2:T(2,128)}), f32[2,100,32,128]{3,0,1,2:T(2,128)S(1)}, u32[]{:S(2)}, u32[]{:S(2)}) async-start(f32[2,100,32,128]{3,0,1,2:T(2,128)} %copy.74), calls=%async_computation | async-start | bytes 6553600 | tf_op jit(solution)/shard_map/all_to_all | solution.py:101
  181.3 60.5 %all-to-all-start.1 = ((f32[16,100,4,128]{3,2,1,0:T(4,128)}), f32[16,100,4,128]{3,2,1,0:T(4,128)}, u32[]{:S(2)}, u32[]{:S(2)}) async-start(f32[16,100,4,128]{3,2,1,0:T(4,128)} %copy.78), calls=%async_computation.1 | async-start | bytes 6553600 | tf_op jit(solution)/shard_map/all_to_all | solution.py:72
  201.8 23.6 %copy-start.4 = (f32[25,8,32,128]{3,2,1,0:T(8,128)S(1)}, f32[25,8,32,128]{3,2,1,0:T(8,128)}, u32[]{:S(2)}) copy-start(f32[25,8,32,128]{3,2,1,0:T(8,128)} %copy-done.3) | copy-start | bytes 9830404
  247.7 1.4 copy-start.7
  247.7 2.4 copy-start.8
  248.6 2.7 copy-start.6
  298.6 37.5 %collective-permute-start.2 = (f32[2,100,32,128]{3,2,1,0:T(8,128)S(1)}, f32[2,100,32,128]{3,2,1,0:T(8,128)S(1)}, u32[]{:S(2)}, u32[]{:S(2)}) collective-permute-start(f32[2,100,32,128]{3,2,1,0:T(8,128)S(1)} %fusion.20), channel_id=1, source_target_pairs={{0,8},{8,16},{16,24},{1,9},{9,17},{17,25},{2,10},{10,18},{18,26},{... | collective-permute-start | bytes 9830408 | tf_op jit(solution)/shard_map/ppermute | solution.py:16
  300.5 40.0 %collective-permute-start.3 = (f32[2,100,32,128]{3,2,1,0:T(8,128)S(1)}, f32[2,100,32,128]{3,2,1,0:T(8,128)S(1)}, u32[]{:S(2)}, u32[]{:S(2)}) collective-permute-start(f32[2,100,32,128]{3,2,1,0:T(8,128)S(1)} %fusion.20), channel_id=1, source_target_pairs={{8,0},{16,8},{24,16},{9,1},{17,9},{25,17},{10,2},{18,10},{26,18},{... | collective-permute-start | bytes 9830408 | tf_op jit(solution)/shard_map/ppermute | solution.py:19
  340.5 8.0 %copy-start.1 = (f32[2,100,32,128]{3,2,1,0:T(8,128)S(1)}, f32[2,100,32,128]{3,2,1,0:T(8,128)}, u32[]{:S(2)}) copy-start(f32[2,100,32,128]{3,2,1,0:T(8,128)} %param.5) | copy-start | bytes 9830404
where the time goes:
time: 355 us; the launch traced here: 349 us
  local copies, waits for them, and re-layouts  128 us (36%)
  waiting for transfers between devices  128 us (36%)
  matrix products  41.1 us (12%)
  other arithmetic  30.1 us (8%)
  starting transfers between devices  21.6 us (6%)
    ppermute x2, waiting for transfers between devices, extended(): lax.ppermute(lax.slice_in_dim(block, block.shape[dim] - width, None, axis...  66.4 us
    gather x4, local copies, waits for them, and re-layouts, reorder_cells(): reordered = jnp.take(flattened, positions, axis=0)  54.4 us
    all_to_all x1, waiting for transfers between devices, on_device(): lax.all_to_all(picked, 'member', split_axis=2, concat_axis=0, tiled=True)  42.4 us
    dot_general x2, matrix products, band_rows(): jnp.einsum('rp,mvpk->mvrk', lat_band, padded, precision=lax.Precision.HIG...  19 us
    scatter x1, local copies, waits for them, and re-layouts, on_device(): jnp.zeros((mesh_locations,), jnp.int32).at[order]  15.7 us
    unnamed x24, local copies, waits for them, and re-layouts  14.1 us
    all_to_all x1, waiting for transfers between devices, pair_terms(): lax.all_to_all(apart, 'member', split_axis=0, concat_axis=2, tiled=True)  13.9 us
    dot_general x2, matrix products, smooth_surface(): jnp.einsum('mvrl,lk->mvrk', values, lon_matrix(), precision=lax.Precision...  9.23 us
  transfers between devices with their start and end apart: 6, of which 6 were waited for; matrix products, arithmetic and copies ran while one was open for 13% of the time, Pallas kernels for 0%

commit v1 on v0

v1 whole, which is shorter than its diff:
```python
import functools

import jax
import jax.numpy as jnp
import numpy as np
from jax import lax
from jax.experimental import pallas as pl
from jax.experimental.pallas import tpu as pltpu
from jax.sharding import PartitionSpec as P

HALF = 32
PATCH = 128
EPS = 1e-06
STEP = 4
VMEM = 56 * 1024 * 1024
F32 = jnp.float32
BF16 = jnp.bfloat16


def bell(out_cells, in_cells):
    sigma = HALF / 2.0
    steps = np.arange(-HALF, HALF + 1)
    norm = np.sum(np.exp(-(steps**2) / (2.0 * sigma**2)))
    offset = np.asarray(in_cells)[None, :] - np.asarray(out_cells)[:, None]
    value = 0.5 * np.exp(-(offset**2) / (2.0 * sigma**2)) / norm
    value = jnp.asarray(np.where(np.abs(offset) <= HALF, value, 0.0), F32)
    return halves(value)


def halves(x):
    head = x.astype(BF16)
    return head, (x - head.astype(F32)).astype(BF16)


def lon_weights(lon):
    head, tail = bell(range(lon), range(lon))
    return jnp.concatenate([head, head, tail], axis=0)


def lat_weights(rows, pad):
    head, tail = bell(range(rows), range(-pad, rows + pad))
    return jnp.concatenate([head, head, tail], axis=1)


def along_lon(x, weights):
    head, tail = halves(x)
    return 0.5 * x + jnp.dot(
        jnp.concatenate([head, tail, head], axis=1), weights, preferred_element_type=F32
    )


def along_lat(x, weights, own):
    head, tail = halves(x)
    return 0.5 * own + jnp.dot(
        weights, jnp.concatenate([head, tail, head], axis=0), preferred_element_type=F32
    )


def patch_sums(squares, hot):
    head, tail = halves(squares)
    return lax.dot_general(
        jnp.concatenate([head, tail], axis=0),
        hot,
        (((1,), (1,)), ((), ())),
        preferred_element_type=F32,
    )


def on_cells(weights, hot):
    return jnp.dot(weights, jnp.concatenate([hot, hot], axis=0), preferred_element_type=F32)


def head_and_tail(weights):
    return jnp.concatenate(halves(weights), axis=1)


def field_kernel(
    regions, me_ref, field_ref, truth_ref, map_ref, lon_ref, lat_ref, out_ref, cells, hots
):
    sources, _, held, rows, lon = field_ref.shape
    devices = sources // regions
    members = devices * held
    steps = rows // STEP
    patches = hots.shape[1]
    shifts = members // 2
    scale = float(np.sqrt(PATCH))

    @pl.when(pl.program_id(0) == 0)
    def _():
        patch = lax.broadcasted_iota(jnp.int32, (patches, lon), 0).astype(F32)

        def build(block, carry):
            for j in range(STEP):
                own = map_ref[pl.ds(block * STEP + j, 1), :]
                hots[block, :, j * lon : (j + 1) * lon] = (patch == own).astype(BF16)
            return carry

        lax.fori_loop(0, regions * steps, build, 0)

    def smoothed(pair):
        wide = jnp.concatenate([along_lon(x, lon_ref[...]) for x in pair], axis=1)
        return along_lat(wide, lat_ref[...], wide)

    every = regions * rows
    for device in range(devices):
        pair = [
            jnp.concatenate(
                [field_ref[region * devices + device, 0, k] for region in range(regions)], axis=0
            )
            for k in range(held)
        ]
        result = smoothed(pair)
        for k in range(held):
            cells[pl.ds(device * held + k, every, stride=members), :] = result[
                :, k * lon : (k + 1) * lon
            ]

    for region in range(regions):
        own_truth = lax.rem(me_ref[0] - region + regions, regions)

        def load(step, j):
            row = step * STEP + j
            start = pl.multiple_of((region * rows + row) * members, members)
            a = cells[pl.ds(start, members), :]
            return start, a, a - truth_ref[own_truth, 0, pl.ds(row, 1), :]

        def first(step, total):
            columns = []
            for j in range(STEP):
                _, a, miss = load(step, j)
                gaps = [a - pltpu.roll(a, s, 0) for s in range(1, shifts + 1)] + [miss]
                columns.append(jnp.concatenate([gap * gap for gap in gaps], axis=0))
            squares = jnp.concatenate(columns, axis=1)
            return total + patch_sums(squares, hots[region * steps + step])

        height = (shifts + 1) * members
        total = lax.fori_loop(0, steps, first, jnp.zeros((2 * height, patches), F32))
        weights = lax.rsqrt(total[:height] + total[height:] + EPS)
        factor = jnp.where(
            lax.broadcasted_iota(jnp.int32, (height, patches), 0) < shifts * members,
            -scale / members,
            scale,
        )
        weights = head_and_tail(weights * factor)

        def second(step, carry):
            spread = on_cells(weights, hots[region * steps + step])
            for j in range(STEP):
                start, a, miss = load(step, j)
                w = spread[:, j * lon : (j + 1) * lon]
                h = w[shifts * members :] * miss
                for s in range(1, shifts + 1):
                    pull = w[(s - 1) * members : s * members] * (a - pltpu.roll(a, s, 0))
                    h = h + pull
                    if 2 * s != members:
                        h = h - pltpu.roll(pull, members - s, 0)
                cells[pl.ds(start, members), :] = h
            return carry

        lax.fori_loop(0, steps, second, 0)

    for device in range(devices):
        result = smoothed(
            [cells[pl.ds(device * held + k, every, stride=members), :] for k in range(held)]
        )
        for region in range(regions):
            for k in range(held):
                out_ref[region * devices + device, 0, k] = result[
                    region * rows : (region + 1) * rows, k * lon : (k + 1) * lon
                ]


def whole_fields(fields, truth, patch_map, regions):
    sources, count, held, rows, lon = fields.shape
    members = sources // regions * held
    patches = rows * lon // PATCH
    every = regions * rows
    me = lax.axis_index("region").reshape(1)
    block = pl.BlockSpec((sources, 1, held, rows, lon), lambda v, me: (0, v, 0, 0, 0))
    pairs = every * lon * members * (members // 2 + 1)
    return pl.pallas_call(
        functools.partial(field_kernel, regions),
        out_shape=jax.ShapeDtypeStruct(fields.shape, F32),
        grid_spec=pltpu.PrefetchScalarGridSpec(
            num_scalar_prefetch=1,
            grid=(count,),
            in_specs=[
                block,
                pl.BlockSpec((regions, 1, rows, lon), lambda v, me: (0, v, 0, 0)),
                pl.BlockSpec((every, lon), lambda v, me: (0, 0)),
                pl.BlockSpec((3 * lon, lon), lambda v, me: (0, 0)),
                pl.BlockSpec((every, 3 * every), lambda v, me: (0, 0)),
            ],
            out_specs=block,
            scratch_shapes=[
                pltpu.VMEM((every * members, lon), F32),
                pltpu.VMEM((every // STEP, patches, STEP * lon), BF16),
            ],
        ),
        compiler_params=pltpu.CompilerParams(vmem_limit_bytes=VMEM),
        cost_estimate=pl.CostEstimate(
            flops=count * pairs * patches * 8, bytes_accessed=8 * fields.size, transcendentals=0
        ),
        name="whole_fields",
    )(me, fields, truth, patch_map, lon_weights(lon), lat_weights(every, 0))


def smooth_kernel(own_ref, low_ref, high_ref, lon_ref, lat_ref, out_ref):
    held = own_ref.shape[0]
    for k in range(held):
        rows = [ref[k, 0] for ref in (low_ref, own_ref, high_ref)]
        wide = along_lon(jnp.concatenate(rows, axis=0), lon_ref[...])
        pad = rows[0].shape[0]
        out_ref[k, 0] = along_lat(wide, lat_ref[...], wide[pad : pad + rows[1].shape[0]])


def smoothed_rows(own):
    held, count, rows, lon = own.shape
    regions = lax.axis_size("region")
    up = [(i, i + 1) for i in range(regions - 1)]
    low = lax.ppermute(own[:, :, rows - HALF :], "region", up)
    high = lax.ppermute(own[:, :, :HALF], "region", [(b, a) for a, b in up])
    edge = pl.BlockSpec((held, 1, HALF, lon), lambda v: (0, v, 0, 0))
    block = pl.BlockSpec((held, 1, rows, lon), lambda v: (0, v, 0, 0))
    span = rows + 2 * HALF
    return pl.pallas_call(
        smooth_kernel,
        out_shape=jax.ShapeDtypeStruct(own.shape, F32),
        grid=(count,),
        in_specs=[
            block,
            edge,
            edge,
            pl.BlockSpec((3 * lon, lon), lambda v: (0, 0)),
            pl.BlockSpec((rows, 3 * span), lambda v: (0, 0)),
        ],
        out_specs=block,
        compiler_params=pltpu.CompilerParams(vmem_limit_bytes=VMEM),
        name="smoothed_rows",
    )(own, low, high, lon_weights(lon), lat_weights(rows, HALF))


def share_kernel(all_ref, own_ref, truth_ref, map_ref, out_ref, cells, hots):
    devices, held, _, rows, lon = all_ref.shape
    members = devices * held
    patches = hots.shape[1]
    scale = float(np.sqrt(PATCH))
    steps = rows // STEP

    @pl.when(pl.program_id(0) == 0)
    def _():
        patch = lax.broadcasted_iota(jnp.int32, (patches, lon), 0).astype(F32)
        for row in range(rows):
            hots[row // STEP, :, row % STEP * lon : (row % STEP + 1) * lon] = (
                patch == map_ref[row : row + 1, :]
            ).astype(BF16)

    for device in range(devices):
        for k in range(held):
            cells[pl.ds(device * held + k, rows, stride=members), :] = all_ref[device, k, 0]

    def gaps(step, j):
        row = step * STEP + j
        a = cells[pl.ds(pl.multiple_of(row * members, members), members), :]
        truth = truth_ref[0, pl.ds(row, 1), :]
        result = []
        for k in range(held):
            own = own_ref[k, 0, pl.ds(row, 1), :]
            result += [own - a, jnp.broadcast_to(own - truth, (8, lon))]
        return row, result

    def first(step, total):
        columns = [
            jnp.concatenate([gap * gap for gap in gaps(step, j)[1]], axis=0) for j in range(STEP)
        ]
        return total + patch_sums(jnp.concatenate(columns, axis=1), hots[step])

    height = held * (members + 8)
    total = lax.fori_loop(0, steps, first, jnp.zeros((2 * height, patches), F32))
    weights = lax.rsqrt(total[:height] + total[height:] + EPS)
    place = lax.rem(lax.broadcasted_iota(jnp.int32, (height, patches), 0), members + 8)
    weights = head_and_tail(weights * jnp.where(place < members, -scale / members, scale))

    def second(step, carry):
        spread = on_cells(weights, hots[step])
        for j in range(STEP):
            row, parts = gaps(step, j)
            w = spread[:, j * lon : (j + 1) * lon]
            for k in range(held):
                base = k * (members + 8)
                pull = w[base : base + members] * parts[2 * k]
                toward = w[base + members : base + members + 1] * parts[2 * k + 1][:1]
                out_ref[k, 0, pl.ds(row, 1), :] = toward + jnp.sum(pull, axis=0, keepdims=True)
        return carry

    lax.fori_loop(0, steps, second, 0)


def own_members(smooth, truth, patch_map):
    held, count, rows, lon = smooth.shape
    devices = lax.axis_size("member")
    patches = rows * lon // PATCH
    everyone = lax.all_gather(smooth, "member")
    block = pl.BlockSpec((held, 1, rows, lon), lambda v: (0, v, 0, 0))
    return pl.pallas_call(
        share_kernel,
        out_shape=jax.ShapeDtypeStruct(smooth.shape, F32),
        grid=(count,),
        in_specs=[
            pl.BlockSpec((devices, held, 1, rows, lon), lambda v: (0, 0, v, 0, 0)),
            block,
            pl.BlockSpec((1, rows, lon), lambda v: (v, 0, 0)),
            pl.BlockSpec((rows, lon), lambda v: (0, 0)),
        ],
        out_specs=block,
        scratch_shapes=[
            pltpu.VMEM((rows * devices * held, lon), F32),
            pltpu.VMEM((rows // STEP, patches, STEP * lon), BF16),
        ],
        compiler_params=pltpu.CompilerParams(vmem_limit_bytes=VMEM),
        name="own_members",
    )(everyone, smooth, truth, patch_map)


def patch_of_cell(order, rows, lon):
    position = jnp.arange(rows * lon, dtype=jnp.int32)
    in_row = jnp.arange(rows, dtype=jnp.int32)[:, None] == (order // lon)[None]
    at_lon = (order % lon)[:, None] == jnp.arange(lon, dtype=jnp.int32)[None]
    patch = jnp.where(in_row, (position // PATCH)[None], 0)
    return jnp.dot(
        patch.astype(F32), at_lon.astype(F32), precision=lax.Precision.HIGHEST
    )


def on_device(predicted_states, observed_analysis, tile_location_sequence):
    held, variables, rows, lon = predicted_states.shape
    regions, devices = lax.axis_size("region"), lax.axis_size("member")
    total = regions * devices
    share = variables // total
    whole = share * total
    patch_map = patch_of_cell(tile_location_sequence[0], rows, lon)
    parts = []
    if share:
        region, member = lax.axis_index("region"), lax.axis_index("member")
        maps = lax.all_gather(patch_map, "region").reshape(regions * rows, lon)
        truth = []
        for shift in range(regions):
            owner = lax.rem(region + shift, regions) * devices + member
            piece = lax.dynamic_slice_in_dim(observed_analysis, owner * share, share, axis=0)
            if shift:
                piece = lax.ppermute(
                    piece, "region", [(i, (i + shift) % regions) for i in range(regions)]
                )
            truth.append(piece)
        truth = jnp.stack(truth)
        sent = predicted_states[:, :whole].reshape(held, total, share, rows, lon)
        fields = lax.all_to_all(
            jnp.transpose(sent, (1, 2, 0, 3, 4)), ("region", "member"), 0, 0, tiled=True
        )
        result = whole_fields(fields, truth, maps, regions)
        result = lax.all_to_all(result, ("region", "member"), 0, 0, tiled=True)
        parts.append(jnp.transpose(result, (2, 0, 1, 3, 4)).reshape(held, whole, rows, lon))
    if whole < variables:
        smooth = smoothed_rows(predicted_states[:, whole:])
        h = own_members(smooth, observed_analysis[whole:], patch_map)
        parts.append(smoothed_rows(h))
    return jnp.concatenate(parts, axis=1)


def solution(mesh):
    in_specs = (P("member", None, "region", None), P(None, "region", None), P("region", None))
    out_specs = P("member", None, "region", None)
    return jax.shard_map(
        on_device, mesh=mesh, in_specs=in_specs, out_specs=out_specs, check_vma=False
    )
```

time: 355 us -> 274 us (0.77); the launches traced: 349 us -> 273 us
  local copies, waits for them, and re-layouts: 128 us -> 10.3 us
  Pallas kernels: 0 us -> 76.6 us
  matrix products: 41.1 us -> 1 us
  other arithmetic: 30.1 us -> 3.78 us
  blocking collectives: 0 us -> 19.3 us
  between operations: 0.75 us -> 13.5 us
  waiting for transfers between devices: 128 us -> 122 us
  starting transfers between devices: 21.6 us -> 26.7 us
    pallas_call x0 -> x4, Pallas kernels: none -> 76.6 us  [the longest x1 56.6 us: whole_fields(): pl.pallas_call(functools.partial(field_kernel, regions), out_shape=jax.Sh...]
    all_gather x0 -> x1, waiting for transfers between devices: none -> 55.3 us  [own_members(): everyone = lax.all_gather(smooth, 'member')]
    gather x4 -> x0, local copies, waits for them, and re-layouts: 54.4 us -> none  [reorder_cells(): reordered = jnp.take(flattened, positions, axis=0)]
    ppermute x4 -> x7, waiting for transfers between devices: 71.6 us -> 18 us  [the longest x2 11.7 us: smoothed_rows(): low = lax.ppermute(own[:, :, rows - HALF:], 'region', up)]
    dot_general x6 -> x1, matrix products: 41.1 us -> 1 us  [patch_of_cell(): jnp.dot(patch.astype(F32), at_lon.astype(F32), precision=lax.Precision.HI...]
    all_gather x0 -> x1, blocking collectives: none -> 19.3 us  [on_device(): maps = lax.all_gather(patch_map, 'region').reshape(regions * rows, lon)]
    scatter x1 -> x0, local copies, waits for them, and re-layouts: 15.7 us -> none  [on_device(): jnp.zeros((mesh_locations,), jnp.int32).at[order]]
    transpose x2 -> x0, other arithmetic: 12.3 us -> none  [the longest x1 8.39 us: reorder_cells(): flattened = values.reshape(-1, cell_count).T]
  transfers between devices with their start and end apart: 6 -> 10, of which waited for: 6 -> 6; matrix products, arithmetic and copies ran while one was open for 13% -> 2% of each run, Pallas kernels for 0% -> 7%
where the time goes in v1:
time: 274 us; the launch traced here: 273 us
  waiting for transfers between devices  122 us (45%)
  Pallas kernels  76.6 us (28%)
  starting transfers between devices  26.7 us (10%)
  blocking collectives  19.3 us (7%)
  between operations  13.5 us (5%)
  local copies, waits for them, and re-layouts  10.3 us (4%)
  other arithmetic  3.78 us (1%)
    pallas_call x1, Pallas kernels, whole_fields(): pl.pallas_call(functools.partial(field_kernel, regions), out_shape=jax.Sh...  56.6 us
    all_gather x1, waiting for transfers between devices, own_members(): everyone = lax.all_gather(smooth, 'member')  55.3 us
    all_to_all x1, waiting for transfers between devices, on_device(): lax.all_to_all(jnp.transpose(sent, (1, 2, 0, 3, 4)), ('region', 'member')...  48.4 us
    all_gather x1, blocking collectives, on_device(): maps = lax.all_gather(patch_map, 'region').reshape(regions * rows, lon)  19.3 us
    pallas_call x1, Pallas kernels, own_members(): pl.pallas_call(share_kernel, out_shape=jax.ShapeDtypeStruct(smooth.shape,...  12.1 us
    ppermute x2, waiting for transfers between devices, smoothed_rows(): low = lax.ppermute(own[:, :, rows - HALF:], 'region', up)  11.7 us
    ppermute x2, starting transfers between devices, smoothed_rows(): low = lax.ppermute(own[:, :, rows - HALF:], 'region', up)  10.5 us
    pallas_call x2, Pallas kernels, smoothed_rows(): pl.pallas_call(smooth_kernel, out_shape=jax.ShapeDtypeStruct(own.shape, F...  7.89 us
  transfers between devices with their start and end apart: 10, of which 6 were waited for; matrix products, arithmetic and copies ran while one was open for 2% of the time, Pallas kernels for 7%

profile of v1, /device:TPU:1, one launch (start us, length us, event | category | flops | bytes accessed | tf_op | source)
XLA Modules:
  0.0 273.0 jit_solution(16179201166651954051)
XLA Ops:
  6.5 1.9 slice-done
  8.4 2.1 copy.12
  10.5 7.1 %all-to-all-start = ((f32[32,3,2,32,128]{4,3,2,1,0:T(8,128)}), f32[32,3,2,32,128]{4,3,2,1,0:T(8,128)S(1)}, u32[]{:S(2)}, u32[]{:S(2)}) async-start(f32[32,3,2,32,128]{4,3,2,1,0:T(8,128)} %bitcast.18), calls=%async_computation | async-start | bytes 6291456 | tf_op jit(solution)/shard_map/all_to_all | solution.py:357
  18.6 1.7 collective-permute-start
  20.9 1.0 fusion.map_ref
  21.9 19.3 %all-gather.map_ref = f32[128,128]{1,0:T(8,128)} all-gather(f32[32,128]{1,0:T(8,128)S(1)} %fusion.map_ref), channel_id=2, replica_groups=mesh['region'=4,'member'=8] {'region'}, dimensions={0}, use_global_device_ids=true | all-gather | bytes 81920 | tf_op jit(solution)/shard_map/all_gather | solution.py:345
  41.9 48.4 %all-to-all-done.field_ref = f32[32,3,2,32,128]{4,3,2,1,0:T(8,128)S(1)} async-done(((f32[32,3,2,32,128]{4,3,2,1,0:T(8,128)}), f32[32,3,2,32,128]{4,3,2,1,0:T(8,128)S(1)}, u32[]{:S(2)}, u32[]{:S(2)}) %all-to-all-start) | async-done | bytes 3145760 | tf_op jit(solution)/shard_map/all_to_all | solution.py:357
  90.3 1.7 copy-done
  92.0 56.6 %whole_fields.1 = f32[32,3,2,32,128]{4,3,2,1,0:T(8,128)} custom-call(s32[1]{0:T(128)} %bitcast.me_ref, f32[32,3,2,32,128]{4,3,2,1,0:T(8,128)} %copy-done, f32[4,3,32,128]{3,2,1,0:T(8,128)} %pad_maximum_fusion.1.truth_ref, f32[128,128]{1,0:T(8,128)} %all-gather.map_ref, bf16[384,128]{1,0:T(8,128)(2,1)} %constant.76.lon_ref, bf16[128,384]{1,0:T(8,128)(2,1)} %constant.77.lat_ref), custom_call_target="tpu_custom_call" | custom-call | flops 1811939328 | bytes 6291456 | tf_op jit(solution)/shard_map/whole_fields/pallas_call | solution.py:181
  148.6 3.0 %all-to-all-start.1 = ((f32[32,3,2,32,128]{4,3,2,1,0:T(8,128)}), f32[32,3,2,32,128]{4,3,2,1,0:T(8,128)S(1)}, u32[]{:S(2)}, u32[]{:S(2)}) async-start(f32[32,3,2,32,128]{4,3,2,1,0:T(8,128)} %whole_fields.1), calls=%async_computation.1 | async-start | bytes 6291456 | tf_op jit(solution)/shard_map/all_to_all | solution.py:361
  151.7 0.9 slice.10.own_ref
  152.6 3.5 %collective-permute-start.3 = (f32[2,4,32,128]{3,2,1,0:T(8,128)S(1)}, f32[2,4,32,128]{3,2,1,0:T(8,128)S(1)}, u32[]{:S(2)}, u32[]{:S(2)}) collective-permute-start(f32[2,4,32,128]{3,2,1,0:T(8,128)S(1)} %slice.10.own_ref), channel_id=1, source_target_pairs={{0,8},{8,16},{16,24},{1,9},{9,17},{17,25},{2,10},{10,18},{18,26},{... | collective-permute-start | bytes 393224 | tf_op jit(solution)/shard_map/ppermute | solution.py:221
  156.2 1.9 collective-permute-start.4
  158.1 11.3 %collective-permute-done.3.low_ref = f32[2,4,32,128]{3,2,1,0:T(8,128)S(1)} collective-permute-done((f32[2,4,32,128]{3,2,1,0:T(8,128)S(1)}, f32[2,4,32,128]{3,2,1,0:T(8,128)S(1)}, u32[]{:S(2)}, u32[]{:S(2)}) %collective-permute-start.3) | collective-permute-done | bytes 131104 | tf_op jit(solution)/shard_map/ppermute | solution.py:221
  169.4 2.1 collective-permute-done.4.high_ref
  172.2 3.9 %smoothed_rows.2.own_ref = f32[2,4,32,128]{3,2,1,0:T(8,128)} custom-call(f32[2,4,32,128]{3,2,1,0:T(8,128)} %copy-done.1, f32[2,4,32,128]{3,2,1,0:T(8,128)} %copy-done.3, f32[2,4,32,128]{3,2,1,0:T(8,128)} %copy-done.5, bf16[384,128]{1,0:T(8,128)(2,1)} %constant.76.lon_ref, bf16[32,288]{1,0:T(8,128)(2,1)} %constant.82.lat_ref), custom_call_target="tpu_custom_call" | custom-call | tf_op jit(solution)/shard_map/smoothed_rows/pallas_call | solution.py:226
  176.2 1.5 slice.11.truth_ref
  177.7 55.3 %all-gather.4.cloned.1.call-done = f32[16,4,32,128]{3,2,1,0:T(8,128)} async-done(((f32[2,4,32,128]{3,2,1,0:T(8,128)}), f32[16,4,32,128]{3,2,1,0:T(8,128)}) %all-gather.4.cloned.1.call-update) | async-done | bytes 1048592 | tf_op jit(solution)/shard_map/all_gather | solution.py:303
  233.0 12.1 %own_members.1.own_ref = f32[2,4,32,128]{3,2,1,0:T(8,128)} custom-call(f32[8,2,4,32,128]{4,3,2,1,0:T(8,128)} %bitcast.19, f32[2,4,32,128]{3,2,1,0:T(8,128)} %smoothed_rows.2.own_ref, f32[4,32,128]{2,1,0:T(8,128)} %slice.11.truth_ref, f32[32,128]{1,0:T(8,128)} %copy-done.6), custom_call_target="tpu_custom_call" | custom-call | tf_op jit(solution)/shard_map/own_members/pallas_call | solution.py:305
  245.1 6.9 %collective-permute-start.5 = (f32[2,4,32,128]{3,2,1,0:T(8,128)}, f32[2,4,32,128]{3,2,1,0:T(8,128)S(1)}, u32[]{:S(2)}, u32[]{:S(2)}) collective-permute-start(f32[2,4,32,128]{3,2,1,0:T(8,128)} %own_members.1.own_ref), channel_id=1, source_target_pairs={{0,8},{8,16},{16,24},{1,9},{9,17},{17,25},{2,10},{10,18},{18,26},{... | collective-permute-start | bytes 393224 | tf_op jit(solution)/shard_map/ppermute | solution.py:221
  252.1 1.9 collective-permute-start.6
  254.3 4.3 %collective-permute-done.6.high_ref = f32[2,4,32,128]{3,2,1,0:T(8,128)S(1)} collective-permute-done((f32[2,4,32,128]{3,2,1,0:T(8,128)}, f32[2,4,32,128]{3,2,1,0:T(8,128)S(1)}, u32[]{:S(2)}, u32[]{:S(2)}) %collective-permute-start.6) | collective-permute-done | bytes 131104 | tf_op jit(solution)/shard_map/ppermute | solution.py:222
  259.2 4.0 %smoothed_rows.3 = f32[2,4,32,128]{3,2,1,0:T(8,128)} custom-call(f32[2,4,32,128]{3,2,1,0:T(8,128)} %own_members.1.own_ref, f32[2,4,32,128]{3,2,1,0:T(8,128)} %copy-done.2, f32[2,4,32,128]{3,2,1,0:T(8,128)} %copy-done.4, bf16[384,128]{1,0:T(8,128)(2,1)} %constant.76.lon_ref, bf16[32,288]{1,0:T(8,128)(2,1)} %constant.82.lat_ref), custom_call_target="tpu_custom_call" | custom-call | tf_op jit(solution)/shard_map/smoothed_rows/pallas_call | solution.py:226
  263.2 3.0 %pad_maximum_fusion = f32[2,100,32,128]{3,2,1,0:T(8,128)} fusion(f32[2,4,32,128]{3,2,1,0:T(8,128)} %smoothed_rows.3, f32[32,3,2,32,128]{4,3,2,1,0:T(8,128)S(1)} %all-to-all-done.1), kind=kLoop, calls=%fused_computation | loop fusion | flops 819200 | bytes 6553600 | tf_op jit(solution)/shard_map/concatenate | solution.py:367
  (29 shorter events, 3.9 us)
Async XLA Ops:
  6.5 1.9 slice-start
  10.5 10.3 %copy-start.7 = (s32[1,4096]{1,0:T(1,128)S(1)}, s32[1,4096]{1,0:T(1,128)}, u32[]{:S(2)}) copy-start(s32[1,4096]{1,0:T(1,128)} %param.11) | copy-start | bytes 49156
  10.5 79.8 %all-to-all-start = ((f32[32,3,2,32,128]{4,3,2,1,0:T(8,128)}), f32[32,3,2,32,128]{4,3,2,1,0:T(8,128)S(1)}, u32[]{:S(2)}, u32[]{:S(2)}) async-start(f32[32,3,2,32,128]{4,3,2,1,0:T(8,128)} %bitcast.18), calls=%async_computation | async-start | bytes 6291456 | tf_op jit(solution)/shard_map/all_to_all | solution.py:357
  18.6 22.6 %collective-permute-start = (f32[3,32,128]{2,1,0:T(8,128)S(1)}, f32[3,32,128]{2,1,0:T(8,128)S(1)}, u32[]{:S(2)}, u32[]{:S(2)}) collective-permute-start(f32[3,32,128]{2,1,0:T(8,128)S(1)} %get-tuple-element.7), channel_id=1, source_target_pairs={{0,8},{8,16},{16,24},{24,0},{1,9},{9,17},{17,25},{25,1},{2,10},{10... | collective-permute-start | bytes 147464 | tf_op jit(solution)/shard_map/ppermute | solution.py:351
  20.3 20.9 %collective-permute-start.1 = (f32[3,32,128]{2,1,0:T(8,128)S(1)}, f32[3,32,128]{2,1,0:T(8,128)S(1)}, u32[]{:S(2)}, u32[]{:S(2)}) collective-permute-start(f32[3,32,128]{2,1,0:T(8,128)S(1)} %get-tuple-element.6), channel_id=1, source_target_pairs={{0,16},{8,24},{16,0},{24,8},{1,17},{9,25},{17,1},{25,9},{2,18},{10... | collective-permute-start | bytes 147464 | tf_op jit(solution)/shard_map/ppermute | solution.py:351
  20.3 20.9 %collective-permute-start.2 = (f32[3,32,128]{2,1,0:T(8,128)S(1)}, f32[3,32,128]{2,1,0:T(8,128)S(1)}, u32[]{:S(2)}, u32[]{:S(2)}) collective-permute-start(f32[3,32,128]{2,1,0:T(8,128)S(1)} %get-tuple-element.8), channel_id=1, source_target_pairs={{0,24},{8,0},{16,8},{24,16},{1,25},{9,1},{17,9},{25,17},{2,26},{10... | collective-permute-start | bytes 147464 | tf_op jit(solution)/shard_map/ppermute | solution.py:351
  21.9 126.7 %copy-start.6 = (f32[32,128]{1,0:T(8,128)}, f32[32,128]{1,0:T(8,128)S(1)}, u32[]{:S(2)}) copy-start(f32[32,128]{1,0:T(8,128)S(1)} %fusion.map_ref) | copy-start | bytes 49156
  90.3 1.7 copy-start
  148.6 114.6 %all-to-all-start.1 = ((f32[32,3,2,32,128]{4,3,2,1,0:T(8,128)}), f32[32,3,2,32,128]{4,3,2,1,0:T(8,128)S(1)}, u32[]{:S(2)}, u32[]{:S(2)}) async-start(f32[32,3,2,32,128]{4,3,2,1,0:T(8,128)} %whole_fields.1), calls=%async_computation.1 | async-start | bytes 6291456 | tf_op jit(solution)/shard_map/all_to_all | solution.py:361
  151.6 81.4 %all-gather.4.cloned.1.call-start = ((), (), s32[]{:S(2)}) async-start(), calls=%async_computation.2 | async-start | bytes 1179648 | tf_op jit(solution)/shard_map/all_gather | solution.py:303
  152.6 19.0 %copy-start.1 = (f32[2,4,32,128]{3,2,1,0:T(8,128)}, f32[2,4,32,128]{3,2,1,0:T(8,128)S(1)}, u32[]{:S(2)}) copy-start(f32[2,4,32,128]{3,2,1,0:T(8,128)S(1)} %slice.10.own_ref) | copy-start | bytes 393220
  152.6 16.8 %collective-permute-start.3 = (f32[2,4,32,128]{3,2,1,0:T(8,128)S(1)}, f32[2,4,32,128]{3,2,1,0:T(8,128)S(1)}, u32[]{:S(2)}, u32[]{:S(2)}) collective-permute-start(f32[2,4,32,128]{3,2,1,0:T(8,128)S(1)} %slice.10.own_ref), channel_id=1, source_target_pairs={{0,8},{8,16},{16,24},{1,9},{9,17},{17,25},{2,10},{10,18},{18,26},{... | collective-permute-start | bytes 393224 | tf_op jit(solution)/shard_map/ppermute | solution.py:221
  156.2 15.4 %collective-permute-start.4 = (f32[2,4,32,128]{3,2,1,0:T(8,128)S(1)}, f32[2,4,32,128]{3,2,1,0:T(8,128)S(1)}, u32[]{:S(2)}, u32[]{:S(2)}) collective-permute-start(f32[2,4,32,128]{3,2,1,0:T(8,128)S(1)} %slice.10.own_ref), channel_id=1, source_target_pairs={{8,0},{16,8},{24,16},{9,1},{17,9},{25,17},{10,2},{18,10},{26,18},{... | collective-permute-start | bytes 393224 | tf_op jit(solution)/shard_map/ppermute | solution.py:222
  169.4 2.1 copy-start.3
  171.6 0.6 copy-start.5
  245.1 9.2 %collective-permute-start.5 = (f32[2,4,32,128]{3,2,1,0:T(8,128)}, f32[2,4,32,128]{3,2,1,0:T(8,128)S(1)}, u32[]{:S(2)}, u32[]{:S(2)}) collective-permute-start(f32[2,4,32,128]{3,2,1,0:T(8,128)} %own_members.1.own_ref), channel_id=1, source_target_pairs={{0,8},{8,16},{16,24},{1,9},{9,17},{17,25},{2,10},{10,18},{18,26},{... | collective-permute-start | bytes 393224 | tf_op jit(solution)/shard_map/ppermute | solution.py:221
  252.1 6.5 %collective-permute-start.6 = (f32[2,4,32,128]{3,2,1,0:T(8,128)}, f32[2,4,32,128]{3,2,1,0:T(8,128)S(1)}, u32[]{:S(2)}, u32[]{:S(2)}) collective-permute-start(f32[2,4,32,128]{3,2,1,0:T(8,128)} %own_members.1.own_ref), channel_id=1, source_target_pairs={{8,0},{16,8},{24,16},{9,1},{17,9},{25,17},{10,2},{18,10},{26,18},{... | collective-permute-start | bytes 393224 | tf_op jit(solution)/shard_map/ppermute | solution.py:222
  254.3 4.3 %copy-start.2 = (f32[2,4,32,128]{3,2,1,0:T(8,128)}, f32[2,4,32,128]{3,2,1,0:T(8,128)S(1)}, u32[]{:S(2)}) copy-start(f32[2,4,32,128]{3,2,1,0:T(8,128)S(1)} %collective-permute-done.5.low_ref) | copy-start | bytes 393220
  258.6 0.6 copy-start.4
Sparse Core Ops, SparseCore 0:
  176.3 56.6 all-gather.3

commit v2 on v1

--- a/solution.py
+++ b/solution.py
@@ -11,7 +11,8 @@
 HALF = 32
 PATCH = 128
 EPS = 1e-06
-STEP = 4
+STEP = 32
+BLOCK = 8
 VMEM = 56 * 1024 * 1024
 F32 = jnp.float32
 BF16 = jnp.bfloat16
@@ -57,9 +58,8 @@
 
 
 def patch_sums(squares, hot):
-    head, tail = halves(squares)
     return lax.dot_general(
-        jnp.concatenate([head, tail], axis=0),
+        squares,
         hot,
         (((1,), (1,)), ((), ())),
         preferred_element_type=F32,
@@ -74,16 +74,50 @@
     return jnp.concatenate(halves(weights), axis=1)
 
 
+def member_gaps(blocks):
+    gaps = [x - pltpu.roll(x, s, 0) for x in blocks for s in range(1, BLOCK // 2 + 1)]
+    for b, x in enumerate(blocks):
+        for y in blocks[b + 1 :]:
+            gaps.append(x - y)
+            gaps += [x - pltpu.roll(y, s, 0) for s in range(1, BLOCK)]
+    return gaps
+
+
+def member_pulls(pulls, count):
+    pulls = iter(pulls)
+    sums = [0.0] * count
+    for b in range(count):
+        for s in range(1, BLOCK // 2 + 1):
+            pull = next(pulls)
+            sums[b] = sums[b] + pull
+            if 2 * s != BLOCK:
+                sums[b] = sums[b] - pltpu.roll(pull, BLOCK - s, 0)
+    for b in range(count):
+        for c in range(b + 1, count):
+            for s in range(BLOCK):
+                pull = next(pulls)
+                sums[b] = sums[b] + pull
+                sums[c] = sums[c] - (pltpu.roll(pull, BLOCK - s, 0) if s else pull)
+    return sums
+
+
 def field_kernel(
     regions, me_ref, field_ref, truth_ref, map_ref, lon_ref, lat_ref, out_ref, cells, hots
 ):
-    sources, _, held, rows, lon = field_ref.shape
+    sources, _, lon = field_ref.shape
+    rows = truth_ref.shape[2]
+    held = field_ref.shape[1] // rows
     devices = sources // regions
     members = devices * held
+    blocks = members // BLOCK
+    pairs = blocks * (BLOCK // 2) + blocks * (blocks - 1) // 2 * BLOCK
+    height = (pairs + blocks) * BLOCK
     steps = rows // STEP
     patches = hots.shape[1]
-    shifts = members // 2
     scale = float(np.sqrt(PATCH))
+
+    def shift_of(region):
+        return lax.rem(me_ref[0] - region + regions, regions)
 
     @pl.when(pl.program_id(0) == 0)
     def _():
@@ -91,7 +125,7 @@
 
         def build(block, carry):
             for j in range(STEP):
-                own = map_ref[pl.ds(block * STEP + j, 1), :]
+                own = map_ref[shift_of(block // steps), 0, pl.ds(block % steps * STEP + j, 1), :]
                 hots[block, :, j * lon : (j + 1) * lon] = (patch == own).astype(BF16)
             return carry
 
@@ -105,7 +139,11 @@
     for device in range(devices):
         pair = [
             jnp.concatenate(
-                [field_ref[region * devices + device, 0, k] for region in range(regions)], axis=0
+                [
+                    field_ref[region * devices + device, k * rows : (k + 1) * rows, :]
+                    for region in range(regions)
+                ],
+                axis=0,
             )
             for k in range(held)
         ]
@@ -116,28 +154,31 @@
             ]
 
     for region in range(regions):
-        own_truth = lax.rem(me_ref[0] - region + regions, regions)
-
-        def load(step, j):
-            row = step * STEP + j
+        shift = shift_of(region)
+
+        def load(row):
             start = pl.multiple_of((region * rows + row) * members, members)
-            a = cells[pl.ds(start, members), :]
-            return start, a, a - truth_ref[own_truth, 0, pl.ds(row, 1), :]
+            a = [cells[pl.ds(start + b * BLOCK, BLOCK), :] for b in range(blocks)]
+            truth = truth_ref[shift, 0, pl.ds(row, 1), :]
+            return start, member_gaps(a) + [x - truth for x in a]
 
         def first(step, total):
-            columns = []
+            heads, tails = [], []
             for j in range(STEP):
-                _, a, miss = load(step, j)
-                gaps = [a - pltpu.roll(a, s, 0) for s in range(1, shifts + 1)] + [miss]
-                columns.append(jnp.concatenate([gap * gap for gap in gaps], axis=0))
-            squares = jnp.concatenate(columns, axis=1)
+                head, tail = halves(
+                    jnp.concatenate([gap * gap for gap in load(step * STEP + j)[1]], axis=0)
+                )
+                heads.append(head)
+                tails.append(tail)
+            squares = jnp.concatenate(
+                [jnp.concatenate(heads, axis=1), jnp.concatenate(tails, axis=1)], axis=0
+            )
             return total + patch_sums(squares, hots[region * steps + step])
 
-        height = (shifts + 1) * members
         total = lax.fori_loop(0, steps, first, jnp.zeros((2 * height, patches), F32))
         weights = lax.rsqrt(total[:height] + total[height:] + EPS)
         factor = jnp.where(
-            lax.broadcasted_iota(jnp.int32, (height, patches), 0) < shifts * members,
+            lax.broadcasted_iota(jnp.int32, (height, patches), 0) < pairs * BLOCK,
             -scale / members,
             scale,
         )
@@ -146,15 +187,12 @@
         def second(step, carry):
             spread = on_cells(weights, hots[region * steps + step])
             for j in range(STEP):
-                start, a, miss = load(step, j)
+                start, gaps = load(step * STEP + j)
                 w = spread[:, j * lon : (j + 1) * lon]
-                h = w[shifts * members :] * miss
-                for s in range(1, shifts + 1):
-                    pull = w[(s - 1) * members : s * members] * (a - pltpu.roll(a, s, 0))
-                    h = h + pull
-                    if 2 * s != members:
-                        h = h - pltpu.roll(pull, members - s, 0)
-                cells[pl.ds(start, members), :] = h
+                terms = [w[i * BLOCK : (i + 1) * BLOCK] * gap for i, gap in enumerate(gaps)]
+                sums = member_pulls(terms[:pairs], blocks)
+                for b in range(blocks):
+                    cells[pl.ds(start + b * BLOCK, BLOCK), :] = sums[b] + terms[pairs + b]
             return carry
 
         lax.fori_loop(0, steps, second, 0)
@@ -165,29 +203,30 @@
         )
         for region in range(regions):
             for k in range(held):
-                out_ref[region * devices + device, 0, k] = result[
+                out_ref[region * devices + device, k * rows : (k + 1) * rows, :] = result[
                     region * rows : (region + 1) * rows, k * lon : (k + 1) * lon
                 ]
 
 
-def whole_fields(fields, truth, patch_map, regions):
-    sources, count, held, rows, lon = fields.shape
+def whole_fields(fields, count, held, extra, offset):
+    sources, _, lon = fields.shape
+    regions, variables, rows, _ = extra.shape
     members = sources // regions * held
     patches = rows * lon // PATCH
     every = regions * rows
     me = lax.axis_index("region").reshape(1)
-    block = pl.BlockSpec((sources, 1, held, rows, lon), lambda v, me: (0, v, 0, 0, 0))
+    block = pl.BlockSpec((sources, held * rows, lon), lambda v, me: (0, v, 0))
     pairs = every * lon * members * (members // 2 + 1)
     return pl.pallas_call(
         functools.partial(field_kernel, regions),
-        out_shape=jax.ShapeDtypeStruct(fields.shape, F32),
+        out_shape=jax.ShapeDtypeStruct((sources, count * held * rows, lon), F32),
         grid_spec=pltpu.PrefetchScalarGridSpec(
             num_scalar_prefetch=1,
             grid=(count,),
             in_specs=[
                 block,
-                pl.BlockSpec((regions, 1, rows, lon), lambda v, me: (0, v, 0, 0)),
-                pl.BlockSpec((every, lon), lambda v, me: (0, 0)),
+                pl.BlockSpec((regions, 1, rows, lon), lambda v, me: (0, v + offset, 0, 0)),
+                pl.BlockSpec((regions, 1, rows, lon), lambda v, me: (0, variables - 1, 0, 0)),
                 pl.BlockSpec((3 * lon, lon), lambda v, me: (0, 0)),
                 pl.BlockSpec((every, 3 * every), lambda v, me: (0, 0)),
             ],
@@ -199,10 +238,12 @@
         ),
         compiler_params=pltpu.CompilerParams(vmem_limit_bytes=VMEM),
         cost_estimate=pl.CostEstimate(
-            flops=count * pairs * patches * 8, bytes_accessed=8 * fields.size, transcendentals=0
+            flops=count * pairs * patches * 8,
+            bytes_accessed=8 * count * every * lon * members,
+            transcendentals=0,
         ),
         name="whole_fields",
-    )(me, fields, truth, patch_map, lon_weights(lon), lat_weights(every, 0))
+    )(me, fields, extra, extra, lon_weights(lon), lat_weights(every, 0))
 
 
 def smooth_kernel(own_ref, low_ref, high_ref, lon_ref, lat_ref, out_ref):
@@ -273,7 +314,8 @@
         columns = [
             jnp.concatenate([gap * gap for gap in gaps(step, j)[1]], axis=0) for j in range(STEP)
         ]
-        return total + patch_sums(jnp.concatenate(columns, axis=1), hots[step])
+        squares = jnp.concatenate(halves(jnp.concatenate(columns, axis=1)), axis=0)
+        return total + patch_sums(squares, hots[step])
 
     height = held * (members + 8)
     total = lax.fori_loop(0, steps, first, jnp.zeros((2 * height, patches), F32))
@@ -296,11 +338,10 @@
     lax.fori_loop(0, steps, second, 0)
 
 
-def own_members(smooth, truth, patch_map):
+def own_members(everyone, smooth, truth, patch_map):
     held, count, rows, lon = smooth.shape
-    devices = lax.axis_size("member")
+    devices = everyone.shape[0]
     patches = rows * lon // PATCH
-    everyone = lax.all_gather(smooth, "member")
     block = pl.BlockSpec((held, 1, rows, lon), lambda v: (0, v, 0, 0))
     return pl.pallas_call(
         share_kernel,
@@ -332,39 +373,139 @@
     )
 
 
-def on_device(predicted_states, observed_analysis, tile_location_sequence):
-    held, variables, rows, lon = predicted_states.shape
+def exchange(blocks):
+    return lax.all_to_all(blocks, ("region", "member"), 0, 0, tiled=True)
+
+
+def sent_rows(x, count):
+    held, variables, rows, lon = x.shape
+    total = variables // count
+    x = jnp.transpose(x.reshape(held, total, count, rows, lon), (1, 2, 0, 3, 4))
+    return x.reshape(total, count * held * rows, lon)
+
+
+def kept_rows(blocks, held, rows):
+    total, height, lon = blocks.shape
+    count = height // (held * rows)
+    x = blocks.reshape(total, count, held, rows, lon)
+    return jnp.transpose(x, (2, 0, 1, 3, 4)).reshape(held, total * count, rows, lon)
+
+
+def is_power(n):
+    return n & (n - 1) == 0
+
+
+def sent_pieces(x, regions, devices):
+    held, variables, rows, lon = x.shape
+    near = devices // variables
+    x = x.reshape(held, variables, regions, near, rows // (regions * near), lon)
+    x = jnp.transpose(x, (2, 1, 3, 0, 4, 5))
+    return x.reshape(regions * devices, -1, lon)
+
+
+def kept_pieces(blocks, held, variables, regions, devices):
+    near = devices // variables
+    lon = blocks.shape[-1]
+    x = blocks.reshape(regions, variables, near, held, -1, lon)
+    return jnp.transpose(x, (3, 1, 0, 2, 4, 5)).reshape(held, variables, -1, lon)
+
+
+def plane_gather(x, near, beside):
+    x = x[None]
+    for axis, size in (("member", near), ("region", lax.axis_size("region"))):
+        index, step = lax.axis_index(axis), 1
+        while step < size:
+            count = lax.axis_size(axis)
+            other = lax.ppermute(x, axis, [(i, i ^ step) for i in range(count)])
+            if beside is not None:
+                other, beside = lax.optimization_barrier((other, beside))
+                result, beside = beside, None
+            low = (index & step) == 0
+            x = jnp.concatenate([jnp.where(low, x, other), jnp.where(low, other, x)], axis=0)
+            step *= 2
+    return x, result
+
+
+def extras(observed, patch_map, starts, counts):
+    regions = lax.axis_size("region")
+    region, member = lax.axis_index("region"), lax.axis_index("member")
+    result = []
+    for shift in range(regions):
+        owner = lax.rem(region + shift, regions), member
+        pieces = [
+            lax.dynamic_slice_in_dim(observed, start(*owner), count, axis=0)
+            for start, count in zip(starts, counts)
+        ]
+        piece = jnp.concatenate(pieces + [patch_map[None]], axis=0)
+        if shift:
+            ring = [(i, (i + shift) % regions) for i in range(regions)]
+            piece = lax.ppermute(piece, "region", ring)
+        result.append(piece)
+    return jnp.stack(result)
+
+
+def spread_over_all(forecast, observed, patch_map):
+    held, variables, rows, lon = forecast.shape
     regions, devices = lax.axis_size("region"), lax.axis_size("member")
+    region, member = lax.axis_index("region"), lax.axis_index("member")
     total = regions * devices
     share = variables // total
-    whole = share * total
+    chunks = [count for count in (share // 2, share - share // 2) if count]
+    left = variables - share * total
+    sent, starts, counts, begin = [], [], [], 0
+    for count in chunks:
+        sent.append(sent_rows(forecast[:, begin : begin + count * total], count))
+        starts.append(lambda r, m, b=begin, c=count: b + (r * devices + m) * c)
+        counts.append(count)
+        begin += count * total
+    if left:
+        near = devices // left
+        sent[0] = jnp.concatenate(
+            [sent[0], sent_pieces(forecast[:, begin:], regions, devices)], axis=1
+        )
+        starts.append(lambda r, m, b=begin: b + m // near)
+        counts.append(1)
+    extra = extras(observed, patch_map, starts, counts)
+    if len(chunks) > 1:
+        sent[1:], extra = lax.optimization_barrier((sent[1:], extra))
+    fields = [exchange(part) for part in sent]
+    results = [
+        whole_fields(field, count, held, extra, sum(chunks[:i]))
+        for i, (field, count) in enumerate(zip(fields, chunks))
+    ]
+    body = chunks[0] * held * rows
+    if left:
+        piece = rows // (regions * near)
+        field, results[0] = plane_gather(fields[0][:, body:], near, results[0])
+        field = field.reshape(-1, total, held, piece, lon)
+        field = jnp.transpose(field, (1, 2, 0, 3, 4)).reshape(total, held * rows, lon)
+        result = whole_fields(field, 1, held, extra, share).reshape(total, held, rows, lon)
+        place = region * near + lax.rem(member, near)
+        result = lax.dynamic_slice_in_dim(result, place * piece, piece, axis=2)
+        results[0] = jnp.concatenate([results[0], result.reshape(total, -1, lon)], axis=1)
+    backs = [exchange(result) for result in results]
+    parts = [kept_rows(back[:, : count * held * rows], held, rows) for back, count in zip(backs, chunks)]
+    if left:
+        parts.append(kept_pieces(backs[0][:, body:], held, left, regions, devices))
+    return jnp.concatenate(parts, axis=1)
+
+
+def on_device(predicted_states, observed_analysis, tile_location_sequence):
+    _, variables, rows, lon = predicted_states.shape
+    regions, devices = lax.axis_size("region"), lax.axis_size("member")
     patch_map = patch_of_cell(tile_location_sequence[0], rows, lon)
-    parts = []
-    if share:
-        region, member = lax.axis_index("region"), lax.axis_index("member")
-        maps = lax.all_gather(patch_map, "region").reshape(regions * rows, lon)
-        truth = []
-        for shift in range(regions):
-            owner = lax.rem(region + shift, regions) * devices + member
-            piece = lax.dynamic_slice_in_dim(observed_analysis, owner * share, share, axis=0)
-            if shift:
-                piece = lax.ppermute(
-                    piece, "region", [(i, (i + shift) % regions) for i in range(regions)]
-                )
-            truth.append(piece)
-        truth = jnp.stack(truth)
-        sent = predicted_states[:, :whole].reshape(held, total, share, rows, lon)
-        fields = lax.all_to_all(
-            jnp.transpose(sent, (1, 2, 0, 3, 4)), ("region", "member"), 0, 0, tiled=True
-        )
-        result = whole_fields(fields, truth, maps, regions)
-        result = lax.all_to_all(result, ("region", "member"), 0, 0, tiled=True)
-        parts.append(jnp.transpose(result, (2, 0, 1, 3, 4)).reshape(held, whole, rows, lon))
-    if whole < variables:
-        smooth = smoothed_rows(predicted_states[:, whole:])
-        h = own_members(smooth, observed_analysis[whole:], patch_map)
-        parts.append(smoothed_rows(h))
-    return jnp.concatenate(parts, axis=1)
+    left = variables % (regions * devices)
+    planes = left == 0 or (
+        devices % left == 0
+        and rows % (regions * devices // left) == 0
+        and is_power(regions)
+        and is_power(devices // left)
+    )
+    if variables >= regions * devices and planes:
+        return spread_over_all(predicted_states, observed_analysis, patch_map)
+    smooth = smoothed_rows(predicted_states)
+    everyone = lax.all_gather(smooth, "member")
+    return smoothed_rows(own_members(everyone, smooth, observed_analysis, patch_map))
 
 
 def solution(mesh):

time: 274 us -> 195 us (0.71)
  Pallas kernels: 76.6 us -> 44.2 us
  blocking collectives: 19.3 us -> 0 us
  waiting for transfers between devices: 122 us -> 108 us
  between operations: 13.5 us -> 0.29 us
  starting transfers between devices: 26.7 us -> 22.6 us
  other arithmetic: 3.78 us -> 7.13 us
    all_gather x1 -> x0, waiting for transfers between devices: 55.3 us -> none  [own_members(): everyone = lax.all_gather(smooth, 'member')]
    all_to_all x2 -> x4, waiting for transfers between devices: 48.4 us -> 72.3 us  [exchange(): return lax.all_to_all(blocks, ('region', 'member'), 0, 0, tiled=True)]
    pallas_call x3 -> x0, Pallas kernels: 20 us -> none  [the longest x1 12.1 us: own_members(): pl.pallas_call(share_kernel, out_shape=jax.ShapeDtypeStruct(smooth.shape,...]
    all_gather x1 -> x0, blocking collectives: 19.3 us -> none  [on_device(): maps = lax.all_gather(patch_map, 'region').reshape(regions * rows, lon)]
    ppermute x7 -> x6, waiting for transfers between devices: 18 us -> 35.2 us  [the longest x3 28.5 us: plane_gather(): other = lax.ppermute(x, axis, [(i, i ^ step) for i in range(count)])]
    pallas_call x1 -> x3, Pallas kernels: 56.6 us -> 44.2 us  [whole_fields(): pl.pallas_call(functools.partial(field_kernel, regions), out_shape=jax.Sh...]
    ppermute x7 -> x6, starting transfers between devices: 16.5 us -> 5.93 us  [the longest x3 3.7 us: plane_gather(): other = lax.ppermute(x, axis, [(i, i ^ step) for i in range(count)])]
    all_to_all x2 -> x4, starting transfers between devices: 10.1 us -> 16.7 us  [exchange(): return lax.all_to_all(blocks, ('region', 'member'), 0, 0, tiled=True)]
  transfers between devices with their start and end apart: 10 -> 10, of which waited for: 6 -> 9; matrix products, arithmetic and copies ran while one was open for 2% -> 6% of each run, Pallas kernels for 7% -> 23%
where the time goes in v2:
time: 195 us; the launch traced here: 193 us
  waiting for transfers between devices  108 us (55%)
  Pallas kernels  44.2 us (23%)
  starting transfers between devices  22.6 us (12%)
  local copies, waits for them, and re-layouts  10.4 us (5%)
  other arithmetic  7.13 us (4%)
    all_to_all x4, waiting for transfers between devices, exchange(): return lax.all_to_all(blocks, ('region', 'member'), 0, 0, tiled=True)  72.3 us
    pallas_call x3, Pallas kernels, whole_fields(): pl.pallas_call(functools.partial(field_kernel, regions), out_shape=jax.Sh...  44.2 us
    ppermute x3, waiting for transfers between devices, plane_gather(): other = lax.ppermute(x, axis, [(i, i ^ step) for i in range(count)])  28.5 us
    all_to_all x4, starting transfers between devices, exchange(): return lax.all_to_all(blocks, ('region', 'member'), 0, 0, tiled=True)  16.7 us
    ppermute x3, waiting for transfers between devices, extras(): piece = lax.ppermute(piece, 'region', ring)  6.73 us
  transfers between devices with their start and end apart: 10, of which 9 were waited for; matrix products, arithmetic and copies ran while one was open for 6% of the time, Pallas kernels for 23%

profile of v2, /device:TPU:1, one launch (start us, length us, event | category | flops | bytes accessed | tf_op | source)
XLA Modules:
  0.0 193.1 jit_solution(336440904046715877)
XLA Ops:
  0.0 1.3 slice_bitcast_fusion
  1.5 1.1 pad_maximum_fusion.1
  2.6 7.1 %all-to-all-start = ((f32[32,72,128]{2,1,0:T(8,128)}), f32[32,72,128]{2,1,0:T(8,128)S(1)}, u32[]{:S(2)}, u32[]{:S(2)}) async-start(f32[32,72,128]{2,1,0:T(8,128)} %pad_maximum_fusion.1), calls=%async_computation | async-start | bytes 2359296 | tf_op jit(solution)/shard_map/all_to_all | solution.py:377
  12.6 1.7 collective-permute-start.1
  15.9 1.5 copy.12
  18.0 5.5 %collective-permute-done.2 = f32[5,32,128]{2,1,0:T(8,128)S(1)} collective-permute-done((f32[5,32,128]{2,1,0:T(8,128)S(1)}, f32[5,32,128]{2,1,0:T(8,128)S(1)}, u32[]{:S(2)}, u32[]{:S(2)}) %collective-permute-start.2) | collective-permute-done | bytes 81952 | tf_op jit(solution)/shard_map/ppermute | solution.py:442
  24.9 14.7 %all-to-all-done.field_ref = f32[32,72,128]{2,1,0:T(8,128)S(1)} async-done(((f32[32,72,128]{2,1,0:T(8,128)}), f32[32,72,128]{2,1,0:T(8,128)S(1)}, u32[]{:S(2)}, u32[]{:S(2)}) %all-to-all-start) | async-done | bytes 1179680 | tf_op jit(solution)/shard_map/all_to_all | solution.py:377
  39.5 3.2 %all-to-all-start.2 = ((f32[32,128,128]{2,1,0:T(8,128)}), f32[32,128,128]{2,1,0:T(8,128)S(1)}, u32[]{:S(2)}, u32[]{:S(2)}) async-start(f32[32,128,128]{2,1,0:T(8,128)} %bitcast.10), calls=%async_computation.2 | async-start | bytes 4194304 | tf_op jit(solution)/shard_map/all_to_all | solution.py:377
  42.7 1.5 collective-permute-start
  44.2 11.6 %whole_fields.3 = f32[32,64,128]{2,1,0:T(8,128)} custom-call(s32[1]{0:T(128)} %bitcast.7.me_ref, f32[32,72,128]{2,1,0:T(8,128)} %copy-done.1, f32[4,5,32,128]{3,2,1,0:T(8,128)} %pad_maximum_fusion.5.truth_ref.map_ref, f32[4,5,32,128]{3,2,1,0:T(8,128)} %pad_maximum_fusion.5.truth_ref.map_ref, bf16[384,128]{1,0:T(8,128)(2,1)} %constant.101.lon_ref, ...), custom_call_target="tpu_custom_call" | custom-call | flops 603979776 | bytes 2097152 | tf_op jit(solution)/shard_map/whole_fields/pallas_call | solution.py:220
  55.8 12.6 %collective-permute-done = f32[1,32,8,128]{3,2,1,0:T(8,128)S(1)} collective-permute-done((f32[1,32,8,128]{3,2,1,0:T(8,128)S(1)}, f32[1,32,8,128]{3,2,1,0:T(8,128)S(1)}, u32[]{:S(2)}, u32[]{:S(2)}) %collective-permute-start) | collective-permute-done | bytes 131104 | tf_op jit(solution)/shard_map/ppermute | solution.py:419
  69.4 1.1 collective-permute-start.4
  70.4 1.2 collective-permute-done.4
  72.5 1.2 collective-permute-start.5
  73.6 14.7 %collective-permute-done.5 = f32[4,32,8,128]{3,2,1,0:T(8,128)S(1)} collective-permute-done((f32[4,32,8,128]{3,2,1,0:T(8,128)}, f32[4,32,8,128]{3,2,1,0:T(8,128)S(1)}, u32[]{:S(2)}, u32[]{:S(2)}) %collective-permute-start.5) | collective-permute-done | bytes 524320 | tf_op jit(solution)/shard_map/ppermute | solution.py:419
  88.5 1.3 copy.13
  89.8 11.9 %whole_fields.4 = f32[32,64,128]{2,1,0:T(8,128)} custom-call(s32[1]{0:T(128)} %bitcast.7.me_ref, f32[32,64,128]{2,1,0:T(8,128)} %bitcast.54, f32[4,5,32,128]{3,2,1,0:T(8,128)} %pad_maximum_fusion.5.truth_ref.map_ref, f32[4,5,32,128]{3,2,1,0:T(8,128)} %pad_maximum_fusion.5.truth_ref.map_ref, bf16[384,128]{1,0:T(8,128)(2,1)} %constant.101.lon_ref, ...), custom_call_target="tpu_custom_call" | custom-call | flops 603979776 | bytes 2097152 | tf_op jit(solution)/shard_map/whole_fields/pallas_call | solution.py:220
  102.6 1.1 pad_maximum_fusion.2
  103.8 3.3 %all-to-all-start.1 = ((f32[32,72,128]{2,1,0:T(8,128)}), f32[32,72,128]{2,1,0:T(8,128)S(1)}, u32[]{:S(2)}, u32[]{:S(2)}) async-start(f32[32,72,128]{2,1,0:T(8,128)} %pad_maximum_fusion.2), calls=%async_computation.1 | async-start | bytes 2359296 | tf_op jit(solution)/shard_map/all_to_all | solution.py:377
  107.0 20.7 %whole_fields.5 = f32[32,128,128]{2,1,0:T(8,128)} custom-call(s32[1]{0:T(128)} %bitcast.7.me_ref, f32[32,128,128]{2,1,0:T(8,128)} %copy-done, f32[4,5,32,128]{3,2,1,0:T(8,128)} %pad_maximum_fusion.5.truth_ref.map_ref, f32[4,5,32,128]{3,2,1,0:T(8,128)} %pad_maximum_fusion.5.truth_ref.map_ref, bf16[384,128]{1,0:T(8,128)(2,1)} %constant.101.lon_ref, ...), custom_call_target="tpu_custom_call" | custom-call | flops 1207959552 | bytes 4194304 | tf_op jit(solution)/shard_map/whole_fields/pallas_call | solution.py:220
  127.8 9.2 %all-to-all-done.1 = f32[32,72,128]{2,1,0:T(8,128)S(1)} async-done(((f32[32,72,128]{2,1,0:T(8,128)}), f32[32,72,128]{2,1,0:T(8,128)S(1)}, u32[]{:S(2)}, u32[]{:S(2)}) %all-to-all-start.1) | async-done | bytes 1179680 | tf_op jit(solution)/shard_map/all_to_all | solution.py:377
  137.0 3.2 %all-to-all-start.3 = ((f32[32,128,128]{2,1,0:T(8,128)}), f32[32,128,128]{2,1,0:T(8,128)S(1)}, u32[]{:S(2)}, u32[]{:S(2)}) async-start(f32[32,128,128]{2,1,0:T(8,128)} %whole_fields.5), calls=%async_computation.3 | async-start | bytes 4194304 | tf_op jit(solution)/shard_map/all_to_all | solution.py:377
  141.4 48.4 %all-to-all-done.3 = f32[32,128,128]{2,1,0:T(8,128)S(1)} async-done(((f32[32,128,128]{2,1,0:T(8,128)}), f32[32,128,128]{2,1,0:T(8,128)S(1)}, u32[]{:S(2)}, u32[]{:S(2)}) %all-to-all-start.3) | async-done | bytes 2097184 | tf_op jit(solution)/shard_map/all_to_all | solution.py:377
  191.0 2.0 %pad_maximum_fusion = f32[2,100,32,128]{3,2,1,0:T(8,128)} fusion(f32[2,4,32,128]{3,2,1,0:T(8,128)S(1)} %bitcast.59, f32[2,64,32,128]{3,2,1,0:T(8,128)S(1)} %bitcast.49, f32[2,32,32,128]{3,2,1,0:T(8,128)S(1)} %bitcast.53), kind=kLoop, calls=%fused_computation | loop fusion | flops 1638400 | bytes 6553600 | tf_op jit(solution)/shard_map/concatenate | solution.py:490
  (41 shorter events, 11.8 us)
Async XLA Ops:
  0.0 1.3 slice-start
  1.5 9.9 %copy-start.4 = (s32[1,4096]{1,0:T(1,128)S(1)}, s32[1,4096]{1,0:T(1,128)}, u32[]{:S(2)}) copy-start(s32[1,4096]{1,0:T(1,128)} %param.11) | copy-start | bytes 49156
  2.6 36.9 %all-to-all-start = ((f32[32,72,128]{2,1,0:T(8,128)}), f32[32,72,128]{2,1,0:T(8,128)S(1)}, u32[]{:S(2)}, u32[]{:S(2)}) async-start(f32[32,72,128]{2,1,0:T(8,128)} %pad_maximum_fusion.1), calls=%async_computation | async-start | bytes 2359296 | tf_op jit(solution)/shard_map/all_to_all | solution.py:377
  12.6 5.4 %collective-permute-start.1 = (f32[5,32,128]{2,1,0:T(8,128)S(1)}, f32[5,32,128]{2,1,0:T(8,128)S(1)}, u32[]{:S(2)}, u32[]{:S(2)}) collective-permute-start(f32[5,32,128]{2,1,0:T(8,128)S(1)} %get-tuple-element.29), channel_id=1, source_target_pairs={{0,8},{8,16},{16,24},{24,0},{1,9},{9,17},{17,25},{25,1},{2,10},{10... | collective-permute-start | bytes 245768 | tf_op jit(solution)/shard_map/ppermute | solution.py:442
  14.3 9.3 %collective-permute-start.2 = (f32[5,32,128]{2,1,0:T(8,128)S(1)}, f32[5,32,128]{2,1,0:T(8,128)S(1)}, u32[]{:S(2)}, u32[]{:S(2)}) collective-permute-start(f32[5,32,128]{2,1,0:T(8,128)S(1)} %get-tuple-element.30), channel_id=1, source_target_pairs={{0,16},{8,24},{16,0},{24,8},{1,17},{9,25},{17,1},{25,9},{2,18},{10... | collective-permute-start | bytes 245768 | tf_op jit(solution)/shard_map/ppermute | solution.py:442
  14.3 1.6 slice-start.1
  14.3 9.9 %collective-permute-start.3 = (f32[5,32,128]{2,1,0:T(8,128)S(1)}, f32[5,32,128]{2,1,0:T(8,128)S(1)}, u32[]{:S(2)}, u32[]{:S(2)}) collective-permute-start(f32[5,32,128]{2,1,0:T(8,128)S(1)} %get-tuple-element.31), channel_id=1, source_target_pairs={{0,24},{8,0},{16,8},{24,16},{1,25},{9,1},{17,9},{25,17},{2,26},{10... | collective-permute-start | bytes 245768 | tf_op jit(solution)/shard_map/ppermute | solution.py:442
  39.5 3.2 %copy-start.1 = (f32[32,72,128]{2,1,0:T(8,128)}, f32[32,72,128]{2,1,0:T(8,128)S(1)}, u32[]{:S(2)}) copy-start(f32[32,72,128]{2,1,0:T(8,128)S(1)} %all-to-all-done.field_ref) | copy-start | bytes 3538948
  39.5 64.2 %all-to-all-start.2 = ((f32[32,128,128]{2,1,0:T(8,128)}), f32[32,128,128]{2,1,0:T(8,128)S(1)}, u32[]{:S(2)}, u32[]{:S(2)}) async-start(f32[32,128,128]{2,1,0:T(8,128)} %bitcast.10), calls=%async_computation.2 | async-start | bytes 4194304 | tf_op jit(solution)/shard_map/all_to_all | solution.py:377
  42.7 25.7 %collective-permute-start = (f32[1,32,8,128]{3,2,1,0:T(8,128)S(1)}, f32[1,32,8,128]{3,2,1,0:T(8,128)S(1)}, u32[]{:S(2)}, u32[]{:S(2)}) collective-permute-start(f32[1,32,8,128]{3,2,1,0:T(8,128)S(1)} %slice_bitcast_fusion.1), channel_id=1, source_target_pairs={{0,1},{1,0},{2,3},{3,2},{4,5},{5,4},{6,7},{7,6},{8,9},{9,8},{10,11... | collective-permute-start | bytes 393224 | tf_op jit(solution)/shard_map/ppermute | solution.py:419
  69.4 2.2 %collective-permute-start.4 = (f32[2,32,8,128]{3,2,1,0:T(8,128)S(1)}, f32[2,32,8,128]{3,2,1,0:T(8,128)S(1)}, u32[]{:S(2)}, u32[]{:S(2)}) collective-permute-start(f32[2,32,8,128]{3,2,1,0:T(8,128)S(1)} %pad_maximum_fusion.6), channel_id=1, source_target_pairs={{0,8},{8,0},{16,24},{24,16},{1,9},{9,1},{17,25},{25,17},{2,10},{10... | collective-permute-start | bytes 786440 | tf_op jit(solution)/shard_map/ppermute | solution.py:419
  72.5 15.8 %collective-permute-start.5 = (f32[4,32,8,128]{3,2,1,0:T(8,128)}, f32[4,32,8,128]{3,2,1,0:T(8,128)S(1)}, u32[]{:S(2)}, u32[]{:S(2)}) collective-permute-start(f32[4,32,8,128]{3,2,1,0:T(8,128)} %pad_maximum_fusion.4), channel_id=1, source_target_pairs={{0,16},{8,24},{16,0},{24,8},{1,17},{9,25},{17,1},{25,9},{2,18},{10... | collective-permute-start | bytes 1572872 | tf_op jit(solution)/shard_map/ppermute | solution.py:419
  89.8 12.8 %copy-start.2 = (f32[32,64,128]{2,1,0:T(8,128)S(1)}, f32[32,64,128]{2,1,0:T(8,128)}, u32[]{:S(2)}) copy-start(f32[32,64,128]{2,1,0:T(8,128)} %whole_fields.3) | copy-start | bytes 3145732
  103.8 3.3 %copy-start = (f32[32,128,128]{2,1,0:T(8,128)}, f32[32,128,128]{2,1,0:T(8,128)S(1)}, u32[]{:S(2)}) copy-start(f32[32,128,128]{2,1,0:T(8,128)S(1)} %all-to-all-done.2.field_ref) | copy-start | bytes 6291460
  103.8 33.2 %all-to-all-start.1 = ((f32[32,72,128]{2,1,0:T(8,128)}), f32[32,72,128]{2,1,0:T(8,128)S(1)}, u32[]{:S(2)}, u32[]{:S(2)}) async-start(f32[32,72,128]{2,1,0:T(8,128)} %pad_maximum_fusion.2), calls=%async_computation.1 | async-start | bytes 2359296 | tf_op jit(solution)/shard_map/all_to_all | solution.py:377
  137.0 52.8 %all-to-all-start.3 = ((f32[32,128,128]{2,1,0:T(8,128)}), f32[32,128,128]{2,1,0:T(8,128)S(1)}, u32[]{:S(2)}, u32[]{:S(2)}) async-start(f32[32,128,128]{2,1,0:T(8,128)} %whole_fields.5), calls=%async_computation.3 | async-start | bytes 4194304 | tf_op jit(solution)/shard_map/all_to_all | solution.py:377
  189.8 1.2 copy-start.3

commit v3 on v2

--- a/solution.py
+++ b/solution.py
@@ -410,20 +410,27 @@
     return jnp.transpose(x, (3, 1, 0, 2, 4, 5)).reshape(held, variables, -1, lon)
 
 
+def after(x, first):
+    return lax.optimization_barrier((x, first))[0]
+
+
 def plane_gather(x, near, beside):
     x = x[None]
+    first = True
     for axis, size in (("member", near), ("region", lax.axis_size("region"))):
         index, step = lax.axis_index(axis), 1
         while step < size:
             count = lax.axis_size(axis)
             other = lax.ppermute(x, axis, [(i, i ^ step) for i in range(count)])
-            if beside is not None:
+            if first:
                 other, beside = lax.optimization_barrier((other, beside))
-                result, beside = beside, None
+                first = False
             low = (index & step) == 0
             x = jnp.concatenate([jnp.where(low, x, other), jnp.where(low, other, x)], axis=0)
             step *= 2
-    return x, result
+            if axis == "region" and step * 2 == size:
+                x, beside = lax.optimization_barrier((x, beside))
+    return x, beside
 
 
 def extras(observed, patch_map, starts, counts):
@@ -450,7 +457,7 @@
     region, member = lax.axis_index("region"), lax.axis_index("member")
     total = regions * devices
     share = variables // total
-    chunks = [count for count in (share // 2, share - share // 2) if count]
+    chunks = [count for count in (share - share // 2, share // 2) if count]
     left = variables - share * total
     sent, starts, counts, begin = [], [], [], 0
     for count in chunks:
@@ -482,11 +489,14 @@
         result = whole_fields(field, 1, held, extra, share).reshape(total, held, rows, lon)
         place = region * near + lax.rem(member, near)
         result = lax.dynamic_slice_in_dim(result, place * piece, piece, axis=2)
-        results[0] = jnp.concatenate([results[0], result.reshape(total, -1, lon)], axis=1)
-    backs = [exchange(result) for result in results]
+        results[-1] = jnp.concatenate([results[-1], result.reshape(total, -1, lon)], axis=1)
+    backs = []
+    for result in results:
+        backs.append(exchange(after(result, backs[-1:])))
     parts = [kept_rows(back[:, : count * held * rows], held, rows) for back, count in zip(backs, chunks)]
     if left:
-        parts.append(kept_pieces(backs[0][:, body:], held, left, regions, devices))
+        last = chunks[-1] * held * rows
+        parts.append(kept_pieces(backs[-1][:, last:], held, left, regions, devices))
     return jnp.concatenate(parts, axis=1)
 
 

time: 195 us -> 187 us (0.959)
  waiting for transfers between devices: 108 us -> 95.6 us
  starting transfers between devices: 22.6 us -> 26 us
    ppermute x3, waiting for transfers between devices: 28.5 us -> 19.2 us  [plane_gather(): other = lax.ppermute(x, axis, [(i, i ^ step) for i in range(count)])]
    all_to_all x4, waiting for transfers between devices: 72.3 us -> 63.2 us  [exchange(): return lax.all_to_all(blocks, ('region', 'member'), 0, 0, tiled=True)]
    ppermute x3, waiting for transfers between devices: 6.73 us -> 13.2 us  [extras(): piece = lax.ppermute(piece, 'region', ring)]
    all_to_all x4, starting transfers between devices: 16.7 us -> 20.2 us  [exchange(): return lax.all_to_all(blocks, ('region', 'member'), 0, 0, tiled=True)]
  transfers between devices with their start and end apart: 10 -> 10, of which waited for: 9 -> 9; matrix products, arithmetic and copies ran while one was open for 6% -> 7% of each run, Pallas kernels for 23% -> 24%
where the time goes in v3:
time: 187 us; the launch traced here: 186 us
  waiting for transfers between devices  95.6 us (51%)
  Pallas kernels  44.2 us (24%)
  starting transfers between devices  26 us (14%)
  local copies, waits for them, and re-layouts  11.2 us (6%)
  other arithmetic  7.52 us (4%)
    all_to_all x4, waiting for transfers between devices, exchange(): return lax.all_to_all(blocks, ('region', 'member'), 0, 0, tiled=True)  63.2 us
    pallas_call x3, Pallas kernels, whole_fields(): pl.pallas_call(functools.partial(field_kernel, regions), out_shape=jax.Sh...  44.2 us
    all_to_all x4, starting transfers between devices, exchange(): return lax.all_to_all(blocks, ('region', 'member'), 0, 0, tiled=True)  20.2 us
    ppermute x3, waiting for transfers between devices, plane_gather(): other = lax.ppermute(x, axis, [(i, i ^ step) for i in range(count)])  19.2 us
    ppermute x3, waiting for transfers between devices, extras(): piece = lax.ppermute(piece, 'region', ring)  13.2 us
  transfers between devices with their start and end apart: 10, of which 9 were waited for; matrix products, arithmetic and copies ran while one was open for 7% of the time, Pallas kernels for 24%

profile of v3, /device:TPU:1, one launch (start us, length us, event | category | flops | bytes accessed | tf_op | source)
XLA Modules:
  0.0 185.8 jit_solution(13976897649466308335)
XLA Ops:
  1.9 1.5 pad_maximum_fusion.1
  3.4 7.1 %all-to-all-start = ((f32[32,136,128]{2,1,0:T(8,128)}), f32[32,136,128]{2,1,0:T(8,128)S(1)}, u32[]{:S(2)}, u32[]{:S(2)}) async-start(f32[32,136,128]{2,1,0:T(8,128)} %pad_maximum_fusion.1), calls=%async_computation | async-start | bytes 4456448 | tf_op jit(solution)/shard_map/all_to_all | solution.py:377
  13.4 1.7 collective-permute-start.1
  15.6 1.3 slice_bitcast_fusion
  18.0 5.8 %collective-permute-done.1 = f32[5,32,128]{2,1,0:T(8,128)S(1)} collective-permute-done((f32[5,32,128]{2,1,0:T(8,128)S(1)}, f32[5,32,128]{2,1,0:T(8,128)S(1)}, u32[]{:S(2)}, u32[]{:S(2)}) %collective-permute-start.1) | collective-permute-done | bytes 81952 | tf_op jit(solution)/shard_map/ppermute | solution.py:449
  23.8 6.5 %collective-permute-done.2 = f32[5,32,128]{2,1,0:T(8,128)S(1)} collective-permute-done((f32[5,32,128]{2,1,0:T(8,128)S(1)}, f32[5,32,128]{2,1,0:T(8,128)S(1)}, u32[]{:S(2)}, u32[]{:S(2)}) %collective-permute-start.2) | collective-permute-done | bytes 81952 | tf_op jit(solution)/shard_map/ppermute | solution.py:449
  31.9 31.0 %all-to-all-done.field_ref = f32[32,136,128]{2,1,0:T(8,128)S(1)} async-done(((f32[32,136,128]{2,1,0:T(8,128)}), f32[32,136,128]{2,1,0:T(8,128)S(1)}, u32[]{:S(2)}, u32[]{:S(2)}) %all-to-all-start) | async-done | bytes 2228256 | tf_op jit(solution)/shard_map/all_to_all | solution.py:377
  62.9 3.1 %all-to-all-start.2 = ((f32[32,64,128]{2,1,0:T(8,128)}), f32[32,64,128]{2,1,0:T(8,128)S(1)}, u32[]{:S(2)}, u32[]{:S(2)}) async-start(f32[32,64,128]{2,1,0:T(8,128)} %bitcast.56), calls=%async_computation.2 | async-start | bytes 2097152 | tf_op jit(solution)/shard_map/all_to_all | solution.py:377
  66.1 1.5 collective-permute-start
  67.6 20.8 %whole_fields.3 = f32[32,128,128]{2,1,0:T(8,128)} custom-call(s32[1]{0:T(128)} %bitcast.7.me_ref, f32[32,136,128]{2,1,0:T(8,128)} %copy-done, f32[4,5,32,128]{3,2,1,0:T(8,128)} %pad_maximum_fusion.5.truth_ref.map_ref, f32[4,5,32,128]{3,2,1,0:T(8,128)} %pad_maximum_fusion.5.truth_ref.map_ref, bf16[384,128]{1,0:T(8,128)(2,1)} %constant.103.lon_ref, ...), custom_call_target="tpu_custom_call" | custom-call | flops 1207959552 | bytes 4194304 | tf_op jit(solution)/shard_map/whole_fields/pallas_call | solution.py:220
  90.0 1.2 collective-permute-done.4
  92.0 1.2 all-to-all-done.2.field_ref
  94.2 3.7 %all-to-all-start.1 = ((f32[32,128,128]{2,1,0:T(8,128)}), f32[32,128,128]{2,1,0:T(8,128)S(1)}, u32[]{:S(2)}, u32[]{:S(2)}) async-start(f32[32,128,128]{2,1,0:T(8,128)} %whole_fields.3), calls=%async_computation.1 | async-start | bytes 4194304 | tf_op jit(solution)/shard_map/all_to_all | solution.py:377
  97.9 1.5 collective-permute-start.5
  99.3 11.6 %whole_fields.4 = f32[32,64,128]{2,1,0:T(8,128)} custom-call(s32[1]{0:T(128)} %bitcast.7.me_ref, f32[32,64,128]{2,1,0:T(8,128)} %copy-done.2, f32[4,5,32,128]{3,2,1,0:T(8,128)} %pad_maximum_fusion.5.truth_ref.map_ref, f32[4,5,32,128]{3,2,1,0:T(8,128)} %pad_maximum_fusion.5.truth_ref.map_ref, bf16[384,128]{1,0:T(8,128)(2,1)} %constant.103.lon_ref, ...), custom_call_target="tpu_custom_call" | custom-call | flops 603979776 | bytes 2097152 | tf_op jit(solution)/shard_map/whole_fields/pallas_call | solution.py:220
  110.9 18.0 %collective-permute-done.5 = f32[4,32,8,128]{3,2,1,0:T(8,128)S(1)} collective-permute-done((f32[4,32,8,128]{3,2,1,0:T(8,128)}, f32[4,32,8,128]{3,2,1,0:T(8,128)S(1)}, u32[]{:S(2)}, u32[]{:S(2)}) %collective-permute-start.5) | collective-permute-done | bytes 524320 | tf_op jit(solution)/shard_map/ppermute | solution.py:424
  129.1 1.3 copy.14
  130.3 11.9 %whole_fields.5 = f32[32,64,128]{2,1,0:T(8,128)} custom-call(s32[1]{0:T(128)} %bitcast.7.me_ref, f32[32,64,128]{2,1,0:T(8,128)} %bitcast.55, f32[4,5,32,128]{3,2,1,0:T(8,128)} %pad_maximum_fusion.5.truth_ref.map_ref, f32[4,5,32,128]{3,2,1,0:T(8,128)} %pad_maximum_fusion.5.truth_ref.map_ref, bf16[384,128]{1,0:T(8,128)(2,1)} %constant.103.lon_ref, ...), custom_call_target="tpu_custom_call" | custom-call | flops 603979776 | bytes 2097152 | tf_op jit(solution)/shard_map/whole_fields/pallas_call | solution.py:220
  143.2 1.1 pad_maximum_fusion.2
  144.3 3.1 %all-to-all-done.1 = f32[32,128,128]{2,1,0:T(8,128)S(1)} async-done(((f32[32,128,128]{2,1,0:T(8,128)}), f32[32,128,128]{2,1,0:T(8,128)S(1)}, u32[]{:S(2)}, u32[]{:S(2)}) %all-to-all-start.1) | async-done | bytes 2097184 | tf_op jit(solution)/shard_map/all_to_all | solution.py:377
  147.4 6.3 %all-to-all-start.3 = ((f32[32,72,128]{2,1,0:T(8,128)}), f32[32,72,128]{2,1,0:T(8,128)S(1)}, u32[]{:S(2)}, u32[]{:S(2)}) async-start(f32[32,72,128]{2,1,0:T(8,128)} %pad_maximum_fusion.2), calls=%async_computation.3 | async-start | bytes 2359296 | tf_op jit(solution)/shard_map/all_to_all | solution.py:377
  153.7 1.8 copy.13
  155.5 28.0 %all-to-all-done.3 = f32[32,72,128]{2,1,0:T(8,128)S(1)} async-done(((f32[32,72,128]{2,1,0:T(8,128)}), f32[32,72,128]{2,1,0:T(8,128)S(1)}, u32[]{:S(2)}, u32[]{:S(2)}) %all-to-all-start.3) | async-done | bytes 1179680 | tf_op jit(solution)/shard_map/all_to_all | solution.py:377
  183.8 2.0 %pad_maximum_fusion = f32[2,100,32,128]{3,2,1,0:T(8,128)} fusion(f32[2,4,32,128]{3,2,1,0:T(8,128)S(1)} %bitcast.62, f32[2,32,32,128]{3,2,1,0:T(8,128)S(1)} %bitcast.54, f32[2,64,32,128]{3,2,1,0:T(8,128)S(1)} %bitcast.49), kind=kLoop, calls=%fused_computation | loop fusion | flops 1638400 | bytes 6553600 | tf_op jit(solution)/shard_map/concatenate | solution.py:500
  (43 shorter events, 12.7 us)
Async XLA Ops:
  0.0 0.9 slice-start
  0.0 1.7 slice-start.1
  3.4 8.8 %copy-start.5 = (s32[1,4096]{1,0:T(1,128)S(1)}, s32[1,4096]{1,0:T(1,128)}, u32[]{:S(2)}) copy-start(s32[1,4096]{1,0:T(1,128)} %param.11) | copy-start | bytes 49156
  3.4 59.5 %all-to-all-start = ((f32[32,136,128]{2,1,0:T(8,128)}), f32[32,136,128]{2,1,0:T(8,128)S(1)}, u32[]{:S(2)}, u32[]{:S(2)}) async-start(f32[32,136,128]{2,1,0:T(8,128)} %pad_maximum_fusion.1), calls=%async_computation | async-start | bytes 4456448 | tf_op jit(solution)/shard_map/all_to_all | solution.py:377
  13.4 10.4 %collective-permute-start.1 = (f32[5,32,128]{2,1,0:T(8,128)S(1)}, f32[5,32,128]{2,1,0:T(8,128)S(1)}, u32[]{:S(2)}, u32[]{:S(2)}) collective-permute-start(f32[5,32,128]{2,1,0:T(8,128)S(1)} %get-tuple-element.35), channel_id=1, source_target_pairs={{0,8},{8,16},{16,24},{24,0},{1,9},{9,17},{17,25},{25,1},{2,10},{10... | collective-permute-start | bytes 245768 | tf_op jit(solution)/shard_map/ppermute | solution.py:449
  15.1 15.2 %collective-permute-start.2 = (f32[5,32,128]{2,1,0:T(8,128)S(1)}, f32[5,32,128]{2,1,0:T(8,128)S(1)}, u32[]{:S(2)}, u32[]{:S(2)}) collective-permute-start(f32[5,32,128]{2,1,0:T(8,128)S(1)} %get-tuple-element.36), channel_id=1, source_target_pairs={{0,16},{8,24},{16,0},{24,8},{1,17},{9,25},{17,1},{25,9},{2,18},{10... | collective-permute-start | bytes 245768 | tf_op jit(solution)/shard_map/ppermute | solution.py:449
  15.1 16.1 %collective-permute-start.3 = (f32[5,32,128]{2,1,0:T(8,128)S(1)}, f32[5,32,128]{2,1,0:T(8,128)S(1)}, u32[]{:S(2)}, u32[]{:S(2)}) collective-permute-start(f32[5,32,128]{2,1,0:T(8,128)S(1)} %get-tuple-element.37), channel_id=1, source_target_pairs={{0,24},{8,0},{16,8},{24,16},{1,25},{9,1},{17,9},{25,17},{2,26},{10... | collective-permute-start | bytes 245768 | tf_op jit(solution)/shard_map/ppermute | solution.py:449
  62.9 4.6 %copy-start = (f32[32,136,128]{2,1,0:T(8,128)}, f32[32,136,128]{2,1,0:T(8,128)S(1)}, u32[]{:S(2)}) copy-start(f32[32,136,128]{2,1,0:T(8,128)S(1)} %all-to-all-done.field_ref) | copy-start | bytes 6684676
  62.9 30.3 %all-to-all-start.2 = ((f32[32,64,128]{2,1,0:T(8,128)}), f32[32,64,128]{2,1,0:T(8,128)S(1)}, u32[]{:S(2)}, u32[]{:S(2)}) async-start(f32[32,64,128]{2,1,0:T(8,128)} %bitcast.56), calls=%async_computation.2 | async-start | bytes 2097152 | tf_op jit(solution)/shard_map/all_to_all | solution.py:377
  66.1 22.3 %collective-permute-start = (f32[1,32,8,128]{3,2,1,0:T(8,128)S(1)}, f32[1,32,8,128]{3,2,1,0:T(8,128)S(1)}, u32[]{:S(2)}, u32[]{:S(2)}) collective-permute-start(f32[1,32,8,128]{3,2,1,0:T(8,128)S(1)} %slice_bitcast_fusion.1), channel_id=1, source_target_pairs={{0,1},{1,0},{2,3},{3,2},{4,5},{5,4},{6,7},{7,6},{8,9},{9,8},{10,11... | collective-permute-start | bytes 393224 | tf_op jit(solution)/shard_map/ppermute | solution.py:424
  89.3 1.9 %collective-permute-start.4 = (f32[2,32,8,128]{3,2,1,0:T(8,128)S(1)}, f32[2,32,8,128]{3,2,1,0:T(8,128)S(1)}, u32[]{:S(2)}, u32[]{:S(2)}) collective-permute-start(f32[2,32,8,128]{3,2,1,0:T(8,128)S(1)} %pad_maximum_fusion.6), channel_id=1, source_target_pairs={{0,8},{8,0},{16,24},{24,16},{1,9},{9,1},{17,25},{25,17},{2,10},{10... | collective-permute-start | bytes 786440 | tf_op jit(solution)/shard_map/ppermute | solution.py:424
  93.2 1.0 copy-start.2
  94.2 53.2 %all-to-all-start.1 = ((f32[32,128,128]{2,1,0:T(8,128)}), f32[32,128,128]{2,1,0:T(8,128)S(1)}, u32[]{:S(2)}, u32[]{:S(2)}) async-start(f32[32,128,128]{2,1,0:T(8,128)} %whole_fields.3), calls=%async_computation.1 | async-start | bytes 4194304 | tf_op jit(solution)/shard_map/all_to_all | solution.py:377
  97.9 31.0 %copy-start.4 = (f32[4,32,8,128]{3,2,1,0:T(8,128)S(1)}, f32[4,32,8,128]{3,2,1,0:T(8,128)}, u32[]{:S(2)}) copy-start(f32[4,32,8,128]{3,2,1,0:T(8,128)} %pad_maximum_fusion.4) | copy-start | bytes 1572868
  97.9 31.0 %collective-permute-start.5 = (f32[4,32,8,128]{3,2,1,0:T(8,128)}, f32[4,32,8,128]{3,2,1,0:T(8,128)S(1)}, u32[]{:S(2)}, u32[]{:S(2)}) collective-permute-start(f32[4,32,8,128]{3,2,1,0:T(8,128)} %pad_maximum_fusion.4), channel_id=1, source_target_pairs={{0,16},{8,24},{16,0},{24,8},{1,17},{9,25},{17,1},{25,9},{2,18},{10... | collective-permute-start | bytes 1572872 | tf_op jit(solution)/shard_map/ppermute | solution.py:424
  130.3 12.9 %copy-start.3 = (f32[32,64,128]{2,1,0:T(8,128)S(1)}, f32[32,64,128]{2,1,0:T(8,128)}, u32[]{:S(2)}) copy-start(f32[32,64,128]{2,1,0:T(8,128)} %whole_fields.4) | copy-start | bytes 3145732
  147.4 6.3 %copy-start.1 = (f32[32,128,128]{2,1,0:T(8,128)}, f32[32,128,128]{2,1,0:T(8,128)S(1)}, u32[]{:S(2)}) copy-start(f32[32,128,128]{2,1,0:T(8,128)S(1)} %all-to-all-done.1) | copy-start | bytes 6291460
  147.4 36.1 %all-to-all-start.3 = ((f32[32,72,128]{2,1,0:T(8,128)}), f32[32,72,128]{2,1,0:T(8,128)S(1)}, u32[]{:S(2)}, u32[]{:S(2)}) async-start(f32[32,72,128]{2,1,0:T(8,128)} %pad_maximum_fusion.2), calls=%async_computation.3 | async-start | bytes 2359296 | tf_op jit(solution)/shard_map/all_to_all | solution.py:377

commit v4 on v3

--- a/solution.py
+++ b/solution.py
@@ -35,26 +35,26 @@
 
 def lon_weights(lon):
     head, tail = bell(range(lon), range(lon))
-    return jnp.concatenate([head, head, tail], axis=0)
+    return jnp.block([[head, tail], [head, jnp.zeros_like(tail)]])
 
 
 def lat_weights(rows, pad):
     head, tail = bell(range(rows), range(-pad, rows + pad))
-    return jnp.concatenate([head, head, tail], axis=1)
+    return jnp.block([[head, head], [tail, jnp.zeros_like(tail)]])
 
 
 def along_lon(x, weights):
-    head, tail = halves(x)
-    return 0.5 * x + jnp.dot(
-        jnp.concatenate([head, tail, head], axis=1), weights, preferred_element_type=F32
-    )
+    lon = x.shape[1]
+    both = jnp.concatenate(halves(x), axis=1)
+    result = jnp.dot(both, weights, preferred_element_type=F32)
+    return 0.5 * x + result[:, :lon] + result[:, lon:]
 
 
 def along_lat(x, weights, own):
-    head, tail = halves(x)
-    return 0.5 * own + jnp.dot(
-        weights, jnp.concatenate([head, tail, head], axis=0), preferred_element_type=F32
-    )
+    rows = own.shape[0]
+    both = jnp.concatenate(halves(x), axis=0)
+    result = jnp.dot(weights, both, preferred_element_type=F32)
+    return 0.5 * own + result[:rows] + result[rows:]
 
 
 def patch_sums(squares, hot):
@@ -102,12 +102,12 @@
 
 
 def field_kernel(
-    regions, me_ref, field_ref, truth_ref, map_ref, lon_ref, lat_ref, out_ref, cells, hots
+    regions, places_ref, field_ref, truth_ref, hots, lon_ref, lat_ref, out_ref, cells
 ):
-    sources, _, lon = field_ref.shape
+    outer, _, inner, _, lon = field_ref.shape
     rows = truth_ref.shape[2]
-    held = field_ref.shape[1] // rows
-    devices = sources // regions
+    held = field_ref.shape[3] // rows
+    devices = outer * inner // regions
     members = devices * held
     blocks = members // BLOCK
     pairs = blocks * (BLOCK // 2) + blocks * (blocks - 1) // 2 * BLOCK
@@ -117,19 +117,11 @@
     scale = float(np.sqrt(PATCH))
 
     def shift_of(region):
-        return lax.rem(me_ref[0] - region + regions, regions)
-
-    @pl.when(pl.program_id(0) == 0)
-    def _():
-        patch = lax.broadcasted_iota(jnp.int32, (patches, lon), 0).astype(F32)
-
-        def build(block, carry):
-            for j in range(STEP):
-                own = map_ref[shift_of(block // steps), 0, pl.ds(block % steps * STEP + j, 1), :]
-                hots[block, :, j * lon : (j + 1) * lon] = (patch == own).astype(BF16)
-            return carry
-
-        lax.fori_loop(0, regions * steps, build, 0)
+        return lax.rem(places_ref[0] - region + regions, regions)
+
+    def place(region, device):
+        index = places_ref[1 + region * devices + device]
+        return (index, 0, 0) if inner == 1 else (index // inner, 0, index % inner)
 
     def smoothed(pair):
         wide = jnp.concatenate([along_lon(x, lon_ref[...]) for x in pair], axis=1)
@@ -140,7 +132,7 @@
         pair = [
             jnp.concatenate(
                 [
-                    field_ref[region * devices + device, k * rows : (k + 1) * rows, :]
+                    field_ref[*place(region, device), k * rows : (k + 1) * rows, :]
                     for region in range(regions)
                 ],
                 axis=0,
@@ -203,47 +195,74 @@
         )
         for region in range(regions):
             for k in range(held):
-                out_ref[region * devices + device, k * rows : (k + 1) * rows, :] = result[
+                out_ref[*place(region, device), k * rows : (k + 1) * rows, :] = result[
                     region * rows : (region + 1) * rows, k * lon : (k + 1) * lon
                 ]
 
 
-def whole_fields(fields, count, held, extra, offset):
-    sources, _, lon = fields.shape
+def hots_kernel(region_ref, extra_ref, hots):
+    regions, _, rows, lon = extra_ref.shape
+    _, patches, _ = hots.shape
+    steps = rows // STEP
+    patch = lax.broadcasted_iota(jnp.int32, (patches, lon), 0).astype(F32)
+    for region in range(regions):
+        shift = lax.rem(region_ref[0] - region + regions, regions)
+        for row in range(rows):
+            block, j = region * steps + row // STEP, row % STEP
+            own = extra_ref[shift, 0, row : row + 1, :]
+            hots[block, :, j * lon : (j + 1) * lon] = (patch == own).astype(BF16)
+
+
+def patch_hots(extra):
+    regions, variables, rows, lon = extra.shape
+    shape = (regions * rows // STEP, rows * lon // PATCH, STEP * lon)
+    return pl.pallas_call(
+        hots_kernel,
+        out_shape=jax.ShapeDtypeStruct(shape, BF16),
+        grid=(1,),
+        in_specs=[
+            pl.BlockSpec(memory_space=pltpu.SMEM),
+            pl.BlockSpec((regions, 1, rows, lon), lambda i: (0, variables - 1, 0, 0)),
+        ],
+        out_specs=pl.BlockSpec(shape, lambda i: (0, 0, 0)),
+        compiler_params=pltpu.CompilerParams(vmem_limit_bytes=VMEM),
+        name="patch_hots",
+    )(lax.axis_index("region").reshape(1), extra)
+
+
+def whole_fields(fields, places, extra, hots, offset):
+    outer, count, inner, height, lon = fields.shape
     regions, variables, rows, _ = extra.shape
-    members = sources // regions * held
+    members = outer * inner // regions * (height // rows)
     patches = rows * lon // PATCH
     every = regions * rows
-    me = lax.axis_index("region").reshape(1)
-    block = pl.BlockSpec((sources, held * rows, lon), lambda v, me: (0, v, 0))
+    table = jnp.concatenate([lax.axis_index("region").reshape(1), places])
+    block = pl.BlockSpec((outer, 1, inner, height, lon), lambda v, table: (0, v, 0, 0, 0))
     pairs = every * lon * members * (members // 2 + 1)
     return pl.pallas_call(
         functools.partial(field_kernel, regions),
-        out_shape=jax.ShapeDtypeStruct((sources, count * held * rows, lon), F32),
+        out_shape=jax.ShapeDtypeStruct(fields.shape, F32),
         grid_spec=pltpu.PrefetchScalarGridSpec(
             num_scalar_prefetch=1,
             grid=(count,),
             in_specs=[
                 block,
-                pl.BlockSpec((regions, 1, rows, lon), lambda v, me: (0, v + offset, 0, 0)),
-                pl.BlockSpec((regions, 1, rows, lon), lambda v, me: (0, variables - 1, 0, 0)),
-                pl.BlockSpec((3 * lon, lon), lambda v, me: (0, 0)),
-                pl.BlockSpec((every, 3 * every), lambda v, me: (0, 0)),
+                pl.BlockSpec((regions, 1, rows, lon), lambda v, table: (0, v + offset, 0, 0)),
+                pl.BlockSpec(hots.shape, lambda v, table: (0, 0, 0)),
+                pl.BlockSpec((2 * lon, 2 * lon), lambda v, table: (0, 0)),
+                pl.BlockSpec((2 * every, 2 * every), lambda v, table: (0, 0)),
             ],
             out_specs=block,
             scratch_shapes=[
                 pltpu.VMEM((every * members, lon), F32),
-                pltpu.VMEM((every // STEP, patches, STEP * lon), BF16),
             ],
         ),
         compiler_params=pltpu.CompilerParams(vmem_limit_bytes=VMEM),
         cost_estimate=pl.CostEstimate(
-            flops=count * pairs * patches * 8,
-            bytes_accessed=8 * count * every * lon * members,
-            transcendentals=0,
+            flops=count * pairs * patches * 8, bytes_accessed=8 * fields.size, transcendentals=0
         ),
         name="whole_fields",
-    )(me, fields, extra, extra, lon_weights(lon), lat_weights(every, 0))
+    )(table, fields, extra, hots, lon_weights(lon), lat_weights(every, 0))
 
 
 def smooth_kernel(own_ref, low_ref, high_ref, lon_ref, lat_ref, out_ref):
@@ -272,8 +291,8 @@
             block,
             edge,
             edge,
-            pl.BlockSpec((3 * lon, lon), lambda v: (0, 0)),
-            pl.BlockSpec((rows, 3 * span), lambda v: (0, 0)),
+            pl.BlockSpec((2 * lon, 2 * lon), lambda v: (0, 0)),
+            pl.BlockSpec((2 * rows, 2 * span), lambda v: (0, 0)),
         ],
         out_specs=block,
         compiler_params=pltpu.CompilerParams(vmem_limit_bytes=VMEM),
@@ -381,56 +400,52 @@
     held, variables, rows, lon = x.shape
     total = variables // count
     x = jnp.transpose(x.reshape(held, total, count, rows, lon), (1, 2, 0, 3, 4))
-    return x.reshape(total, count * held * rows, lon)
-
-
-def kept_rows(blocks, held, rows):
-    total, height, lon = blocks.shape
-    count = height // (held * rows)
-    x = blocks.reshape(total, count, held, rows, lon)
-    return jnp.transpose(x, (2, 0, 1, 3, 4)).reshape(held, total * count, rows, lon)
+    return x.reshape(total, count, 1, held * rows, lon)
+
+
+def kept_rows(blocks, rows):
+    total, count, _, height, lon = blocks.shape
+    x = blocks.reshape(total, count, height // rows, rows, lon)
+    return jnp.transpose(x, (2, 0, 1, 3, 4)).reshape(height // rows, total * count, rows, lon)
 
 
 def is_power(n):
     return n & (n - 1) == 0
 
 
-def sent_pieces(x, regions, devices):
-    held, variables, rows, lon = x.shape
-    near = devices // variables
-    x = x.reshape(held, variables, regions, near, rows // (regions * near), lon)
-    x = jnp.transpose(x, (2, 1, 3, 0, 4, 5))
-    return x.reshape(regions * devices, -1, lon)
-
-
-def kept_pieces(blocks, held, variables, regions, devices):
-    near = devices // variables
-    lon = blocks.shape[-1]
-    x = blocks.reshape(regions, variables, near, held, -1, lon)
-    return jnp.transpose(x, (3, 1, 0, 2, 4, 5)).reshape(held, variables, -1, lon)
-
-
-def after(x, first):
-    return lax.optimization_barrier((x, first))[0]
+def shifted(x, places):
+    count = lax.axis_size("member")
+    return lax.ppermute(x, "member", [(i, (i + places) % count) for i in range(count)])
+
+
+def plane_steps(near):
+    regions = lax.axis_size("region")
+    far = [("region", 1 << bit) for bit in range(1, regions.bit_length() - 1)][::-1]
+    beside = [("member", 1 << bit) for bit in range(near.bit_length() - 1)]
+    return far + beside + [("region", 1)] * (regions > 1)
 
 
 def plane_gather(x, near, beside):
     x = x[None]
-    first = True
-    for axis, size in (("member", near), ("region", lax.axis_size("region"))):
-        index, step = lax.axis_index(axis), 1
-        while step < size:
-            count = lax.axis_size(axis)
-            other = lax.ppermute(x, axis, [(i, i ^ step) for i in range(count)])
-            if first:
-                other, beside = lax.optimization_barrier((other, beside))
-                first = False
-            low = (index & step) == 0
-            x = jnp.concatenate([jnp.where(low, x, other), jnp.where(low, other, x)], axis=0)
-            step *= 2
-            if axis == "region" and step * 2 == size:
-                x, beside = lax.optimization_barrier((x, beside))
+    steps = plane_steps(near)
+    for i, (axis, step) in enumerate(steps):
+        count = lax.axis_size(axis)
+        other = lax.ppermute(x, axis, [(j, j ^ step) for j in range(count)])
+        if i == 0:
+            other, beside = lax.optimization_barrier((other, beside))
+        x = jnp.concatenate([x, other], axis=0)
+        if i == len(steps) - 2:
+            x, beside = lax.optimization_barrier((x, beside))
     return x, beside
+
+
+def plane_index(region, member, near):
+    steps, index = plane_steps(near), 0
+    for i, (axis, step) in enumerate(steps):
+        other = region if axis == "region" else member % near
+        own = lax.axis_index(axis) if axis == "region" else lax.axis_index(axis) % near
+        index = index + jnp.where((other ^ own) & step, 1 << i, 0)
+    return index
 
 
 def extras(observed, patch_map, starts, counts):
@@ -457,47 +472,63 @@
     region, member = lax.axis_index("region"), lax.axis_index("member")
     total = regions * devices
     share = variables // total
+    whole = share * total
+    left = variables - whole
     chunks = [count for count in (share - share // 2, share // 2) if count]
-    left = variables - share * total
     sent, starts, counts, begin = [], [], [], 0
     for count in chunks:
         sent.append(sent_rows(forecast[:, begin : begin + count * total], count))
         starts.append(lambda r, m, b=begin, c=count: b + (r * devices + m) * c)
         counts.append(count)
         begin += count * total
+    shifts = []
     if left:
         near = devices // left
-        sent[0] = jnp.concatenate(
-            [sent[0], sent_pieces(forecast[:, begin:], regions, devices)], axis=1
-        )
+        plane = member // near
         starts.append(lambda r, m, b=begin: b + m // near)
         counts.append(1)
+        for t in range(left):
+            first = begin + lax.rem(plane + t, left)
+            x = lax.dynamic_slice_in_dim(forecast, first, 1, axis=1).reshape(held * rows, lon)
+            shifts.append(shifted(x, t * near) if t else x)
     extra = extras(observed, patch_map, starts, counts)
+    hots = patch_hots(extra)
     if len(chunks) > 1:
-        sent[1:], extra = lax.optimization_barrier((sent[1:], extra))
-    fields = [exchange(part) for part in sent]
+        sent[1:], extra, hots, shifts = lax.optimization_barrier((sent[1:], extra, hots, shifts))
+    order = jnp.arange(total, dtype=jnp.int32)
     results = [
-        whole_fields(field, count, held, extra, sum(chunks[:i]))
-        for i, (field, count) in enumerate(zip(fields, chunks))
+        whole_fields(exchange(part), order, extra, hots, sum(chunks[:i])) for i, part in enumerate(sent)
     ]
-    body = chunks[0] * held * rows
     if left:
-        piece = rows // (regions * near)
-        field, results[0] = plane_gather(fields[0][:, body:], near, results[0])
-        field = field.reshape(-1, total, held, piece, lon)
-        field = jnp.transpose(field, (1, 2, 0, 3, 4)).reshape(total, held * rows, lon)
-        result = whole_fields(field, 1, held, extra, share).reshape(total, held, rows, lon)
-        place = region * near + lax.rem(member, near)
-        result = lax.dynamic_slice_in_dim(result, place * piece, piece, axis=2)
-        results[-1] = jnp.concatenate([results[-1], result.reshape(total, -1, lon)], axis=1)
+        field, results[0] = plane_gather(jnp.stack(shifts), near, results[0])
+        members = order % devices
+        places = plane_index(order // devices, members, near) * left
+        places = places + (plane - members // near) % left
+        result = whole_fields(field[:, None], places, extra, hots, share)
+        result = result[0, 0]
+        shifts = [shifted(result[t], -t * near) if t else result[t] for t in range(left)]
+        shifts = jnp.stack(shifts + shifts).reshape(2 * left, held, rows, lon)
+        last = lax.dynamic_slice_in_dim(shifts, lax.rem(left - plane, left), left, axis=0)
+        last = jnp.swapaxes(last, 0, 1)
+        if len(chunks) > 1:
+            results[1], last = lax.optimization_barrier((results[1], last))
     backs = []
     for result in results:
-        backs.append(exchange(after(result, backs[-1:])))
-    parts = [kept_rows(back[:, : count * held * rows], held, rows) for back, count in zip(backs, chunks)]
+        if backs:
+            result, backs[-1] = lax.optimization_barrier((result, backs[-1]))
+        backs.append(exchange(result))
+    parts = [kept_rows(back, rows) for back in backs]
     if left:
-        last = chunks[-1] * held * rows
-        parts.append(kept_pieces(backs[-1][:, last:], held, left, regions, devices))
-    return jnp.concatenate(parts, axis=1)
+        parts.insert(1, last)
+    out = jnp.concatenate(
+        parts[:1] + [jnp.zeros((held, variables - parts[0].shape[1], rows, lon), F32)], axis=1
+    )
+    places = [parts[0].shape[1]] * 2
+    if left:
+        places = [whole, parts[0].shape[1]]
+    for part, first in zip(parts[1:], places):
+        out = lax.dynamic_update_slice_in_dim(out, part, first, axis=1)
+    return out
 
 
 def on_device(predicted_states, observed_analysis, tile_location_sequence):
@@ -506,10 +537,7 @@
     patch_map = patch_of_cell(tile_location_sequence[0], rows, lon)
     left = variables % (regions * devices)
     planes = left == 0 or (
-        devices % left == 0
-        and rows % (regions * devices // left) == 0
-        and is_power(regions)
-        and is_power(devices // left)
+        devices % left == 0 and is_power(regions) and is_power(devices // left)
     )
     if variables >= regions * devices and planes:
         return spread_over_all(predicted_states, observed_analysis, patch_map)

time: 187 us -> 186 us (level)
  starting transfers between devices: 26 us -> 37.2 us
  waiting for transfers between devices: 95.6 us -> 88 us
  Pallas kernels: 44.2 us -> 39.6 us
  other arithmetic: 7.52 us -> 4.09 us
  local copies, waits for them, and re-layouts: 11.2 us -> 13.8 us
    ppermute x3 -> x9, waiting for transfers between devices: 19.2 us -> 56.5 us  [the longest x6 49.4 us: shifted(): lax.ppermute(x, 'member', [(i, (i + places) % count) for i in range(count)])]
    all_to_all x4, waiting for transfers between devices: 63.2 us -> 26.3 us  [exchange(): return lax.all_to_all(blocks, ('region', 'member'), 0, 0, tiled=True)]
    ppermute x3 -> x9, starting transfers between devices: 3.62 us -> 14.3 us  [the longest x6 11.2 us: shifted(): lax.ppermute(x, 'member', [(i, (i + places) % count) for i in range(count)])]
    ppermute x3, waiting for transfers between devices: 13.2 us -> 5.18 us  [extras(): piece = lax.ppermute(piece, 'region', ring)]
    pallas_call x3, Pallas kernels: 44.2 us -> 37.6 us  [whole_fields(): pl.pallas_call(functools.partial(field_kernel, regions), out_shape=jax.Sh...]
    concatenate x6 -> x4, other arithmetic: 5.64 us -> 2.14 us  [the longest x2 1.26 us: whole_fields(): table = jnp.concatenate([lax.axis_index('region').reshape(1), places])]
    concatenate x0 -> x1, local copies, waits for them, and re-layouts: none -> 2.05 us  [spread_over_all(): jnp.concatenate(parts[:1] + [jnp.zeros((held, variables - parts[0].shape[...]
    pallas_call x0 -> x1, Pallas kernels: none -> 2.04 us  [patch_hots(): pl.pallas_call(hots_kernel, out_shape=jax.ShapeDtypeStruct(shape, BF16),...]
  transfers between devices with their start and end apart: 10 -> 16, of which waited for: 9 -> 10; matrix products, arithmetic and copies ran while one was open for 7% -> 7% of each run, Pallas kernels for 24% -> 22%
where the time goes in v4:
time: 186 us; the launch traced here: 184 us
  waiting for transfers between devices  88 us (47%)
  Pallas kernels  39.6 us (21%)
  starting transfers between devices  37.2 us (20%)
  local copies, waits for them, and re-layouts  13.8 us (7%)
  other arithmetic  4.09 us (2%)
    ppermute x6, waiting for transfers between devices, shifted(): lax.ppermute(x, 'member', [(i, (i + places) % count) for i in range(count)])  49.4 us
    pallas_call x3, Pallas kernels, whole_fields(): pl.pallas_call(functools.partial(field_kernel, regions), out_shape=jax.Sh...  37.6 us
    all_to_all x4, waiting for transfers between devices, exchange(): return lax.all_to_all(blocks, ('region', 'member'), 0, 0, tiled=True)  26.3 us
    all_to_all x4, starting transfers between devices, exchange(): return lax.all_to_all(blocks, ('region', 'member'), 0, 0, tiled=True)  20.7 us
    ppermute x6, starting transfers between devices, shifted(): lax.ppermute(x, 'member', [(i, (i + places) % count) for i in range(count)])  11.2 us
    ppermute x3, waiting for transfers between devices, plane_gather(): other = lax.ppermute(x, axis, [(j, j ^ step) for j in range(count)])  7.11 us
    ppermute x3, waiting for transfers between devices, extras(): piece = lax.ppermute(piece, 'region', ring)  5.18 us
  transfers between devices with their start and end apart: 16, of which 10 were waited for; matrix products, arithmetic and copies ran while one was open for 7% of the time, Pallas kernels for 22%

profile of v4, /device:TPU:1, one launch (start us, length us, event | category | flops | bytes accessed | tf_op | source)
XLA Modules:
  0.0 183.9 jit_solution(9194564125989121534)
XLA Ops:
  0.0 1.6 slice-done
  1.6 1.6 copy.11
  3.2 7.1 %all-to-all-start.1 = ((f32[32,2,1,64,128]{4,3,2,1,0:T(8,128)}), f32[32,2,1,64,128]{4,3,2,1,0:T(8,128)S(1)}, u32[]{:S(2)}, u32[]{:S(2)}) async-start(f32[32,2,1,64,128]{4,3,2,1,0:T(8,128)} %bitcast.64), calls=%async_computation.1 | async-start | bytes 4194304 | tf_op jit(solution)/shard_map/all_to_all | solution.py:396
  13.1 1.7 collective-permute-start
  16.2 2.2 %collective-permute-start.4 = (f32[64,128]{1,0:T(8,128)S(1)}, f32[64,128]{1,0:T(8,128)S(1)}, u32[]{:S(2)}, u32[]{:S(2)}) collective-permute-start(f32[64,128]{1,0:T(8,128)S(1)} %bitcast.86), channel_id=1, source_target_pairs={{0,4},{1,5},{2,6},{3,7},{4,0},{5,1},{6,2},{7,3},{8,12},{9,13},{10,... | collective-permute-start | bytes 98312 | tf_op jit(solution)/shard_map/ppermute | solution.py:418
  19.5 1.3 slice_bitcast_fusion
  22.9 3.1 %collective-permute-start.3 = (f32[64,128]{1,0:T(8,128)S(1)}, f32[64,128]{1,0:T(8,128)S(1)}, u32[]{:S(2)}, u32[]{:S(2)}) collective-permute-start(f32[64,128]{1,0:T(8,128)S(1)} %bitcast.84), channel_id=1, source_target_pairs={{0,2},{1,3},{2,4},{3,5},{4,6},{5,7},{6,0},{7,1},{8,10},{9,11},{10,... | collective-permute-start | bytes 98312 | tf_op jit(solution)/shard_map/ppermute | solution.py:418
  26.0 3.3 %collective-permute-done.1 = f32[5,32,128]{2,1,0:T(8,128)S(1)} collective-permute-done((f32[5,32,128]{2,1,0:T(8,128)S(1)}, f32[5,32,128]{2,1,0:T(8,128)S(1)}, u32[]{:S(2)}, u32[]{:S(2)}) %collective-permute-start.1) | collective-permute-done | bytes 81952 | tf_op jit(solution)/shard_map/ppermute | solution.py:464
  30.9 2.0 %patch_hots.1.hots = bf16[4,32,4096]{2,1,0:T(8,128)(2,1)} custom-call(s32[1]{0:T(128)} %bitcast.region_ref, f32[4,5,32,128]{3,2,1,0:T(8,128)} %pad_maximum_fusion.1.extra_ref.truth_ref), custom_call_target="tpu_custom_call" | custom-call | tf_op jit(solution)/shard_map/patch_hots/pallas_call | solution.py:219
  32.9 27.6 %collective-permute-done.4 = f32[64,128]{1,0:T(8,128)S(1)} collective-permute-done((f32[64,128]{1,0:T(8,128)S(1)}, f32[64,128]{1,0:T(8,128)S(1)}, u32[]{:S(2)}, u32[]{:S(2)}) %collective-permute-start.4) | collective-permute-done | bytes 32800 | tf_op jit(solution)/shard_map/ppermute | solution.py:418
  61.6 3.3 %all-to-all-start = ((f32[32,1,1,64,128]{4,3,2,1,0:T(8,128)}), f32[32,1,1,64,128]{4,3,2,1,0:T(8,128)S(1)}, u32[]{:S(2)}, u32[]{:S(2)}) async-start(f32[32,1,1,64,128]{4,3,2,1,0:T(8,128)} %bitcast.3), calls=%async_computation | async-start | bytes 2097152 | tf_op jit(solution)/shard_map/all_to_all | solution.py:396
  64.9 1.5 collective-permute-start.6
  67.0 17.1 %whole_fields.4 = f32[32,2,1,64,128]{4,3,2,1,0:T(8,128)} custom-call(s32[33]{0:T(128)} %pad_add_fusion.places_ref, f32[32,2,1,64,128]{4,3,2,1,0:T(8,128)} %copy-done, f32[4,5,32,128]{3,2,1,0:T(8,128)} %pad_maximum_fusion.1.extra_ref.truth_ref, bf16[4,32,4096]{2,1,0:T(8,128)(2,1)} %patch_hots.1.hots, bf16[256,256]{1,0:T(8,128)(2,1)} %constant.197.lon_ref, ...), custom_call_target="tpu_custom_call" | custom-call | flops 1207959552 | bytes 4194304 | tf_op jit(solution)/shard_map/whole_fields/pallas_call | solution.py:242
  85.4 7.1 %collective-permute-done.7 = f32[2,4,64,128]{3,2,1,0:T(8,128)S(1)} collective-permute-done((f32[2,4,64,128]{3,2,1,0:T(8,128)S(1)}, f32[2,4,64,128]{3,2,1,0:T(8,128)S(1)}, u32[]{:S(2)}, u32[]{:S(2)}) %collective-permute-start.7) | collective-permute-done | bytes 262176 | tf_op jit(solution)/shard_map/ppermute | solution.py:433
  94.3 6.3 %all-to-all-start.2 = ((f32[32,2,1,64,128]{4,3,2,1,0:T(8,128)}), f32[32,2,1,64,128]{4,3,2,1,0:T(8,128)S(1)}, u32[]{:S(2)}, u32[]{:S(2)}) async-start(f32[32,2,1,64,128]{4,3,2,1,0:T(8,128)} %whole_fields.4), calls=%async_computation.2 | async-start | bytes 4194304 | tf_op jit(solution)/shard_map/all_to_all | solution.py:396
  101.6 10.1 %whole_fields.3 = f32[32,1,1,64,128]{4,3,2,1,0:T(8,128)} custom-call(s32[33]{0:T(128)} %pad_add_fusion.places_ref, f32[32,1,1,64,128]{4,3,2,1,0:T(8,128)} %copy-done.1, f32[4,5,32,128]{3,2,1,0:T(8,128)} %pad_maximum_fusion.1.extra_ref.truth_ref, bf16[4,32,4096]{2,1,0:T(8,128)(2,1)} %patch_hots.1.hots, bf16[256,256]{1,0:T(8,128)(2,1)} %constant.197.lon_ref, ...), custom_call_target="tpu_custom_call" | custom-call | flops 603979776 | bytes 2097152 | tf_op jit(solution)/shard_map/whole_fields/pallas_call | solution.py:242
  112.8 10.4 %whole_fields.5 = f32[8,1,4,64,128]{4,3,2,1,0:T(8,128)} custom-call(s32[33]{0:T(128)} %pad_add_fusion.1.places_ref, f32[8,1,4,64,128]{4,3,2,1,0:T(8,128)} %maximum_bitcast_fusion.field_ref, f32[4,5,32,128]{3,2,1,0:T(8,128)} %pad_maximum_fusion.1.extra_ref.truth_ref, bf16[4,32,4096]{2,1,0:T(8,128)(2,1)} %patch_hots.1.hots, ...), custom_call_target="tpu_custom_call" | custom-call | flops 603979776 | bytes 2097152 | tf_op jit(solution)/shard_map/whole_fields/pallas_call | solution.py:242
  124.0 1.5 collective-permute-start.11
  125.5 2.1 %collective-permute-start.10 = (f32[64,128]{1,0:T(8,128)S(1)}, f32[64,128]{1,0:T(8,128)S(1)}, u32[]{:S(2)}, u32[]{:S(2)}) collective-permute-start(f32[64,128]{1,0:T(8,128)S(1)} %get-tuple-element.49), channel_id=1, source_target_pairs={{0,4},{1,5},{2,6},{3,7},{4,0},{5,1},{6,2},{7,3},{8,12},{9,13},{10,... | collective-permute-start | bytes 98312 | tf_op jit(solution)/shard_map/ppermute | solution.py:418
  128.8 8.2 %collective-permute-done.9 = f32[64,128]{1,0:T(8,128)S(1)} collective-permute-done((f32[64,128]{1,0:T(8,128)S(1)}, f32[64,128]{1,0:T(8,128)S(1)}, u32[]{:S(2)}, u32[]{:S(2)}) %collective-permute-start.9) | collective-permute-done | bytes 32800 | tf_op jit(solution)/shard_map/ppermute | solution.py:418
  137.0 13.7 %collective-permute-done.10 = f32[64,128]{1,0:T(8,128)S(1)} collective-permute-done((f32[64,128]{1,0:T(8,128)S(1)}, f32[64,128]{1,0:T(8,128)S(1)}, u32[]{:S(2)}, u32[]{:S(2)}) %collective-permute-start.10) | collective-permute-done | bytes 32800 | tf_op jit(solution)/shard_map/ppermute | solution.py:418
  151.8 4.0 %all-to-all-start.3 = ((f32[32,1,1,64,128]{4,3,2,1,0:T(8,128)}), f32[32,1,1,64,128]{4,3,2,1,0:T(8,128)S(1)}, u32[]{:S(2)}, u32[]{:S(2)}) async-start(f32[32,1,1,64,128]{4,3,2,1,0:T(8,128)} %whole_fields.3), calls=%async_computation.3 | async-start | bytes 2097152 | tf_op jit(solution)/shard_map/all_to_all | solution.py:396
  156.0 2.1 %concatenate.117 = f32[2,100,32,128]{3,2,1,0:T(8,128)} pad(f32[2,64,32,128]{3,2,1,0:T(8,128)S(1)} %bitcast.66, f32[]{:T(128)} %constant.173.clone.1), padding=0_0x0_36x0_0x0_0 | pad | bytes 5373956 | tf_op jit(solution)/shard_map/concatenate | solution.py:523
  158.7 24.1 %all-to-all-done.3 = f32[32,1,1,64,128]{4,3,2,1,0:T(8,128)S(1)} async-done(((f32[32,1,1,64,128]{4,3,2,1,0:T(8,128)}), f32[32,1,1,64,128]{4,3,2,1,0:T(8,128)S(1)}, u32[]{:S(2)}, u32[]{:S(2)}) %all-to-all-start.3) | async-done | bytes 1048608 | tf_op jit(solution)/shard_map/all_to_all | solution.py:396
  (55 shorter events, 20.7 us)
Async XLA Ops:
  0.0 1.6 slice-start
  3.2 8.8 %copy-start.3 = (s32[1,4096]{1,0:T(1,128)S(1)}, s32[1,4096]{1,0:T(1,128)}, u32[]{:S(2)}) copy-start(s32[1,4096]{1,0:T(1,128)} %param.11) | copy-start | bytes 49156
  3.2 58.4 %all-to-all-start.1 = ((f32[32,2,1,64,128]{4,3,2,1,0:T(8,128)}), f32[32,2,1,64,128]{4,3,2,1,0:T(8,128)S(1)}, u32[]{:S(2)}, u32[]{:S(2)}) async-start(f32[32,2,1,64,128]{4,3,2,1,0:T(8,128)} %bitcast.64), calls=%async_computation.1 | async-start | bytes 4194304 | tf_op jit(solution)/shard_map/all_to_all | solution.py:396
  13.1 9.7 %collective-permute-start = (f32[5,32,128]{2,1,0:T(8,128)S(1)}, f32[5,32,128]{2,1,0:T(8,128)S(1)}, u32[]{:S(2)}, u32[]{:S(2)}) collective-permute-start(f32[5,32,128]{2,1,0:T(8,128)S(1)} %get-tuple-element.53), channel_id=1, source_target_pairs={{0,8},{8,16},{16,24},{24,0},{1,9},{9,17},{17,25},{25,1},{2,10},{10... | collective-permute-start | bytes 245768 | tf_op jit(solution)/shard_map/ppermute | solution.py:464
  14.8 14.5 %collective-permute-start.1 = (f32[5,32,128]{2,1,0:T(8,128)S(1)}, f32[5,32,128]{2,1,0:T(8,128)S(1)}, u32[]{:S(2)}, u32[]{:S(2)}) collective-permute-start(f32[5,32,128]{2,1,0:T(8,128)S(1)} %get-tuple-element.54), channel_id=1, source_target_pairs={{0,16},{8,24},{16,0},{24,8},{1,17},{9,25},{17,1},{25,9},{2,18},{10... | collective-permute-start | bytes 245768 | tf_op jit(solution)/shard_map/ppermute | solution.py:464
  14.8 15.3 %collective-permute-start.2 = (f32[5,32,128]{2,1,0:T(8,128)S(1)}, f32[5,32,128]{2,1,0:T(8,128)S(1)}, u32[]{:S(2)}, u32[]{:S(2)}) collective-permute-start(f32[5,32,128]{2,1,0:T(8,128)S(1)} %get-tuple-element.55), channel_id=1, source_target_pairs={{0,24},{8,0},{16,8},{24,16},{1,25},{9,1},{17,9},{25,17},{2,26},{10... | collective-permute-start | bytes 245768 | tf_op jit(solution)/shard_map/ppermute | solution.py:464
  16.2 44.3 %collective-permute-start.4 = (f32[64,128]{1,0:T(8,128)S(1)}, f32[64,128]{1,0:T(8,128)S(1)}, u32[]{:S(2)}, u32[]{:S(2)}) collective-permute-start(f32[64,128]{1,0:T(8,128)S(1)} %bitcast.86), channel_id=1, source_target_pairs={{0,4},{1,5},{2,6},{3,7},{4,0},{5,1},{6,2},{7,3},{8,12},{9,13},{10,... | collective-permute-start | bytes 98312 | tf_op jit(solution)/shard_map/ppermute | solution.py:418
  18.3 42.2 %collective-permute-start.5 = (f32[64,128]{1,0:T(8,128)S(1)}, f32[64,128]{1,0:T(8,128)S(1)}, u32[]{:S(2)}, u32[]{:S(2)}) collective-permute-start(f32[64,128]{1,0:T(8,128)S(1)} %bitcast.85), channel_id=1, source_target_pairs={{0,6},{1,7},{2,0},{3,1},{4,2},{5,3},{6,4},{7,5},{8,14},{9,15},{10,... | collective-permute-start | bytes 98312 | tf_op jit(solution)/shard_map/ppermute | solution.py:418
  22.9 37.6 %collective-permute-start.3 = (f32[64,128]{1,0:T(8,128)S(1)}, f32[64,128]{1,0:T(8,128)S(1)}, u32[]{:S(2)}, u32[]{:S(2)}) collective-permute-start(f32[64,128]{1,0:T(8,128)S(1)} %bitcast.84), channel_id=1, source_target_pairs={{0,2},{1,3},{2,4},{3,5},{4,6},{5,7},{6,0},{7,1},{8,10},{9,11},{10,... | collective-permute-start | bytes 98312 | tf_op jit(solution)/shard_map/ppermute | solution.py:418
  61.6 5.4 %copy-start = (f32[32,2,1,64,128]{4,3,2,1,0:T(8,128)}, f32[32,2,1,64,128]{4,3,2,1,0:T(8,128)S(1)}, u32[]{:S(2)}) copy-start(f32[32,2,1,64,128]{4,3,2,1,0:T(8,128)S(1)} %all-to-all-done.1.field_ref) | copy-start | bytes 6291460
  61.6 31.7 %all-to-all-start = ((f32[32,1,1,64,128]{4,3,2,1,0:T(8,128)}), f32[32,1,1,64,128]{4,3,2,1,0:T(8,128)S(1)}, u32[]{:S(2)}, u32[]{:S(2)}) async-start(f32[32,1,1,64,128]{4,3,2,1,0:T(8,128)} %bitcast.3), calls=%async_computation | async-start | bytes 2097152 | tf_op jit(solution)/shard_map/all_to_all | solution.py:396
  64.9 19.2 %collective-permute-start.6 = (f32[1,4,64,128]{3,2,1,0:T(8,128)S(1)}, f32[1,4,64,128]{3,2,1,0:T(8,128)S(1)}, u32[]{:S(2)}, u32[]{:S(2)}) collective-permute-start(f32[1,4,64,128]{3,2,1,0:T(8,128)S(1)} %maximum_bitcast_fusion.1), channel_id=1, source_target_pairs={{0,16},{8,24},{16,0},{24,8},{1,17},{9,25},{17,1},{25,9},{2,18},{10... | collective-permute-start | bytes 393224 | tf_op jit(solution)/shard_map/ppermute | solution.py:433
  84.1 8.4 %collective-permute-start.7 = (f32[2,4,64,128]{3,2,1,0:T(8,128)S(1)}, f32[2,4,64,128]{3,2,1,0:T(8,128)S(1)}, u32[]{:S(2)}, u32[]{:S(2)}) collective-permute-start(f32[2,4,64,128]{3,2,1,0:T(8,128)S(1)} %pad_maximum_fusion.2), channel_id=1, source_target_pairs={{0,1},{1,0},{2,3},{3,2},{4,5},{5,4},{6,7},{7,6},{8,9},{9,8},{10,11... | collective-permute-start | bytes 786440 | tf_op jit(solution)/shard_map/ppermute | solution.py:433
  93.3 1.0 copy-start.1
  94.3 57.5 %all-to-all-start.2 = ((f32[32,2,1,64,128]{4,3,2,1,0:T(8,128)}), f32[32,2,1,64,128]{4,3,2,1,0:T(8,128)S(1)}, u32[]{:S(2)}, u32[]{:S(2)}) async-start(f32[32,2,1,64,128]{4,3,2,1,0:T(8,128)} %whole_fields.4), calls=%async_computation.2 | async-start | bytes 4194304 | tf_op jit(solution)/shard_map/all_to_all | solution.py:396
  100.7 11.1 %copy-start.2 = (f32[4,4,64,128]{3,2,1,0:T(8,128)S(1)}, f32[4,4,64,128]{3,2,1,0:T(8,128)}, u32[]{:S(2)}) copy-start(f32[4,4,64,128]{3,2,1,0:T(8,128)} %pad_maximum_fusion) | copy-start | bytes 1572868
  100.7 11.0 %collective-permute-start.8 = (f32[4,4,64,128]{3,2,1,0:T(8,128)}, f32[4,4,64,128]{3,2,1,0:T(8,128)S(1)}, u32[]{:S(2)}, u32[]{:S(2)}) collective-permute-start(f32[4,4,64,128]{3,2,1,0:T(8,128)} %pad_maximum_fusion), channel_id=1, source_target_pairs={{0,8},{8,0},{16,24},{24,16},{1,9},{9,1},{17,25},{25,17},{2,10},{10... | collective-permute-start | bytes 1572872 | tf_op jit(solution)/shard_map/ppermute | solution.py:433
  124.0 26.7 %collective-permute-start.11 = (f32[64,128]{1,0:T(8,128)S(1)}, f32[64,128]{1,0:T(8,128)S(1)}, u32[]{:S(2)}, u32[]{:S(2)}) collective-permute-start(f32[64,128]{1,0:T(8,128)S(1)} %get-tuple-element.48), channel_id=1, source_target_pairs={{0,2},{1,3},{2,4},{3,5},{4,6},{5,7},{6,0},{7,1},{8,10},{9,11},{10,... | collective-permute-start | bytes 98312 | tf_op jit(solution)/shard_map/ppermute | solution.py:418
  125.5 25.1 %collective-permute-start.10 = (f32[64,128]{1,0:T(8,128)S(1)}, f32[64,128]{1,0:T(8,128)S(1)}, u32[]{:S(2)}, u32[]{:S(2)}) collective-permute-start(f32[64,128]{1,0:T(8,128)S(1)} %get-tuple-element.49), channel_id=1, source_target_pairs={{0,4},{1,5},{2,6},{3,7},{4,0},{5,1},{6,2},{7,3},{8,12},{9,13},{10,... | collective-permute-start | bytes 98312 | tf_op jit(solution)/shard_map/ppermute | solution.py:418
  127.7 9.3 %collective-permute-start.9 = (f32[64,128]{1,0:T(8,128)S(1)}, f32[64,128]{1,0:T(8,128)S(1)}, u32[]{:S(2)}, u32[]{:S(2)}) collective-permute-start(f32[64,128]{1,0:T(8,128)S(1)} %get-tuple-element.50), channel_id=1, source_target_pairs={{0,6},{1,7},{2,0},{3,1},{4,2},{5,3},{6,4},{7,5},{8,14},{9,15},{10,... | collective-permute-start | bytes 98312 | tf_op jit(solution)/shard_map/ppermute | solution.py:418
  151.8 31.0 %all-to-all-start.3 = ((f32[32,1,1,64,128]{4,3,2,1,0:T(8,128)}), f32[32,1,1,64,128]{4,3,2,1,0:T(8,128)S(1)}, u32[]{:S(2)}, u32[]{:S(2)}) async-start(f32[32,1,1,64,128]{4,3,2,1,0:T(8,128)} %whole_fields.3), calls=%async_computation.3 | async-start | bytes 2097152 | tf_op jit(solution)/shard_map/all_to_all | solution.py:396

commit v5 on v4

--- a/solution.py
+++ b/solution.py
@@ -426,16 +426,15 @@
 
 
 def plane_gather(x, near, beside):
+    beside = list(beside)
     x = x[None]
     steps = plane_steps(near)
     for i, (axis, step) in enumerate(steps):
         count = lax.axis_size(axis)
         other = lax.ppermute(x, axis, [(j, j ^ step) for j in range(count)])
-        if i == 0:
-            other, beside = lax.optimization_barrier((other, beside))
+        if i < len(beside):
+            other, beside[i] = lax.optimization_barrier((other, beside[i]))
         x = jnp.concatenate([x, other], axis=0)
-        if i == len(steps) - 2:
-            x, beside = lax.optimization_barrier((x, beside))
     return x, beside
 
 
@@ -500,7 +499,7 @@
         whole_fields(exchange(part), order, extra, hots, sum(chunks[:i])) for i, part in enumerate(sent)
     ]
     if left:
-        field, results[0] = plane_gather(jnp.stack(shifts), near, results[0])
+        field, results = plane_gather(jnp.stack(shifts), near, results)
         members = order % devices
         places = plane_index(order // devices, members, near) * left
         places = places + (plane - members // near) % left

time: 186 us -> 182 us (0.978)
  starting transfers between devices: 37.2 us -> 33.7 us
    ppermute x6, waiting for transfers between devices: 49.4 us -> 29.6 us  [shifted(): lax.ppermute(x, 'member', [(i, (i + places) % count) for i in range(count)])]
    ppermute x3, waiting for transfers between devices: 7.11 us -> 17.9 us  [plane_gather(): other = lax.ppermute(x, axis, [(j, j ^ step) for j in range(count)])]
    all_to_all x4, waiting for transfers between devices: 26.3 us -> 34.4 us  [exchange(): return lax.all_to_all(blocks, ('region', 'member'), 0, 0, tiled=True)]
    all_to_all x4, starting transfers between devices: 20.7 us -> 18 us  [exchange(): return lax.all_to_all(blocks, ('region', 'member'), 0, 0, tiled=True)]
  transfers between devices with their start and end apart: 16 -> 16, of which waited for: 10 -> 11; matrix products, arithmetic and copies ran while one was open for 7% -> 8% of each run, Pallas kernels for 22% -> 22%
where the time goes in v5:
time: 182 us; the launch traced here: 180 us
  waiting for transfers between devices  87.1 us (48%)
  Pallas kernels  39.7 us (22%)
  starting transfers between devices  33.7 us (19%)
  local copies, waits for them, and re-layouts  13.8 us (8%)
  other arithmetic  4.34 us (2%)
    pallas_call x3, Pallas kernels, whole_fields(): pl.pallas_call(functools.partial(field_kernel, regions), out_shape=jax.Sh...  37.6 us
    all_to_all x4, waiting for transfers between devices, exchange(): return lax.all_to_all(blocks, ('region', 'member'), 0, 0, tiled=True)  34.4 us
    ppermute x6, waiting for transfers between devices, shifted(): lax.ppermute(x, 'member', [(i, (i + places) % count) for i in range(count)])  29.6 us
    all_to_all x4, starting transfers between devices, exchange(): return lax.all_to_all(blocks, ('region', 'member'), 0, 0, tiled=True)  18 us
    ppermute x3, waiting for transfers between devices, plane_gather(): other = lax.ppermute(x, axis, [(j, j ^ step) for j in range(count)])  17.9 us
    ppermute x6, starting transfers between devices, shifted(): lax.ppermute(x, 'member', [(i, (i + places) % count) for i in range(count)])  9.73 us
    ppermute x3, waiting for transfers between devices, extras(): piece = lax.ppermute(piece, 'region', ring)  5.18 us
    ppermute x3, starting transfers between devices, plane_gather(): other = lax.ppermute(x, axis, [(j, j ^ step) for j in range(count)])  3.83 us
  transfers between devices with their start and end apart: 16, of which 11 were waited for; matrix products, arithmetic and copies ran while one was open for 8% of the time, Pallas kernels for 22%

profile of v5, /device:TPU:1, one launch (start us, length us, event | category | flops | bytes accessed | tf_op | source)
XLA Modules:
  0.0 179.8 jit_solution(10491261728705471948)
XLA Ops:
  0.0 1.6 slice-done
  1.6 1.6 copy.11
  3.2 7.1 %all-to-all-start = ((f32[32,2,1,64,128]{4,3,2,1,0:T(8,128)}), f32[32,2,1,64,128]{4,3,2,1,0:T(8,128)S(1)}, u32[]{:S(2)}, u32[]{:S(2)}) async-start(f32[32,2,1,64,128]{4,3,2,1,0:T(8,128)} %bitcast.64), calls=%async_computation | async-start | bytes 4194304 | tf_op jit(solution)/shard_map/all_to_all | solution.py:396
  13.1 1.7 collective-permute-start
  16.2 2.2 %collective-permute-start.4 = (f32[64,128]{1,0:T(8,128)S(1)}, f32[64,128]{1,0:T(8,128)S(1)}, u32[]{:S(2)}, u32[]{:S(2)}) collective-permute-start(f32[64,128]{1,0:T(8,128)S(1)} %bitcast.86), channel_id=1, source_target_pairs={{0,4},{1,5},{2,6},{3,7},{4,0},{5,1},{6,2},{7,3},{8,12},{9,13},{10,... | collective-permute-start | bytes 98312 | tf_op jit(solution)/shard_map/ppermute | solution.py:418
  22.9 3.1 %collective-permute-start.3 = (f32[64,128]{1,0:T(8,128)S(1)}, f32[64,128]{1,0:T(8,128)S(1)}, u32[]{:S(2)}, u32[]{:S(2)}) collective-permute-start(f32[64,128]{1,0:T(8,128)S(1)} %bitcast.84), channel_id=1, source_target_pairs={{0,2},{1,3},{2,4},{3,5},{4,6},{5,7},{6,0},{7,1},{8,10},{9,11},{10,... | collective-permute-start | bytes 98312 | tf_op jit(solution)/shard_map/ppermute | solution.py:418
  26.0 3.3 %collective-permute-done.1 = f32[5,32,128]{2,1,0:T(8,128)S(1)} collective-permute-done((f32[5,32,128]{2,1,0:T(8,128)S(1)}, f32[5,32,128]{2,1,0:T(8,128)S(1)}, u32[]{:S(2)}, u32[]{:S(2)}) %collective-permute-start.1) | collective-permute-done | bytes 81952 | tf_op jit(solution)/shard_map/ppermute | solution.py:463
  30.9 2.0 %patch_hots.1.hots = bf16[4,32,4096]{2,1,0:T(8,128)(2,1)} custom-call(s32[1]{0:T(128)} %bitcast.10.region_ref, f32[4,5,32,128]{3,2,1,0:T(8,128)} %pad_maximum_fusion.1.extra_ref.truth_ref), custom_call_target="tpu_custom_call" | custom-call | tf_op jit(solution)/shard_map/patch_hots/pallas_call | solution.py:219
  32.9 27.6 %collective-permute-done.4 = f32[64,128]{1,0:T(8,128)S(1)} collective-permute-done((f32[64,128]{1,0:T(8,128)S(1)}, f32[64,128]{1,0:T(8,128)S(1)}, u32[]{:S(2)}, u32[]{:S(2)}) %collective-permute-start.4) | collective-permute-done | bytes 32800 | tf_op jit(solution)/shard_map/ppermute | solution.py:418
  61.6 3.3 %all-to-all-start.1 = ((f32[32,1,1,64,128]{4,3,2,1,0:T(8,128)}), f32[32,1,1,64,128]{4,3,2,1,0:T(8,128)S(1)}, u32[]{:S(2)}, u32[]{:S(2)}) async-start(f32[32,1,1,64,128]{4,3,2,1,0:T(8,128)} %bitcast.2), calls=%async_computation.1 | async-start | bytes 2097152 | tf_op jit(solution)/shard_map/all_to_all | solution.py:396
  64.9 1.5 collective-permute-start.6
  67.0 17.1 %whole_fields.3 = f32[32,2,1,64,128]{4,3,2,1,0:T(8,128)} custom-call(s32[33]{0:T(128)} %pad_add_fusion.places_ref, f32[32,2,1,64,128]{4,3,2,1,0:T(8,128)} %copy-done, f32[4,5,32,128]{3,2,1,0:T(8,128)} %pad_maximum_fusion.1.extra_ref.truth_ref, bf16[4,32,4096]{2,1,0:T(8,128)(2,1)} %patch_hots.1.hots, bf16[256,256]{1,0:T(8,128)(2,1)} %constant.197.lon_ref, ...), custom_call_target="tpu_custom_call" | custom-call | flops 1207959552 | bytes 4194304 | tf_op jit(solution)/shard_map/whole_fields/pallas_call | solution.py:242
  84.1 7.8 %all-to-all-done.1.field_ref = f32[32,1,1,64,128]{4,3,2,1,0:T(8,128)S(1)} async-done(((f32[32,1,1,64,128]{4,3,2,1,0:T(8,128)}), f32[32,1,1,64,128]{4,3,2,1,0:T(8,128)S(1)}, u32[]{:S(2)}, u32[]{:S(2)}) %all-to-all-start.1) | async-done | bytes 1048608 | tf_op jit(solution)/shard_map/all_to_all | solution.py:396
  92.9 3.3 %all-to-all-start.2 = ((f32[32,2,1,64,128]{4,3,2,1,0:T(8,128)}), f32[32,2,1,64,128]{4,3,2,1,0:T(8,128)S(1)}, u32[]{:S(2)}, u32[]{:S(2)}) async-start(f32[32,2,1,64,128]{4,3,2,1,0:T(8,128)} %whole_fields.3), calls=%async_computation.2 | async-start | bytes 4194304 | tf_op jit(solution)/shard_map/all_to_all | solution.py:396
  96.3 1.5 collective-permute-start.7
  97.7 10.1 %whole_fields.4 = f32[32,1,1,64,128]{4,3,2,1,0:T(8,128)} custom-call(s32[33]{0:T(128)} %pad_add_fusion.places_ref, f32[32,1,1,64,128]{4,3,2,1,0:T(8,128)} %copy-done.1, f32[4,5,32,128]{3,2,1,0:T(8,128)} %pad_maximum_fusion.1.extra_ref.truth_ref, bf16[4,32,4096]{2,1,0:T(8,128)(2,1)} %patch_hots.1.hots, bf16[256,256]{1,0:T(8,128)(2,1)} %constant.197.lon_ref, ...), custom_call_target="tpu_custom_call" | custom-call | flops 603979776 | bytes 2097152 | tf_op jit(solution)/shard_map/whole_fields/pallas_call | solution.py:242
  107.8 16.9 %collective-permute-done.7 = f32[2,4,64,128]{3,2,1,0:T(8,128)S(1)} collective-permute-done((f32[2,4,64,128]{3,2,1,0:T(8,128)S(1)}, f32[2,4,64,128]{3,2,1,0:T(8,128)S(1)}, u32[]{:S(2)}, u32[]{:S(2)}) %collective-permute-start.7) | collective-permute-done | bytes 262176 | tf_op jit(solution)/shard_map/ppermute | solution.py:434
  127.4 2.1 %maximum_bitcast_fusion.field_ref = f32[8,1,4,64,128]{4,3,2,1,0:T(8,128)} fusion(f32[4,4,64,128]{3,2,1,0:T(8,128)} %collective-permute-done.8, f32[2,4,64,128]{3,2,1,0:T(8,128)S(1)} %collective-permute-done.7, f32[1,4,64,128]{3,2,1,0:T(8,128)S(1)} %collective-permute-done.6, f32[1,4,64,128]{3,2,1,0:T(8,128)S(1)} %maximum_bitcast_fusion.1), kind=kLoop, calls=%fused_computation.3 | loop fusion | flops 786432 | bytes 2097152 | tf_op jit(solution)/shard_map/broadcast_in_dim | solution.py:506
  129.5 10.4 %whole_fields.5 = f32[8,1,4,64,128]{4,3,2,1,0:T(8,128)} custom-call(s32[33]{0:T(128)} %pad_add_fusion.1.places_ref, f32[8,1,4,64,128]{4,3,2,1,0:T(8,128)} %maximum_bitcast_fusion.field_ref, f32[4,5,32,128]{3,2,1,0:T(8,128)} %pad_maximum_fusion.1.extra_ref.truth_ref, bf16[4,32,4096]{2,1,0:T(8,128)(2,1)} %patch_hots.1.hots, ...), custom_call_target="tpu_custom_call" | custom-call | flops 603979776 | bytes 2097152 | tf_op jit(solution)/shard_map/whole_fields/pallas_call | solution.py:242
  140.8 3.2 %collective-permute-start.9 = (f32[64,128]{1,0:T(8,128)S(1)}, f32[64,128]{1,0:T(8,128)S(1)}, u32[]{:S(2)}, u32[]{:S(2)}) collective-permute-start(f32[64,128]{1,0:T(8,128)S(1)} %get-tuple-element.50), channel_id=1, source_target_pairs={{0,6},{1,7},{2,0},{3,1},{4,2},{5,3},{6,4},{7,5},{8,14},{9,15},{10,... | collective-permute-start | bytes 98312 | tf_op jit(solution)/shard_map/ppermute | solution.py:418
  144.0 2.0 %collective-permute-done.9 = f32[64,128]{1,0:T(8,128)S(1)} collective-permute-done((f32[64,128]{1,0:T(8,128)S(1)}, f32[64,128]{1,0:T(8,128)S(1)}, u32[]{:S(2)}, u32[]{:S(2)}) %collective-permute-start.9) | collective-permute-done | bytes 32800 | tf_op jit(solution)/shard_map/ppermute | solution.py:418
  147.5 4.3 %all-to-all-start.3 = ((f32[32,1,1,64,128]{4,3,2,1,0:T(8,128)}), f32[32,1,1,64,128]{4,3,2,1,0:T(8,128)S(1)}, u32[]{:S(2)}, u32[]{:S(2)}) async-start(f32[32,1,1,64,128]{4,3,2,1,0:T(8,128)} %whole_fields.4), calls=%async_computation.3 | async-start | bytes 2097152 | tf_op jit(solution)/shard_map/all_to_all | solution.py:396
  152.0 2.1 %concatenate.118 = f32[2,100,32,128]{3,2,1,0:T(8,128)} pad(f32[2,64,32,128]{3,2,1,0:T(8,128)S(1)} %bitcast.66, f32[]{:T(128)} %constant.173.clone.1), padding=0_0x0_36x0_0x0_0 | pad | bytes 5373956 | tf_op jit(solution)/shard_map/concatenate | solution.py:522
  154.7 24.1 %all-to-all-done.3 = f32[32,1,1,64,128]{4,3,2,1,0:T(8,128)S(1)} async-done(((f32[32,1,1,64,128]{4,3,2,1,0:T(8,128)}), f32[32,1,1,64,128]{4,3,2,1,0:T(8,128)S(1)}, u32[]{:S(2)}, u32[]{:S(2)}) %all-to-all-start.3) | async-done | bytes 1048608 | tf_op jit(solution)/shard_map/all_to_all | solution.py:396
  (53 shorter events, 19.8 us)
Async XLA Ops:
  0.0 1.6 slice-start
  3.2 8.8 %copy-start.2 = (s32[1,4096]{1,0:T(1,128)S(1)}, s32[1,4096]{1,0:T(1,128)}, u32[]{:S(2)}) copy-start(s32[1,4096]{1,0:T(1,128)} %param.11) | copy-start | bytes 49156
  3.2 58.4 %all-to-all-start = ((f32[32,2,1,64,128]{4,3,2,1,0:T(8,128)}), f32[32,2,1,64,128]{4,3,2,1,0:T(8,128)S(1)}, u32[]{:S(2)}, u32[]{:S(2)}) async-start(f32[32,2,1,64,128]{4,3,2,1,0:T(8,128)} %bitcast.64), calls=%async_computation | async-start | bytes 4194304 | tf_op jit(solution)/shard_map/all_to_all | solution.py:396
  13.1 9.7 %collective-permute-start = (f32[5,32,128]{2,1,0:T(8,128)S(1)}, f32[5,32,128]{2,1,0:T(8,128)S(1)}, u32[]{:S(2)}, u32[]{:S(2)}) collective-permute-start(f32[5,32,128]{2,1,0:T(8,128)S(1)} %get-tuple-element.53), channel_id=1, source_target_pairs={{0,8},{8,16},{16,24},{24,0},{1,9},{9,17},{17,25},{25,1},{2,10},{10... | collective-permute-start | bytes 245768 | tf_op jit(solution)/shard_map/ppermute | solution.py:463
  14.8 14.5 %collective-permute-start.1 = (f32[5,32,128]{2,1,0:T(8,128)S(1)}, f32[5,32,128]{2,1,0:T(8,128)S(1)}, u32[]{:S(2)}, u32[]{:S(2)}) collective-permute-start(f32[5,32,128]{2,1,0:T(8,128)S(1)} %get-tuple-element.54), channel_id=1, source_target_pairs={{0,16},{8,24},{16,0},{24,8},{1,17},{9,25},{17,1},{25,9},{2,18},{10... | collective-permute-start | bytes 245768 | tf_op jit(solution)/shard_map/ppermute | solution.py:463
  14.8 15.3 %collective-permute-start.2 = (f32[5,32,128]{2,1,0:T(8,128)S(1)}, f32[5,32,128]{2,1,0:T(8,128)S(1)}, u32[]{:S(2)}, u32[]{:S(2)}) collective-permute-start(f32[5,32,128]{2,1,0:T(8,128)S(1)} %get-tuple-element.55), channel_id=1, source_target_pairs={{0,24},{8,0},{16,8},{24,16},{1,25},{9,1},{17,9},{25,17},{2,26},{10... | collective-permute-start | bytes 245768 | tf_op jit(solution)/shard_map/ppermute | solution.py:463
  16.2 44.3 %collective-permute-start.4 = (f32[64,128]{1,0:T(8,128)S(1)}, f32[64,128]{1,0:T(8,128)S(1)}, u32[]{:S(2)}, u32[]{:S(2)}) collective-permute-start(f32[64,128]{1,0:T(8,128)S(1)} %bitcast.86), channel_id=1, source_target_pairs={{0,4},{1,5},{2,6},{3,7},{4,0},{5,1},{6,2},{7,3},{8,12},{9,13},{10,... | collective-permute-start | bytes 98312 | tf_op jit(solution)/shard_map/ppermute | solution.py:418
  18.3 42.2 %collective-permute-start.5 = (f32[64,128]{1,0:T(8,128)S(1)}, f32[64,128]{1,0:T(8,128)S(1)}, u32[]{:S(2)}, u32[]{:S(2)}) collective-permute-start(f32[64,128]{1,0:T(8,128)S(1)} %bitcast.85), channel_id=1, source_target_pairs={{0,6},{1,7},{2,0},{3,1},{4,2},{5,3},{6,4},{7,5},{8,14},{9,15},{10,... | collective-permute-start | bytes 98312 | tf_op jit(solution)/shard_map/ppermute | solution.py:418
  22.9 37.6 %collective-permute-start.3 = (f32[64,128]{1,0:T(8,128)S(1)}, f32[64,128]{1,0:T(8,128)S(1)}, u32[]{:S(2)}, u32[]{:S(2)}) collective-permute-start(f32[64,128]{1,0:T(8,128)S(1)} %bitcast.84), channel_id=1, source_target_pairs={{0,2},{1,3},{2,4},{3,5},{4,6},{5,7},{6,0},{7,1},{8,10},{9,11},{10,... | collective-permute-start | bytes 98312 | tf_op jit(solution)/shard_map/ppermute | solution.py:418
  61.6 5.4 %copy-start = (f32[32,2,1,64,128]{4,3,2,1,0:T(8,128)}, f32[32,2,1,64,128]{4,3,2,1,0:T(8,128)S(1)}, u32[]{:S(2)}) copy-start(f32[32,2,1,64,128]{4,3,2,1,0:T(8,128)S(1)} %all-to-all-done.field_ref) | copy-start | bytes 6291460
  61.6 30.3 %all-to-all-start.1 = ((f32[32,1,1,64,128]{4,3,2,1,0:T(8,128)}), f32[32,1,1,64,128]{4,3,2,1,0:T(8,128)S(1)}, u32[]{:S(2)}, u32[]{:S(2)}) async-start(f32[32,1,1,64,128]{4,3,2,1,0:T(8,128)} %bitcast.2), calls=%async_computation.1 | async-start | bytes 2097152 | tf_op jit(solution)/shard_map/all_to_all | solution.py:396
  64.9 19.2 %collective-permute-start.6 = (f32[1,4,64,128]{3,2,1,0:T(8,128)S(1)}, f32[1,4,64,128]{3,2,1,0:T(8,128)S(1)}, u32[]{:S(2)}, u32[]{:S(2)}) collective-permute-start(f32[1,4,64,128]{3,2,1,0:T(8,128)S(1)} %maximum_bitcast_fusion.1), channel_id=1, source_target_pairs={{0,16},{8,24},{16,0},{24,8},{1,17},{9,25},{17,1},{25,9},{2,18},{10... | collective-permute-start | bytes 393224 | tf_op jit(solution)/shard_map/ppermute | solution.py:434
  91.9 1.0 copy-start.1
  92.9 54.6 %all-to-all-start.2 = ((f32[32,2,1,64,128]{4,3,2,1,0:T(8,128)}), f32[32,2,1,64,128]{4,3,2,1,0:T(8,128)S(1)}, u32[]{:S(2)}, u32[]{:S(2)}) async-start(f32[32,2,1,64,128]{4,3,2,1,0:T(8,128)} %whole_fields.3), calls=%async_computation.2 | async-start | bytes 4194304 | tf_op jit(solution)/shard_map/all_to_all | solution.py:396
  96.3 28.5 %collective-permute-start.7 = (f32[2,4,64,128]{3,2,1,0:T(8,128)S(1)}, f32[2,4,64,128]{3,2,1,0:T(8,128)S(1)}, u32[]{:S(2)}, u32[]{:S(2)}) collective-permute-start(f32[2,4,64,128]{3,2,1,0:T(8,128)S(1)} %pad_maximum_fusion.2), channel_id=1, source_target_pairs={{0,1},{1,0},{2,3},{3,2},{4,5},{5,4},{6,7},{7,6},{8,9},{9,8},{10,11... | collective-permute-start | bytes 786440 | tf_op jit(solution)/shard_map/ppermute | solution.py:434
  124.8 2.6 %collective-permute-start.8 = (f32[4,4,64,128]{3,2,1,0:T(8,128)S(1)}, f32[4,4,64,128]{3,2,1,0:T(8,128)}, u32[]{:S(2)}, u32[]{:S(2)}) collective-permute-start(f32[4,4,64,128]{3,2,1,0:T(8,128)S(1)} %pad_maximum_fusion), channel_id=1, source_target_pairs={{0,8},{8,0},{16,24},{24,16},{1,9},{9,1},{17,25},{25,17},{2,10},{10... | collective-permute-start | bytes 1572872 | tf_op jit(solution)/shard_map/ppermute | solution.py:434
  140.7 5.4 %collective-permute-start.11 = (f32[64,128]{1,0:T(8,128)S(1)}, f32[64,128]{1,0:T(8,128)S(1)}, u32[]{:S(2)}, u32[]{:S(2)}) collective-permute-start(f32[64,128]{1,0:T(8,128)S(1)} %get-tuple-element.48), channel_id=1, source_target_pairs={{0,2},{1,3},{2,4},{3,5},{4,6},{5,7},{6,0},{7,1},{8,10},{9,11},{10,... | collective-permute-start | bytes 98312 | tf_op jit(solution)/shard_map/ppermute | solution.py:418
  140.8 5.3 %collective-permute-start.10 = (f32[64,128]{1,0:T(8,128)S(1)}, f32[64,128]{1,0:T(8,128)S(1)}, u32[]{:S(2)}, u32[]{:S(2)}) collective-permute-start(f32[64,128]{1,0:T(8,128)S(1)} %get-tuple-element.49), channel_id=1, source_target_pairs={{0,4},{1,5},{2,6},{3,7},{4,0},{5,1},{6,2},{7,3},{8,12},{9,13},{10,... | collective-permute-start | bytes 98312 | tf_op jit(solution)/shard_map/ppermute | solution.py:418
  140.8 5.2 %collective-permute-start.9 = (f32[64,128]{1,0:T(8,128)S(1)}, f32[64,128]{1,0:T(8,128)S(1)}, u32[]{:S(2)}, u32[]{:S(2)}) collective-permute-start(f32[64,128]{1,0:T(8,128)S(1)} %get-tuple-element.50), channel_id=1, source_target_pairs={{0,6},{1,7},{2,0},{3,1},{4,2},{5,3},{6,4},{7,5},{8,14},{9,15},{10,... | collective-permute-start | bytes 98312 | tf_op jit(solution)/shard_map/ppermute | solution.py:418
  147.5 31.3 %all-to-all-start.3 = ((f32[32,1,1,64,128]{4,3,2,1,0:T(8,128)}), f32[32,1,1,64,128]{4,3,2,1,0:T(8,128)S(1)}, u32[]{:S(2)}, u32[]{:S(2)}) async-start(f32[32,1,1,64,128]{4,3,2,1,0:T(8,128)} %whole_fields.4), calls=%async_computation.3 | async-start | bytes 2097152 | tf_op jit(solution)/shard_map/all_to_all | solution.py:396

commit v6 on v4

--- a/solution.py
+++ b/solution.py
@@ -14,6 +14,7 @@
 STEP = 32
 BLOCK = 8
 VMEM = 56 * 1024 * 1024
+WHOLE = 8 * 1024 * 1024
 F32 = jnp.float32
 BF16 = jnp.bfloat16
 
@@ -115,13 +116,14 @@
     steps = rows // STEP
     patches = hots.shape[1]
     scale = float(np.sqrt(PATCH))
+    own = 0 if field_ref.shape[1] == 1 else pl.program_id(0)
 
     def shift_of(region):
         return lax.rem(places_ref[0] - region + regions, regions)
 
-    def place(region, device):
+    def place(region, device, variable):
         index = places_ref[1 + region * devices + device]
-        return (index, 0, 0) if inner == 1 else (index // inner, 0, index % inner)
+        return (index, variable, 0) if inner == 1 else (index // inner, variable, index % inner)
 
     def smoothed(pair):
         wide = jnp.concatenate([along_lon(x, lon_ref[...]) for x in pair], axis=1)
@@ -132,7 +134,7 @@
         pair = [
             jnp.concatenate(
                 [
-                    field_ref[*place(region, device), k * rows : (k + 1) * rows, :]
+                    field_ref[*place(region, device, own), k * rows : (k + 1) * rows, :]
                     for region in range(regions)
                 ],
                 axis=0,
@@ -195,7 +197,7 @@
         )
         for region in range(regions):
             for k in range(held):
-                out_ref[*place(region, device), k * rows : (k + 1) * rows, :] = result[
+                out_ref[*place(region, device, 0), k * rows : (k + 1) * rows, :] = result[
                     region * rows : (region + 1) * rows, k * lon : (k + 1) * lon
                 ]
 
@@ -246,7 +248,7 @@
             num_scalar_prefetch=1,
             grid=(count,),
             in_specs=[
-                block,
+                pl.BlockSpec(memory_space=pltpu.VMEM) if 4 * fields.size <= WHOLE else block,
                 pl.BlockSpec((regions, 1, rows, lon), lambda v, table: (0, v + offset, 0, 0)),
                 pl.BlockSpec(hots.shape, lambda v, table: (0, 0, 0)),
                 pl.BlockSpec((2 * lon, 2 * lon), lambda v, table: (0, 0)),
@@ -434,8 +436,6 @@
         if i == 0:
             other, beside = lax.optimization_barrier((other, beside))
         x = jnp.concatenate([x, other], axis=0)
-        if i == len(steps) - 2:
-            x, beside = lax.optimization_barrier((x, beside))
     return x, beside
 
 
@@ -474,7 +474,7 @@
     share = variables // total
     whole = share * total
     left = variables - whole
-    chunks = [count for count in (share - share // 2, share // 2) if count]
+    chunks = [count for count in (share // 2, share - share // 2) if count]
     sent, starts, counts, begin = [], [], [], 0
     for count in chunks:
         sent.append(sent_rows(forecast[:, begin : begin + count * total], count))
@@ -506,12 +506,13 @@
         places = places + (plane - members // near) % left
         result = whole_fields(field[:, None], places, extra, hots, share)
         result = result[0, 0]
+        results[0], result = lax.optimization_barrier((results[0], result))
         shifts = [shifted(result[t], -t * near) if t else result[t] for t in range(left)]
+        if len(chunks) > 1:
+            shifts, results[1] = lax.optimization_barrier((shifts, results[1]))
         shifts = jnp.stack(shifts + shifts).reshape(2 * left, held, rows, lon)
         last = lax.dynamic_slice_in_dim(shifts, lax.rem(left - plane, left), left, axis=0)
         last = jnp.swapaxes(last, 0, 1)
-        if len(chunks) > 1:
-            results[1], last = lax.optimization_barrier((results[1], last))
     backs = []
     for result in results:
         if backs:

time: 186 us -> 180 us (0.968)
  waiting for transfers between devices: 88 us -> 83.9 us
  other arithmetic: 4.09 us -> 6.65 us
  local copies, waits for them, and re-layouts: 13.8 us -> 11.5 us
  starting transfers between devices: 37.2 us -> 35.2 us
    ppermute x6, waiting for transfers between devices: 49.4 us -> 15.2 us  [shifted(): lax.ppermute(x, 'member', [(i, (i + places) % count) for i in range(count)])]
    all_to_all x4, waiting for transfers between devices: 26.3 us -> 52.3 us  [exchange(): return lax.all_to_all(blocks, ('region', 'member'), 0, 0, tiled=True)]
    ppermute x3, waiting for transfers between devices: 7.11 us -> 14.9 us  [plane_gather(): other = lax.ppermute(x, axis, [(j, j ^ step) for j in range(count)])]
    ppermute x3, waiting for transfers between devices: 5.18 us -> 1.61 us  [extras(): piece = lax.ppermute(piece, 'region', ring)]
    ppermute x3, starting transfers between devices: 3.02 us -> 5.87 us  [plane_gather(): other = lax.ppermute(x, axis, [(j, j ^ step) for j in range(count)])]
    all_to_all x4, starting transfers between devices: 20.7 us -> 17.9 us  [exchange(): return lax.all_to_all(blocks, ('region', 'member'), 0, 0, tiled=True)]
    ppermute x6, starting transfers between devices: 11.2 us -> 9.29 us  [shifted(): lax.ppermute(x, 'member', [(i, (i + places) % count) for i in range(count)])]
  transfers between devices with their start and end apart: 16 -> 16, of which waited for: 10 -> 11; matrix products, arithmetic and copies ran while one was open for 7% -> 8% of each run, Pallas kernels for 22% -> 22%
where the time goes in v6:
time: 180 us; the launch traced here: 179 us
  waiting for transfers between devices  83.9 us (47%)
  Pallas kernels  40 us (22%)
  starting transfers between devices  35.2 us (20%)
  local copies, waits for them, and re-layouts  11.5 us (6%)
  other arithmetic  6.65 us (4%)
    all_to_all x4, waiting for transfers between devices, exchange(): return lax.all_to_all(blocks, ('region', 'member'), 0, 0, tiled=True)  52.3 us
    pallas_call x3, Pallas kernels, whole_fields(): pl.pallas_call(functools.partial(field_kernel, regions), out_shape=jax.Sh...  38 us
    all_to_all x4, starting transfers between devices, exchange(): return lax.all_to_all(blocks, ('region', 'member'), 0, 0, tiled=True)  17.9 us
    ppermute x6, waiting for transfers between devices, shifted(): lax.ppermute(x, 'member', [(i, (i + places) % count) for i in range(count)])  15.2 us
    ppermute x3, waiting for transfers between devices, plane_gather(): other = lax.ppermute(x, axis, [(j, j ^ step) for j in range(count)])  14.9 us
    ppermute x6, starting transfers between devices, shifted(): lax.ppermute(x, 'member', [(i, (i + places) % count) for i in range(count)])  9.29 us
    ppermute x3, starting transfers between devices, plane_gather(): other = lax.ppermute(x, axis, [(j, j ^ step) for j in range(count)])  5.87 us
  transfers between devices with their start and end apart: 16, of which 11 were waited for; matrix products, arithmetic and copies ran while one was open for 8% of the time, Pallas kernels for 22%

profile of v6, /device:TPU:1, one launch (start us, length us, event | category | flops | bytes accessed | tf_op | source)
XLA Modules:
  0.0 178.6 jit_solution(2197618469329427223)
XLA Ops:
  2.4 7.2 %all-to-all-start = ((f32[32,1,1,64,128]{4,3,2,1,0:T(8,128)}), f32[32,1,1,64,128]{4,3,2,1,0:T(8,128)}, u32[]{:S(2)}, u32[]{:S(2)}) async-start(f32[32,1,1,64,128]{4,3,2,1,0:T(8,128)} %bitcast.74), calls=%async_computation | async-start | bytes 2097152 | tf_op jit(solution)/shard_map/all_to_all | solution.py:398
  13.0 1.6 collective-permute-start
  15.2 2.2 %collective-permute-start.4 = (f32[64,128]{1,0:T(8,128)S(1)}, f32[64,128]{1,0:T(8,128)}, u32[]{:S(2)}, u32[]{:S(2)}) collective-permute-start(f32[64,128]{1,0:T(8,128)S(1)} %bitcast.88), channel_id=1, source_target_pairs={{0,4},{1,5},{2,6},{3,7},{4,0},{5,1},{6,2},{7,3},{8,12},{9,13},{10,... | collective-permute-start | bytes 98312 | tf_op jit(solution)/shard_map/ppermute | solution.py:420
  19.0 1.5 copy.10
  23.3 1.7 pad_maximum_fusion.1.extra_ref.truth_ref
  25.0 2.0 %patch_hots.1.hots = bf16[4,32,4096]{2,1,0:T(8,128)(2,1)} custom-call(s32[1]{0:T(128)} %bitcast.10.region_ref, f32[4,5,32,128]{3,2,1,0:T(8,128)} %pad_maximum_fusion.1.extra_ref.truth_ref), custom_call_target="tpu_custom_call" | custom-call | tf_op jit(solution)/shard_map/patch_hots/pallas_call | solution.py:221
  27.1 9.9 %collective-permute-done.4 = f32[64,128]{1,0:T(8,128)} collective-permute-done((f32[64,128]{1,0:T(8,128)S(1)}, f32[64,128]{1,0:T(8,128)}, u32[]{:S(2)}, u32[]{:S(2)}) %collective-permute-start.4) | collective-permute-done | bytes 32800 | tf_op jit(solution)/shard_map/ppermute | solution.py:420
  38.4 3.4 %all-to-all-start.1 = ((f32[32,2,1,64,128]{4,3,2,1,0:T(8,128)}), f32[32,2,1,64,128]{4,3,2,1,0:T(8,128)S(1)}, u32[]{:S(2)}, u32[]{:S(2)}) async-start(f32[32,2,1,64,128]{4,3,2,1,0:T(8,128)} %bitcast.69), calls=%async_computation.1 | async-start | bytes 4194304 | tf_op jit(solution)/shard_map/all_to_all | solution.py:398
  42.6 1.5 collective-permute-start.6
  44.7 10.1 %whole_fields.3 = f32[32,1,1,64,128]{4,3,2,1,0:T(8,128)} custom-call(s32[33]{0:T(128)} %pad_add_fusion.places_ref, f32[32,1,1,64,128]{4,3,2,1,0:T(8,128)} %all-to-all-done.field_ref, f32[4,5,32,128]{3,2,1,0:T(8,128)} %pad_maximum_fusion.1.extra_ref.truth_ref, bf16[4,32,4096]{2,1,0:T(8,128)(2,1)} %patch_hots.1.hots, bf16[256,256]{1,0:T(8,128)(2,1)} %constant.197.lon_ref, ...), custom_call_target="tpu_custom_call" | custom-call | flops 603979776 | bytes 2097152 | tf_op jit(solution)/shard_map/whole_fields/pallas_call | solution.py:244
  54.8 3.8 %collective-permute-done.6 = f32[1,4,64,128]{3,2,1,0:T(8,128)S(1)} collective-permute-done((f32[1,4,64,128]{3,2,1,0:T(8,128)S(1)}, f32[1,4,64,128]{3,2,1,0:T(8,128)S(1)}, u32[]{:S(2)}, u32[]{:S(2)}) %collective-permute-start.6) | collective-permute-done | bytes 131104 | tf_op jit(solution)/shard_map/ppermute | solution.py:435
  58.7 4.0 %collective-permute-start.7 = (f32[2,4,64,128]{3,2,1,0:T(8,128)S(1)}, f32[2,4,64,128]{3,2,1,0:T(8,128)S(1)}, u32[]{:S(2)}, u32[]{:S(2)}) collective-permute-start(f32[2,4,64,128]{3,2,1,0:T(8,128)S(1)} %pad_maximum_fusion.2), channel_id=1, source_target_pairs={{0,1},{1,0},{2,3},{3,2},{4,5},{5,4},{6,7},{7,6},{8,9},{9,8},{10,11... | collective-permute-start | bytes 786440 | tf_op jit(solution)/shard_map/ppermute | solution.py:435
  62.6 9.9 %collective-permute-done.7 = f32[2,4,64,128]{3,2,1,0:T(8,128)S(1)} collective-permute-done((f32[2,4,64,128]{3,2,1,0:T(8,128)S(1)}, f32[2,4,64,128]{3,2,1,0:T(8,128)S(1)}, u32[]{:S(2)}, u32[]{:S(2)}) %collective-permute-start.7) | collective-permute-done | bytes 262176 | tf_op jit(solution)/shard_map/ppermute | solution.py:435
  74.7 2.1 %maximum_bitcast_fusion.field_ref = f32[8,1,4,64,128]{4,3,2,1,0:T(8,128)} fusion(f32[4,4,64,128]{3,2,1,0:T(8,128)} %collective-permute-done.8, f32[2,4,64,128]{3,2,1,0:T(8,128)S(1)} %collective-permute-done.7, f32[1,4,64,128]{3,2,1,0:T(8,128)S(1)} %collective-permute-done.6, f32[1,4,64,128]{3,2,1,0:T(8,128)S(1)} %maximum_bitcast_fusion.1), kind=kLoop, calls=%fused_computation.3 | loop fusion | flops 786432 | bytes 2097152 | tf_op jit(solution)/shard_map/broadcast_in_dim | solution.py:507
  76.9 10.4 %whole_fields.4 = f32[8,1,4,64,128]{4,3,2,1,0:T(8,128)} custom-call(s32[33]{0:T(128)} %pad_add_fusion.1.places_ref, f32[8,1,4,64,128]{4,3,2,1,0:T(8,128)} %maximum_bitcast_fusion.field_ref, f32[4,5,32,128]{3,2,1,0:T(8,128)} %pad_maximum_fusion.1.extra_ref.truth_ref, bf16[4,32,4096]{2,1,0:T(8,128)(2,1)} %patch_hots.1.hots, ...), custom_call_target="tpu_custom_call" | custom-call | flops 603979776 | bytes 2097152 | tf_op jit(solution)/shard_map/whole_fields/pallas_call | solution.py:244
  88.2 3.0 %all-to-all-done.1.field_ref = f32[32,2,1,64,128]{4,3,2,1,0:T(8,128)S(1)} async-done(((f32[32,2,1,64,128]{4,3,2,1,0:T(8,128)}), f32[32,2,1,64,128]{4,3,2,1,0:T(8,128)S(1)}, u32[]{:S(2)}, u32[]{:S(2)}) %all-to-all-start.1) | async-done | bytes 2097184 | tf_op jit(solution)/shard_map/all_to_all | solution.py:398
  91.1 3.6 %all-to-all-start.2 = ((f32[32,1,1,64,128]{4,3,2,1,0:T(8,128)}), f32[32,1,1,64,128]{4,3,2,1,0:T(8,128)S(1)}, u32[]{:S(2)}, u32[]{:S(2)}) async-start(f32[32,1,1,64,128]{4,3,2,1,0:T(8,128)} %whole_fields.3), calls=%async_computation.2 | async-start | bytes 2097152 | tf_op jit(solution)/shard_map/all_to_all | solution.py:398
  96.2 2.1 %collective-permute-start.10 = (f32[64,128]{1,0:T(8,128)S(1)}, f32[64,128]{1,0:T(8,128)S(1)}, u32[]{:S(2)}, u32[]{:S(2)}) collective-permute-start(f32[64,128]{1,0:T(8,128)S(1)} %get-tuple-element.55), channel_id=1, source_target_pairs={{0,4},{1,5},{2,6},{3,7},{4,0},{5,1},{6,2},{7,3},{8,12},{9,13},{10,... | collective-permute-start | bytes 98312 | tf_op jit(solution)/shard_map/ppermute | solution.py:420
  99.4 17.5 %whole_fields.5 = f32[32,2,1,64,128]{4,3,2,1,0:T(8,128)} custom-call(s32[33]{0:T(128)} %pad_add_fusion.places_ref, f32[32,2,1,64,128]{4,3,2,1,0:T(8,128)} %copy-done, f32[4,5,32,128]{3,2,1,0:T(8,128)} %pad_maximum_fusion.1.extra_ref.truth_ref, bf16[4,32,4096]{2,1,0:T(8,128)(2,1)} %patch_hots.1.hots, bf16[256,256]{1,0:T(8,128)(2,1)} %constant.197.lon_ref, ...), custom_call_target="tpu_custom_call" | custom-call | flops 1207959552 | bytes 4194304 | tf_op jit(solution)/shard_map/whole_fields/pallas_call | solution.py:244
  116.9 5.2 %collective-permute-done.10 = f32[64,128]{1,0:T(8,128)S(1)} collective-permute-done((f32[64,128]{1,0:T(8,128)S(1)}, f32[64,128]{1,0:T(8,128)S(1)}, u32[]{:S(2)}, u32[]{:S(2)}) %collective-permute-start.10) | collective-permute-done | bytes 32800 | tf_op jit(solution)/shard_map/ppermute | solution.py:420
  123.6 3.8 %all-to-all-start.3 = ((f32[32,2,1,64,128]{4,3,2,1,0:T(8,128)}), f32[32,2,1,64,128]{4,3,2,1,0:T(8,128)S(1)}, u32[]{:S(2)}, u32[]{:S(2)}) async-start(f32[32,2,1,64,128]{4,3,2,1,0:T(8,128)} %whole_fields.5), calls=%async_computation.3 | async-start | bytes 4194304 | tf_op jit(solution)/shard_map/all_to_all | solution.py:398
  127.6 2.1 %concatenate.118 = f32[2,100,32,128]{3,2,1,0:T(8,128)} pad(f32[2,32,32,128]{3,2,1,0:T(8,128)S(1)} %bitcast.73, f32[]{:T(128)} %constant.173.clone.1), padding=0_0x0_68x0_0x0_0 | pad | bytes 4325380 | tf_op jit(solution)/shard_map/concatenate | solution.py:524
  130.4 46.5 %all-to-all-done.3 = f32[32,2,1,64,128]{4,3,2,1,0:T(8,128)S(1)} async-done(((f32[32,2,1,64,128]{4,3,2,1,0:T(8,128)}), f32[32,2,1,64,128]{4,3,2,1,0:T(8,128)S(1)}, u32[]{:S(2)}, u32[]{:S(2)}) %all-to-all-start.3) | async-done | bytes 2097184 | tf_op jit(solution)/shard_map/all_to_all | solution.py:398
  177.1 1.5 constant_dynamic-update-slice_fusion.8
  (54 shorter events, 21.7 us)
Async XLA Ops:
  1.3 9.9 %copy-start.2 = (s32[1,4096]{1,0:T(1,128)S(1)}, s32[1,4096]{1,0:T(1,128)}, u32[]{:S(2)}) copy-start(s32[1,4096]{1,0:T(1,128)} %param.11) | copy-start | bytes 49156
  2.4 12.8 %copy-start.1 = (f32[2,100,32,128]{3,2,1,0:T(8,128)S(1)}, f32[2,100,32,128]{3,2,1,0:T(8,128)}, u32[]{:S(2)}) copy-start(f32[2,100,32,128]{3,2,1,0:T(8,128)} %param.9) | copy-start | bytes 9830404
  2.4 36.1 %all-to-all-start = ((f32[32,1,1,64,128]{4,3,2,1,0:T(8,128)}), f32[32,1,1,64,128]{4,3,2,1,0:T(8,128)}, u32[]{:S(2)}, u32[]{:S(2)}) async-start(f32[32,1,1,64,128]{4,3,2,1,0:T(8,128)} %bitcast.74), calls=%async_computation | async-start | bytes 2097152 | tf_op jit(solution)/shard_map/all_to_all | solution.py:398
  13.0 7.5 %collective-permute-start = (f32[5,32,128]{2,1,0:T(8,128)}, f32[5,32,128]{2,1,0:T(8,128)}, u32[]{:S(2)}, u32[]{:S(2)}) collective-permute-start(f32[5,32,128]{2,1,0:T(8,128)} %get-tuple-element.59), channel_id=1, source_target_pairs={{0,8},{8,16},{16,24},{24,0},{1,9},{9,17},{17,25},{25,1},{2,10},{10... | collective-permute-start | bytes 245768 | tf_op jit(solution)/shard_map/ppermute | solution.py:464
  14.6 8.2 %collective-permute-start.1 = (f32[5,32,128]{2,1,0:T(8,128)S(1)}, f32[5,32,128]{2,1,0:T(8,128)}, u32[]{:S(2)}, u32[]{:S(2)}) collective-permute-start(f32[5,32,128]{2,1,0:T(8,128)S(1)} %get-tuple-element.60), channel_id=1, source_target_pairs={{0,16},{8,24},{16,0},{24,8},{1,17},{9,25},{17,1},{25,9},{2,18},{10... | collective-permute-start | bytes 245768 | tf_op jit(solution)/shard_map/ppermute | solution.py:464
  14.7 8.6 %collective-permute-start.2 = (f32[5,32,128]{2,1,0:T(8,128)S(1)}, f32[5,32,128]{2,1,0:T(8,128)}, u32[]{:S(2)}, u32[]{:S(2)}) collective-permute-start(f32[5,32,128]{2,1,0:T(8,128)S(1)} %get-tuple-element.61), channel_id=1, source_target_pairs={{0,24},{8,0},{16,8},{24,16},{1,25},{9,1},{17,9},{25,17},{2,26},{10... | collective-permute-start | bytes 245768 | tf_op jit(solution)/shard_map/ppermute | solution.py:464
  15.2 21.8 %collective-permute-start.4 = (f32[64,128]{1,0:T(8,128)S(1)}, f32[64,128]{1,0:T(8,128)}, u32[]{:S(2)}, u32[]{:S(2)}) collective-permute-start(f32[64,128]{1,0:T(8,128)S(1)} %bitcast.88), channel_id=1, source_target_pairs={{0,4},{1,5},{2,6},{3,7},{4,0},{5,1},{6,2},{7,3},{8,12},{9,13},{10,... | collective-permute-start | bytes 98312 | tf_op jit(solution)/shard_map/ppermute | solution.py:420
  17.4 1.6 slice-start
  17.4 19.7 %collective-permute-start.5 = (f32[64,128]{1,0:T(8,128)S(1)}, f32[64,128]{1,0:T(8,128)}, u32[]{:S(2)}, u32[]{:S(2)}) collective-permute-start(f32[64,128]{1,0:T(8,128)S(1)} %bitcast.87), channel_id=1, source_target_pairs={{0,6},{1,7},{2,0},{3,1},{4,2},{5,3},{6,4},{7,5},{8,14},{9,15},{10,... | collective-permute-start | bytes 98312 | tf_op jit(solution)/shard_map/ppermute | solution.py:420
  20.5 16.5 %collective-permute-start.3 = (f32[64,128]{1,0:T(8,128)S(1)}, f32[64,128]{1,0:T(8,128)S(1)}, u32[]{:S(2)}, u32[]{:S(2)}) collective-permute-start(f32[64,128]{1,0:T(8,128)S(1)} %bitcast.86), channel_id=1, source_target_pairs={{0,2},{1,3},{2,4},{3,5},{4,6},{5,7},{6,0},{7,1},{8,10},{9,11},{10,... | collective-permute-start | bytes 98312 | tf_op jit(solution)/shard_map/ppermute | solution.py:420
  38.4 52.7 %all-to-all-start.1 = ((f32[32,2,1,64,128]{4,3,2,1,0:T(8,128)}), f32[32,2,1,64,128]{4,3,2,1,0:T(8,128)S(1)}, u32[]{:S(2)}, u32[]{:S(2)}) async-start(f32[32,2,1,64,128]{4,3,2,1,0:T(8,128)} %bitcast.69), calls=%async_computation.1 | async-start | bytes 4194304 | tf_op jit(solution)/shard_map/all_to_all | solution.py:398
  42.6 16.0 %collective-permute-start.6 = (f32[1,4,64,128]{3,2,1,0:T(8,128)S(1)}, f32[1,4,64,128]{3,2,1,0:T(8,128)S(1)}, u32[]{:S(2)}, u32[]{:S(2)}) collective-permute-start(f32[1,4,64,128]{3,2,1,0:T(8,128)S(1)} %maximum_bitcast_fusion.1), channel_id=1, source_target_pairs={{0,16},{8,24},{16,0},{24,8},{1,17},{9,25},{17,1},{25,9},{2,18},{10... | collective-permute-start | bytes 393224 | tf_op jit(solution)/shard_map/ppermute | solution.py:435
  58.7 13.9 %collective-permute-start.7 = (f32[2,4,64,128]{3,2,1,0:T(8,128)S(1)}, f32[2,4,64,128]{3,2,1,0:T(8,128)S(1)}, u32[]{:S(2)}, u32[]{:S(2)}) collective-permute-start(f32[2,4,64,128]{3,2,1,0:T(8,128)S(1)} %pad_maximum_fusion.2), channel_id=1, source_target_pairs={{0,1},{1,0},{2,3},{3,2},{4,5},{5,4},{6,7},{7,6},{8,9},{9,8},{10,11... | collective-permute-start | bytes 786440 | tf_op jit(solution)/shard_map/ppermute | solution.py:435
  72.6 2.1 %collective-permute-start.8 = (f32[4,4,64,128]{3,2,1,0:T(8,128)S(1)}, f32[4,4,64,128]{3,2,1,0:T(8,128)}, u32[]{:S(2)}, u32[]{:S(2)}) collective-permute-start(f32[4,4,64,128]{3,2,1,0:T(8,128)S(1)} %pad_maximum_fusion), channel_id=1, source_target_pairs={{0,8},{8,0},{16,24},{24,16},{1,9},{9,1},{17,25},{25,17},{2,10},{10... | collective-permute-start | bytes 1572872 | tf_op jit(solution)/shard_map/ppermute | solution.py:435
  91.1 8.3 %copy-start = (f32[32,2,1,64,128]{4,3,2,1,0:T(8,128)}, f32[32,2,1,64,128]{4,3,2,1,0:T(8,128)S(1)}, u32[]{:S(2)}) copy-start(f32[32,2,1,64,128]{4,3,2,1,0:T(8,128)S(1)} %all-to-all-done.1.field_ref) | copy-start | bytes 6291460
  91.1 32.4 %all-to-all-start.2 = ((f32[32,1,1,64,128]{4,3,2,1,0:T(8,128)}), f32[32,1,1,64,128]{4,3,2,1,0:T(8,128)S(1)}, u32[]{:S(2)}, u32[]{:S(2)}) async-start(f32[32,1,1,64,128]{4,3,2,1,0:T(8,128)} %whole_fields.3), calls=%async_computation.2 | async-start | bytes 2097152 | tf_op jit(solution)/shard_map/all_to_all | solution.py:398
  94.7 22.2 %collective-permute-start.11 = (f32[64,128]{1,0:T(8,128)S(1)}, f32[64,128]{1,0:T(8,128)S(1)}, u32[]{:S(2)}, u32[]{:S(2)}) collective-permute-start(f32[64,128]{1,0:T(8,128)S(1)} %get-tuple-element.54), channel_id=1, source_target_pairs={{0,2},{1,3},{2,4},{3,5},{4,6},{5,7},{6,0},{7,1},{8,10},{9,11},{10,... | collective-permute-start | bytes 98312 | tf_op jit(solution)/shard_map/ppermute | solution.py:420
  96.2 26.0 %collective-permute-start.10 = (f32[64,128]{1,0:T(8,128)S(1)}, f32[64,128]{1,0:T(8,128)S(1)}, u32[]{:S(2)}, u32[]{:S(2)}) collective-permute-start(f32[64,128]{1,0:T(8,128)S(1)} %get-tuple-element.55), channel_id=1, source_target_pairs={{0,4},{1,5},{2,6},{3,7},{4,0},{5,1},{6,2},{7,3},{8,12},{9,13},{10,... | collective-permute-start | bytes 98312 | tf_op jit(solution)/shard_map/ppermute | solution.py:420
  98.3 23.8 %collective-permute-start.9 = (f32[64,128]{1,0:T(8,128)S(1)}, f32[64,128]{1,0:T(8,128)S(1)}, u32[]{:S(2)}, u32[]{:S(2)}) collective-permute-start(f32[64,128]{1,0:T(8,128)S(1)} %get-tuple-element.56), channel_id=1, source_target_pairs={{0,6},{1,7},{2,0},{3,1},{4,2},{5,3},{6,4},{7,5},{8,14},{9,15},{10,... | collective-permute-start | bytes 98312 | tf_op jit(solution)/shard_map/ppermute | solution.py:420
  123.6 53.3 %all-to-all-start.3 = ((f32[32,2,1,64,128]{4,3,2,1,0:T(8,128)}), f32[32,2,1,64,128]{4,3,2,1,0:T(8,128)S(1)}, u32[]{:S(2)}, u32[]{:S(2)}) async-start(f32[32,2,1,64,128]{4,3,2,1,0:T(8,128)} %whole_fields.5), calls=%async_computation.3 | async-start | bytes 4194304 | tf_op jit(solution)/shard_map/all_to_all | solution.py:398
